TPU v7x, 32 devices: a whole 2x2x4 slice. The times are simulated.
32 devices in a mesh: seq: 8 (over z, y), batch: 4 (over x, core).
Axes of the slice: x: 2, y: 2, z: 4, core: 2. Of those that a mesh axis runs over, the one named last changes fastest.
Arguments:
- tokens: bfloat16 [4, 1024, 1408], P('batch', 'seq')
- qkv_weight: bfloat16 [1408, 4224], P('batch'), may hold values from -0.15625 to 0.15625
- out_weight: bfloat16 [1408, 1408], P('batch'), may hold values from -0.15625 to 0.15625
- mask_blocks: int32 [4, 14], replicated, may hold values from 0 to 15, as said below
- owner_map: int32 [4, 16], replicated, may hold values from 0 to 3, as said below
- pred_stream: bfloat16 [4, 4, 1024, 384], P('batch', None, 'seq'), may hold values from -6 to 6
- pred_up: bfloat16 [384, 1536], replicated, may hold values from -0.3125 to 0.3125
- pred_down: bfloat16 [1536, 384], replicated, may hold values from -0.15625 to 0.15625
- pred_proj: bfloat16 [384, 1408], replicated, may hold values from -0.3125 to 0.3125
Outputs:
- grad_up: float32 [384, 1536], P(None, ('seq', 'batch'))
- grad_down: float32 [1536, 384], P(('seq', 'batch'))
Inputs may be any that keep to these rules, and one draw needn't show every extreme that they name: `mask_blocks`: the 14 entries of one clip are distinct block indices; each aligned group of 2 blocks (those of one device) holds 2 or 1 of them. `owner_map`: within one clip, the blocks of one aligned group of 2 have distinct owners.
All inputs are finite; a program needn't handle non-finite values.
Results may differ from a plain program's by a relative error of at most 0.005.
Values may be sent and summed in bfloat16 or wider, within the bound.
No kernel may reach another device: no remote copies, remote signals or barrier semaphores. Data moves between devices by JAX's collectives and lax.ppermute only.
A program may use at most 128 MiB of HBM per device.

v0:
```python
import jax
import jax.numpy as jnp
from jax import lax
from jax.sharding import PartitionSpec as P

H = 16
HD = 88
BLK = 64


gelu_coef = 0.7978845608
gelu_cube = 0.044715


def layer_norm(values):
    center = values - jnp.mean(values, axis=-1, keepdims=True)
    variance = jnp.mean(center * center, axis=-1, keepdims=True)
    factor = lax.rsqrt(variance + 1e-06)
    return (center * factor, factor)


def gelu_tanh(values):
    inner = gelu_coef * (values + gelu_cube * values * values * values)
    return 0.5 * values * (1.0 + jnp.tanh(inner))


def gelu_slope(values):
    inner = gelu_coef * (values + gelu_cube * values * values * values)
    tangent = jnp.tanh(inner)
    return 0.5 * (1.0 + tangent) + 0.5 * values * (1.0 - tangent * tangent) * gelu_coef * (
        1.0 + 3.0 * gelu_cube * values * values
    )


def predictor_grads(stream, target_rows, live_rows, pred_up, pred_down, pred_proj, divisor):
    stream_f = stream.astype(jnp.float32)
    normed_pred = layer_norm(stream_f)[0].astype(jnp.bfloat16)
    hidden_pre = jnp.dot(normed_pred, pred_up, preferred_element_type=jnp.float32)
    hidden = gelu_tanh(hidden_pre).astype(jnp.bfloat16)
    mixed = stream_f + jnp.dot(hidden, pred_down, preferred_element_type=jnp.float32)
    mixed_norm, rstd = layer_norm(mixed)
    mixed_rounded = mixed_norm.astype(jnp.bfloat16)
    prediction = jnp.dot(mixed_rounded, pred_proj, preferred_element_type=jnp.float32)
    error = (prediction - target_rows.astype(jnp.float32)) * live_rows[:, None]
    grad_pred = (error / divisor).astype(jnp.bfloat16)
    grad_norm = jnp.dot(grad_pred, pred_proj.T, preferred_element_type=jnp.float32)
    first_mean = jnp.mean(grad_norm, axis=-1, keepdims=True)
    second_mean = jnp.mean(grad_norm * mixed_norm, axis=-1, keepdims=True)
    grad_mixed = (rstd * (grad_norm - first_mean - mixed_norm * second_mean)).astype(jnp.bfloat16)
    grad_down = jnp.dot(hidden.T, grad_mixed, preferred_element_type=jnp.float32)
    grad_hidden = jnp.dot(grad_mixed, pred_down.T, preferred_element_type=jnp.float32)
    grad_pre = (grad_hidden * gelu_slope(hidden_pre)).astype(jnp.bfloat16)
    grad_up = jnp.dot(normed_pred.T, grad_pre, preferred_element_type=jnp.float32)
    return (grad_up, grad_down)


def per_device(
    tokens,
    qkv_weight,
    out_weight,
    mask_blocks,
    owner_map,
    pred_stream,
    pred_up,
    pred_down,
    pred_proj,
):
    stream_in = tokens[0]
    tok_rows, width = stream_in.shape
    clip_now = lax.axis_index("batch")
    shard_now = lax.axis_index("seq")
    owners = lax.axis_size("batch")
    stream_f = stream_in.astype(jnp.float32)
    normed = layer_norm(stream_f)[0].astype(jnp.bfloat16)

    def fold_rows(left, piece):
        return jnp.dot(left, piece, preferred_element_type=jnp.float32)

    projected = fold_rows(normed, lax.all_gather(qkv_weight, "batch", axis=0, tiled=True))
    projected = projected.astype(jnp.bfloat16)
    queries = projected[:, :width].reshape(tok_rows, H, HD)
    keys_values = projected[:, width:]
    scale = 1.0 / HD**0.5

    def attend_block(carry, block):
        weighted, totals = carry
        block_keys = block[:, :width].reshape(block.shape[0], H, HD)
        block_values = block[:, width:].reshape(block.shape[0], H, HD)
        scores = (
            jnp.einsum("qhd,khd->hqk", queries, block_keys, preferred_element_type=jnp.float32)
            * scale
        )
        weights = jnp.exp(scores)
        totals = totals + jnp.sum(weights, axis=2)
        weighted = weighted + jnp.einsum(
            "hqk,khd->qhd",
            weights.astype(jnp.bfloat16),
            block_values,
            preferred_element_type=jnp.float32,
        )
        return (weighted, totals)

    start_state = (jnp.zeros((tok_rows, H, HD), jnp.float32), jnp.zeros((H, tok_rows), jnp.float32))
    piece = lax.all_gather(keys_values, "seq", axis=0, tiled=True)
    rows = piece.shape[0]
    blocks = piece.reshape(rows // 512, 512, piece.shape[1])
    weighted, totals = lax.scan(
        lambda state, block: (attend_block(state, block), None), start_state, blocks
    )[0]
    attended = (weighted / totals.T[:, :, None]).reshape(tok_rows, width).astype(jnp.bfloat16)
    attn_out = fold_rows(attended, lax.all_gather(out_weight, "batch", axis=0, tiled=True))
    target = layer_norm(stream_f + attn_out)[0].astype(jnp.bfloat16)
    blocks_dev = tok_rows // BLK
    block_ids = shard_now * blocks_dev + jnp.arange(blocks_dev, dtype=jnp.int32)
    owner_ids = jnp.arange(owners, dtype=jnp.int32)
    all_masked = jnp.any(mask_blocks[:, :, None] == block_ids[None, None, :], axis=1)
    all_owner = lax.dynamic_slice_in_dim(owner_map, shard_now * blocks_dev, blocks_dev, 1)
    my_masked = lax.dynamic_slice_in_dim(all_masked, clip_now, 1, 0)[0]
    my_owner = lax.dynamic_slice_in_dim(all_owner, clip_now, 1, 0)[0]
    send_select = (my_masked[None, :] & (my_owner[None, :] == owner_ids[:, None])).astype(
        jnp.bfloat16
    )
    target_blocks = target.reshape(blocks_dev, BLK, width)
    outgoing = jnp.einsum(
        "ob,brd->ord", send_select, target_blocks, preferred_element_type=jnp.float32
    ).astype(jnp.bfloat16)
    incoming = lax.all_to_all(outgoing, "batch", split_axis=0, concat_axis=0, tiled=True)
    recv_flags = all_masked & (all_owner == clip_now)
    recv_select = recv_flags.astype(jnp.bfloat16)
    live_clip = jnp.any(recv_flags, axis=1).astype(jnp.float32)
    live_rows = jnp.broadcast_to(live_clip[:, None], (owners, BLK)).reshape(owners * BLK)
    stream_blocks = pred_stream[0].reshape(owners, blocks_dev, BLK, pred_stream.shape[3])
    stream_picked = jnp.einsum(
        "cb,cbrd->crd", recv_select, stream_blocks, preferred_element_type=jnp.float32
    ).astype(jnp.bfloat16)
    stream_rows = stream_picked.reshape(owners * BLK, pred_stream.shape[3])
    target_rows = incoming.reshape(owners * BLK, width)
    divisor = float(owners * mask_blocks.shape[1])
    grad_up, grad_down = predictor_grads(
        stream_rows, target_rows, live_rows, pred_up, pred_down, pred_proj, divisor
    )
    return (
        lax.psum_scatter(grad_up, ("seq", "batch"), scatter_dimension=1, tiled=True),
        lax.psum_scatter(grad_down, ("seq", "batch"), scatter_dimension=0, tiled=True),
    )


def solution(mesh):
    in_specs = (
        P("batch", "seq", None),
        P("batch", None),
        P("batch", None),
        P(),
        P(),
        P("batch", None, "seq", None),
        P(),
        P(),
        P(),
    )
    out_specs = (P(None, ("seq", "batch")), P(("seq", "batch"), None))
    return jax.shard_map(
        per_device, mesh=mesh, in_specs=in_specs, out_specs=out_specs, check_vma=False
    )
```

profile of v0, /device:TPU:0, one launch (start us, length us, event | category | flops | bytes accessed | tf_op | source)
XLA Modules:
  0.0 461.7 jit_solution(2672985606502696183)
XLA Ops:
  7.2 0.7 all-gather.4.cloned.1.call-update
  8.7 81.9 %all-gather.4.cloned.1.call-done = bf16[1408,4224]{1,0:T(8,128)(2,1)} async-done(((bf16[352,4224]{1,0:T(8,128)(2,1)}), bf16[1408,4224]{1,0:T(8,128)(2,1)}) %all-gather.4.cloned.1.call-update) | async-done | bytes 11894800 | tf_op jit(solution)/shard_map/all_gather | solution.py:79
  90.5 6.3 %convolution_convert_fusion = bf16[128,4224]{1,0:T(8,128)(2,1)S(1)} fusion(bf16[1408,4224]{1,0:T(8,128)(2,1)} %all-gather.4.cloned.1.call-done, bf16[1,128,1408]{2,1,0:T(8,128)(2,1)S(1)} %copy-done.2, f32[128]{0:T(128)S(1)} %add_rsqrt_fusion.3, f32[128]{0:T(128)S(1)} %broadcast_multiply_fusion.5), kind=kOutput, calls=%fused_computation.10 | convolution fusion | flops 1523793920 | bytes 13337600 | tf_op jit(solution)/shard_map/dot_general | solution.py:77
  96.9 0.9 slice.18
  97.9 0.7 all-gather.8.cloned.1.call-update
  100.2 0.7 dynamic-slice_reduce_fusion
  102.5 1.8 fusion.64
  104.3 2.0 fusion.61
  106.4 0.9 copy.27
  107.3 83.3 %all-gather.6.cloned.1.call-done = bf16[1024,2816]{1,0:T(8,128)(2,1)} async-done(((bf16[128,2816]{1,0:T(8,128)(2,1)}), bf16[1024,2816]{1,0:T(8,128)(2,1)}) %all-gather.6.cloned.1.call-update) | async-done | bytes 5767184 | tf_op jit(solution)/shard_map/all_gather | solution.py:104
  190.6 33.3 %while.13 = (s32[]{:T(128)}, f32[128,16,88]{0,2,1:T(8,128)S(1)}, f32[16,128]{1,0:T(8,128)S(1)}, bf16[2,512,2816]{2,1,0:T(8,128)(2,1)}, bf16[128,16,88]{0,2,1:T(8,128)(2,1)}, /*index=5*/s32[]{:T(128)}, s32[]{:T(128)}) while((s32[]{:T(128)}, f32[128,16,88]{0,2,1:T(8,128)S(1)}, f32[16,128]{1,0:T(8,128)S(1)}, ...), condition=%wide.region_9.10_spmd.clone, body=%wide.region_7.0_spmd.clone.sunk | while | flops 373655552 | bytes 31850612 | solution.py:107
  190.6 3.6 constant_dynamic-slice_fusion.3
  194.3 4.7 %copy.44 = bf16[1,512,2816]{1,2,0:T(8,128)(2,1)} copy(bf16[1,512,2816]{2,1,0:T(8,128)(2,1)} %constant_dynamic-slice_fusion.3) | data formatting | bytes 5767168 | tf_op jit(solution)/shard_map/while/body/jit(dynamic_index_in_dim)/dynamic_slice | solution.py:107
  199.0 2.2 fusion.87
  201.2 3.0 bitcast_reduce_fusion.2
  204.2 3.2 fusion.88
  207.4 3.6 constant_dynamic-slice_fusion.3
  211.1 4.6 %copy.44 = bf16[1,512,2816]{1,2,0:T(8,128)(2,1)} copy(bf16[1,512,2816]{2,1,0:T(8,128)(2,1)} %constant_dynamic-slice_fusion.3) | data formatting | bytes 5767168 | tf_op jit(solution)/shard_map/while/body/jit(dynamic_index_in_dim)/dynamic_slice | solution.py:107
  215.7 2.0 fusion.87
  217.7 3.0 bitcast_reduce_fusion.2
  220.7 3.2 fusion.88
  224.1 3.1 fusion.60
  227.8 0.8 convolution_convert_fusion.1
  228.6 0.9 copy.30
  229.5 3.5 all-to-all-start
  233.3 10.6 %all-to-all-done = bf16[4,64,1408]{2,1,0:T(8,128)(2,1)S(1)} async-done(((bf16[4,64,1408]{2,1,0:T(8,128)(2,1)}), bf16[4,64,1408]{2,1,0:T(8,128)(2,1)S(1)}, u32[]{:S(2)}, u32[]{:S(2)}) %all-to-all-start) | async-done | bytes 720928 | tf_op jit(solution)/shard_map/all_to_all | solution.py:127
  244.0 0.9 copy-done.5
  244.8 3.6 fusion.57
  248.5 3.3 fusion.56
  251.9 4.2 fusion.14
  256.1 94.5 %reduce-scatter.5.cloned.1.call-done = f32[48,384]{1,0:T(8,128)} async-done(((f32[1536,384]{1,0:T(8,128)}), f32[48,384]{1,0:T(8,128)}) %reduce-scatter.5.cloned.1.call-update) | async-done | bytes 73744 | tf_op jit(solution)/shard_map/reduce_scatter | solution.py:144
  350.6 104.6 %reduce-scatter.3.cloned.1.call-done = f32[384,48]{0,1:T(8,128)} async-done(((f32[384,1536]{0,1:T(8,128)}), f32[384,48]{0,1:T(8,128)}) %reduce-scatter.3.cloned.1.call-update) | async-done | bytes 73744 | tf_op jit(solution)/shard_map/reduce_scatter | solution.py:143
  (74 shorter events, 5.1 us)
Async XLA Ops:
  7.2 97.2 %copy-start = (bf16[1536,384]{1,0:T(8,128)(2,1)S(1)}, bf16[1536,384]{1,0:T(8,128)(2,1)}, u32[]{:S(2)}) copy-start(bf16[1536,384]{1,0:T(8,128)(2,1)} %param.18) | copy-start | bytes 3538948
  7.2 1.1 copy-start.2
  7.2 83.3 %all-gather.4.cloned.1.call-start = ((), (), s32[]{:S(2)}) async-start(), calls=%async_computation.3 | async-start | bytes 14868480 | tf_op jit(solution)/shard_map/all_gather | solution.py:79
  7.9 182.7 %all-gather.6.cloned.1.call-start = ((), (), s32[]{:S(2)}) async-start(), calls=%async_computation.4 | async-start | bytes 6488064 | tf_op jit(solution)/shard_map/all_gather | solution.py:104
  96.9 1.7 copy-start.7
  96.9 1.9 copy-start.8
  96.9 2.2 copy-start.12
  97.8 126.2 %all-gather.8.cloned.1.call-start = ((), (), s32[]{:S(2)}) async-start(), calls=%async_computation.5 | async-start | bytes 4956160 | tf_op jit(solution)/shard_map/all_gather | solution.py:111
  104.3 2.1 copy-start.3
  199.0 2.2 copy-start.1
  215.7 2.0 copy-start.1
  227.1 0.7 copy-start.11
  227.1 0.7 copy-start.13
  228.6 4.5 copy-start.10
  228.6 4.5 copy-start.6
  228.6 16.2 %copy-start.9 = (f32[256]{0:T(256)S(1)}, f32[256]{0:T(256)}, u32[]{:S(2)}) copy-start(f32[256]{0:T(256)} %mul.149) | copy-start | bytes 3076
  229.5 14.4 %all-to-all-start = ((bf16[4,64,1408]{2,1,0:T(8,128)(2,1)}), bf16[4,64,1408]{2,1,0:T(8,128)(2,1)S(1)}, u32[]{:S(2)}, u32[]{:S(2)}) async-start(bf16[4,64,1408]{2,1,0:T(8,128)(2,1)} %copy.30), calls=%async_computation | async-start | bytes 1441792 | tf_op jit(solution)/shard_map/all_to_all | solution.py:127
  233.0 117.5 %reduce-scatter.5.cloned.1.call-start = ((), (), s32[]{:S(2)}) async-start(), calls=%async_computation.7 | async-start | bytes 2433024 | tf_op jit(solution)/shard_map/reduce_scatter | solution.py:144
  244.0 0.9 copy-start.5
  244.8 3.7 copy-start.4
  251.8 203.3 %reduce-scatter.3.cloned.1.call-start = ((), (), s32[]{:S(2)}) async-start(), calls=%async_computation.6 | async-start | bytes 2433024 | tf_op jit(solution)/shard_map/reduce_scatter | solution.py:143
Sparse Core Ops, SparseCore 0:
  9.6 80.8 all-gather.3
  98.0 92.6 all-gather.5
  192.2 31.3 all-gather.7
  252.0 98.5 reduce-scatter.4
  357.1 97.9 reduce-scatter.2
where the time goes:
time: 462 us
  waiting for transfers between devices  376 us (81%)
  matrix products  38.1 us (8%)
  local copies, waits for them, and re-layouts  27.6 us (6%)
  between operations  14.1 us (3%)
    reduce_scatter x1, waiting for transfers between devices, per_device(): lax.psum_scatter(grad_up, ('seq', 'batch'), scatter_dimension=1, tiled=True)  105 us
    reduce_scatter x1, waiting for transfers between devices, per_device(): lax.psum_scatter(grad_down, ('seq', 'batch'), scatter_dimension=0, tiled=...  94.5 us
    all_gather x1, waiting for transfers between devices, per_device(): piece = lax.all_gather(keys_values, 'seq', axis=0, tiled=True)  83.3 us
    all_gather x1, waiting for transfers between devices, per_device(): lax.all_gather(qkv_weight, 'batch', axis=0, tiled=True)  81.9 us
    dynamic_slice x4, local copies, waits for them, and re-layouts, per_device(): lax.scan(lambda state, block: (attend_block(state, block), None), start_s...  16.6 us
    all_to_all x1, waiting for transfers between devices, per_device(): lax.all_to_all(outgoing, 'batch', split_axis=0, concat_axis=0, tiled=True)  10.6 us
    dot_general x2, matrix products, fold_rows(): return jnp.dot(left, piece, preferred_element_type=jnp.float32)  9.42 us
  transfers between devices with their start and end apart: 6, of which 5 were waited for; matrix products, arithmetic and copies ran while one was open for 10% of the time, Pallas kernels for 0%

commit v1 on v0

--- a/solution.py
+++ b/solution.py
@@ -1,6 +1,8 @@
 import jax
 import jax.numpy as jnp
 from jax import lax
+from jax.experimental import pallas as pl
+from jax.experimental.pallas import tpu as pltpu
 from jax.sharding import PartitionSpec as P
 
 H = 16
@@ -145,19 +147,297 @@
     )
 
 
+def take(array, index):
+    return lax.dynamic_index_in_dim(array, index, 0, keepdims=False)
+
+
+def weight_kernel(place_ref, own_ref, one_ref, two_ref, three_ref, out_ref, held):
+    place = place_ref[0]
+    for step, piece_ref in enumerate((own_ref, one_ref, two_ref, three_ref)):
+        held[place ^ step] = piece_ref[...]
+    slabs, rows, columns = held.shape
+    out_ref[...] = held[...].reshape(slabs * rows, columns).T
+
+
+def attend_kernel(normed_ref, weight_ref, out_ref, projected):
+    projected[...] = lax.dot_general(
+        weight_ref[...],
+        normed_ref[...],
+        (((1,), (1,)), ((), ())),
+        preferred_element_type=jnp.float32,
+    )
+    part = projected.shape[0] // 3
+    blocks, _, block_rows = out_ref.shape
+    pad = jnp.zeros((-HD % 128, projected.shape[1]), jnp.float32)
+    log2_scale = 1.4426950408889634 / HD**0.5
+
+    def head_rows(which, head):
+        start = which * part + head * HD
+        rows = projected[start : start + HD, :]
+        return jnp.concatenate([rows, pad], axis=0).astype(jnp.bfloat16)
+
+    wide = 2
+    for head in range(part // HD):
+        queries = head_rows(0, head)
+        keys = head_rows(1, head).T
+        values = head_rows(2, head)
+        for block in range(blocks // wide):
+            span = block_rows * wide
+            scores = jnp.dot(
+                keys,
+                queries[:, block * span : (block + 1) * span],
+                preferred_element_type=jnp.float32,
+            )
+            weights = jnp.exp2(scores * log2_scale)
+            totals = jnp.sum(weights, axis=0, keepdims=True)
+            summed = jnp.dot(
+                values, weights.astype(jnp.bfloat16), preferred_element_type=jnp.float32
+            )
+            attended = summed[:HD] / totals
+            for inner in range(wide):
+                out_ref[block * wide + inner, head * HD : (head + 1) * HD, :] = attended[
+                    :, inner * block_rows : (inner + 1) * block_rows
+                ]
+
+
+def loss_kernel(
+    place_ref,
+    att_ref,
+    own_ref,
+    one_ref,
+    two_ref,
+    three_ref,
+    raw_ref,
+    prediction_ref,
+    mixed_norm_ref,
+    rstd_ref,
+    live_ref,
+    proj_ref,
+    out_ref,
+):
+    place = place_ref[0]
+    summed = raw_ref[...].astype(jnp.float32)
+    for step, slab_ref in enumerate((own_ref, one_ref, two_ref, three_ref)):
+        summed = summed + lax.dot_general(
+            att_ref[place ^ step],
+            slab_ref[...],
+            (((0,), (0,)), ((), ())),
+            preferred_element_type=jnp.float32,
+        )
+    target = layer_norm(summed)[0].astype(jnp.bfloat16)
+    error = (prediction_ref[...] - target.astype(jnp.float32)) * live_ref[...]
+    grad_pred = error.astype(jnp.bfloat16)
+    grad_norm = lax.dot_general(
+        grad_pred, proj_ref[...], (((1,), (1,)), ((), ())), preferred_element_type=jnp.float32
+    )
+    mixed_norm = mixed_norm_ref[...]
+    first_mean = jnp.mean(grad_norm, axis=-1, keepdims=True)
+    second_mean = jnp.mean(grad_norm * mixed_norm, axis=-1, keepdims=True)
+    out_ref[...] = (rstd_ref[...] * (grad_norm - first_mean - mixed_norm * second_mean)).astype(
+        jnp.bfloat16
+    )
+
+
+def grads_kernel(grad_ref, normed_ref, hidden_ref, slope_ref, down_ref, out_ref):
+    grad_mixed = grad_ref[...]
+    pieces, half, _ = out_ref.shape
+    half = half // 2
+    over_rows = (((0,), (0,)), ((), ()))
+    grad_down = lax.dot_general(
+        hidden_ref[...], grad_mixed, over_rows, preferred_element_type=jnp.float32
+    )
+    grad_hidden = lax.dot_general(
+        grad_mixed, down_ref[...], (((1,), (1,)), ((), ())), preferred_element_type=jnp.float32
+    )
+    grad_pre = (grad_hidden * slope_ref[...]).astype(jnp.bfloat16)
+    grad_up = lax.dot_general(
+        grad_pre, normed_ref[...], over_rows, preferred_element_type=jnp.float32
+    )
+    for piece in range(pieces):
+        rows = slice(piece * half, (piece + 1) * half)
+        out_ref[piece, :half, :] = grad_up[rows].astype(jnp.bfloat16)
+        out_ref[piece, half:, :] = grad_down[rows].astype(jnp.bfloat16)
+
+
+def in_vmem(kernel, out_shape, operands, places=0, scratch=()):
+    return pl.pallas_call(
+        kernel,
+        out_shape=out_shape,
+        in_specs=[pl.BlockSpec(memory_space=pltpu.SMEM)] * places
+        + [pl.BlockSpec(memory_space=pltpu.VMEM)] * (len(operands) - places),
+        out_specs=pl.BlockSpec(memory_space=pltpu.VMEM),
+        scratch_shapes=list(scratch),
+        compiler_params=pltpu.CompilerParams(vmem_limit_bytes=40 * 2**20),
+    )(*operands)
+
+
+CLIP_GROUP = ("k", "zl", "y")
+ROW_GROUP = ("y", "x", "k")
+BATCH_GROUP = ("x", "k")
+SUM_GROUP = ("zh", "zl")
+
+
+def head_shard(
+    tokens,
+    qkv_weight,
+    out_weight,
+    mask_blocks,
+    owner_map,
+    pred_stream,
+    pred_up,
+    pred_down,
+    pred_proj,
+):
+    zh, zl, y, x, k = (lax.axis_index(name) for name in ("zh", "zl", "y", "x", "k"))
+    batch = 2 * x + k
+    seq = 4 * zh + 2 * zl + y
+    place = batch.astype(jnp.int32)[None]
+    _, tok_rows, width = tokens.shape
+    owners, blk_dev = pred_stream.shape[1], tok_rows // BLK
+    pred_width, units = pred_up.shape
+
+    def swap_clips(value):
+        return lax.ppermute(value, ("zh", "k"), ((0, 0), (1, 2), (2, 1), (3, 3)))
+
+    def swap(value, bits):
+        return lax.ppermute(value, BATCH_GROUP, tuple((i, i ^ bits) for i in range(owners)))
+
+    raw = swap_clips(tokens[0])
+
+    part = width // 8
+
+    def columns_of(core):
+        first = (4 * core + 2 * zl + y) * part
+        return jnp.concatenate(
+            [
+                lax.dynamic_slice(
+                    qkv_weight, (0, which * width + first), (qkv_weight.shape[0], part)
+                )
+                for which in range(3)
+            ],
+            axis=1,
+        )
+
+    own_columns, other_columns = columns_of(k), columns_of(1 - k)
+    qkv_two = swap(own_columns, 2)
+    qkv_three = swap(other_columns, 3)
+    qkv_one = swap(other_columns, 1)
+
+    stream_blocks = pred_stream[0].reshape(owners, blk_dev, BLK, pred_width)
+    owner_here = lax.dynamic_slice_in_dim(owner_map, seq * blk_dev, blk_dev, 1)
+    mine = (owner_here == batch)[:, :, None, None]
+    compact = jnp.sum(jnp.where(mine, stream_blocks, 0), axis=1).astype(jnp.bfloat16)
+    arrived = lax.all_to_all(compact, BATCH_GROUP, split_axis=0, concat_axis=0, tiled=True)
+    stream = jnp.concatenate(
+        [take(arrived, take(owner_here, batch)[i]) for i in range(blk_dev)], axis=0
+    )
+    stream = swap_clips(stream)
+
+    stream_f = stream.astype(jnp.float32)
+    normed_pred = layer_norm(stream_f)[0].astype(jnp.bfloat16)
+    normed_rows = lax.all_gather(normed_pred, ROW_GROUP, axis=0, tiled=True)
+
+    raw_f = raw.astype(jnp.float32)
+    normed = layer_norm(raw_f)[0].astype(jnp.bfloat16)
+    normed_all = lax.all_gather(normed, CLIP_GROUP, axis=0, tiled=True)
+
+    out_two = swap(out_weight, 2)
+    out_one = swap(out_weight, 1)
+    out_three = swap(out_two, 1)
+
+    hidden = gelu_tanh(jnp.dot(normed_pred, pred_up, preferred_element_type=jnp.float32))
+    mixed = stream_f + jnp.dot(
+        hidden.astype(jnp.bfloat16), pred_down, preferred_element_type=jnp.float32
+    )
+    mixed_norm, rstd = layer_norm(mixed)
+    prediction = jnp.dot(
+        mixed_norm.astype(jnp.bfloat16), pred_proj, preferred_element_type=jnp.float32
+    )
+
+    mine_rows = 4 * y + batch
+    up_mine = lax.dynamic_index_in_dim(
+        pred_up.reshape(pred_width, 4, 8, units // 32), mine_rows, 2, keepdims=False
+    ).reshape(pred_width, units // 8)
+    down_mine = lax.dynamic_index_in_dim(
+        pred_down.reshape(4, 8, units // 32, pred_width), mine_rows, 1, keepdims=False
+    ).reshape(units // 8, pred_width)
+    pre_rows = jnp.dot(normed_rows, up_mine, preferred_element_type=jnp.float32)
+    hidden_rows = gelu_tanh(pre_rows).astype(jnp.bfloat16)
+    slope_rows = gelu_slope(pre_rows)
+
+    clip = 2 * x + zh
+    shard = 4 * k + 2 * zl + y
+    block_ids = shard * blk_dev + jnp.arange(blk_dev, dtype=jnp.int32)
+    masked = jnp.any(take(mask_blocks, clip)[:, None] == block_ids[None, :], axis=0)
+    divisor = float(owners * mask_blocks.shape[1])
+    live = jnp.repeat(masked.astype(jnp.float32) / divisor, BLK)[:, None]
+
+    slab = qkv_weight.shape[0]
+    qkv_columns = in_vmem(
+        weight_kernel,
+        jax.ShapeDtypeStruct((3 * part, width), jnp.bfloat16),
+        (place, own_columns, qkv_one, qkv_two, qkv_three),
+        places=1,
+        scratch=(pltpu.VMEM((owners, slab, 3 * part), jnp.bfloat16),),
+    )
+    attended = in_vmem(
+        attend_kernel,
+        jax.ShapeDtypeStruct((8, part, tok_rows), jnp.float32),
+        (normed_all, qkv_columns),
+        scratch=(pltpu.VMEM((3 * part, normed_all.shape[0]), jnp.float32),),
+    ).astype(jnp.bfloat16)
+    attended = lax.all_to_all(attended, CLIP_GROUP, split_axis=0, concat_axis=0, tiled=True)
+    attended = attended.reshape(owners, slab, tok_rows)
+
+    grad_mixed = in_vmem(
+        loss_kernel,
+        jax.ShapeDtypeStruct((tok_rows, pred_width), jnp.bfloat16),
+        (
+            place,
+            attended,
+            out_weight,
+            out_one,
+            out_two,
+            out_three,
+            raw,
+            prediction,
+            mixed_norm,
+            rstd,
+            live,
+            pred_proj,
+        ),
+        places=1,
+    )
+    grad_rows = lax.all_gather(grad_mixed, ROW_GROUP, axis=0, tiled=True)
+    grads = in_vmem(
+        grads_kernel,
+        jax.ShapeDtypeStruct((4, units // 16, pred_width), jnp.bfloat16),
+        (grad_rows, normed_rows, hidden_rows, slope_rows, down_mine),
+    )
+    grads = lax.all_to_all(grads, SUM_GROUP, split_axis=0, concat_axis=0, tiled=True)
+    total = jnp.sum(grads.astype(jnp.float32), axis=0)
+    half = units // 32
+    return total[:half].T, total[half:]
+
+
 def solution(mesh):
+    if mesh.shape["seq"] == 8 and mesh.shape["batch"] == 4:
+        names = ("zh", "zl", "y", "x", "k")
+        step, batch, seq = head_shard, BATCH_GROUP, names[:3]
+        mesh = jax.sharding.Mesh(mesh.devices.reshape(2, 2, 2, 2, 2), names)
+    else:
+        step, batch, seq = per_device, "batch", "seq"
+    everyone = (seq, batch) if isinstance(seq, str) else seq + batch
     in_specs = (
-        P("batch", "seq", None),
-        P("batch", None),
-        P("batch", None),
+        P(batch, seq, None),
+        P(batch, None),
+        P(batch, None),
         P(),
         P(),
-        P("batch", None, "seq", None),
+        P(batch, None, seq, None),
         P(),
         P(),
         P(),
     )
-    out_specs = (P(None, ("seq", "batch")), P(("seq", "batch"), None))
-    return jax.shard_map(
-        per_device, mesh=mesh, in_specs=in_specs, out_specs=out_specs, check_vma=False
-    )
+    out_specs = (P(None, everyone), P(everyone, None))
+    return jax.shard_map(step, mesh=mesh, in_specs=in_specs, out_specs=out_specs, check_vma=False)

time: 462 us -> 154 us (0.33)
  waiting for transfers between devices: 376 us -> 19.4 us
  blocking collectives: 0 us -> 38.7 us
  matrix products: 38.1 us -> 5.97 us
  starting transfers between devices: 3.69 us -> 32.7 us
  Pallas kernels: 0 us -> 11.3 us
  local copies, waits for them, and re-layouts: 27.6 us -> 18.2 us
  other arithmetic: 1.76 us -> 8.47 us
    reduce_scatter x2 -> x0, waiting for transfers between devices: 199 us -> none  [the longest x1 105 us: per_device(): lax.psum_scatter(grad_up, ('seq', 'batch'), scatter_dimension=1, tiled=True)]
    all_gather x3 -> x1, waiting for transfers between devices: 165 us -> 0.02 us  [head_shard(): normed_all = lax.all_gather(normed, CLIP_GROUP, axis=0, tiled=True)]
    dot_general x13 -> x3, matrix products: 38.1 us -> 5.97 us  [the longest x1 2.67 us: head_shard(): jnp.dot(hidden.astype(jnp.bfloat16), pred_down, preferred_element_type=jn...]
    ppermute x0 -> x8, starting transfers between devices: none -> 24.8 us  [the longest x6 22.4 us: swap(): lax.ppermute(value, BATCH_GROUP, tuple(((i, i ^ bits) for i in range(owne...]
    all_gather x0 -> x2, blocking collectives: none -> 23.6 us  [the longest x1 13.6 us: head_shard(): normed_rows = lax.all_gather(normed_pred, ROW_GROUP, axis=0, tiled=True)]
    all_to_all x0 -> x1, blocking collectives: none -> 15.1 us  [head_shard(): lax.all_to_all(grads, SUM_GROUP, split_axis=0, concat_axis=0, tiled=True)]
    dynamic_slice x6 -> x4, local copies, waits for them, and re-layouts: 17.4 us -> 4.25 us  [the longest x1 1.9 us: columns_of(): lax.dynamic_slice(qkv_weight, (0, which * width + first), (qkv_weight.sha...]
    pallas_call x0 -> x4, Pallas kernels: none -> 11.3 us  [in_vmem(): pl.pallas_call(kernel, out_shape=out_shape, in_specs=[pl.BlockSpec(memory...]
  transfers between devices with their start and end apart: 6 -> 11, of which waited for: 5 -> 1; matrix products, arithmetic and copies ran while one was open for 10% -> 15% of each run, Pallas kernels for 0% -> 4%
where the time goes in v1:
time: 154 us; the launch traced here: 153 us
  blocking collectives  38.7 us (25%)
  starting transfers between devices  32.7 us (21%)
  waiting for transfers between devices  19.4 us (13%)
  local copies, waits for them, and re-layouts  18.2 us (12%)
  between operations  18.1 us (12%)
  Pallas kernels  11.3 us (7%)
  other arithmetic  8.47 us (6%)
  matrix products  5.97 us (4%)
    ppermute x6, starting transfers between devices, swap(): lax.ppermute(value, BATCH_GROUP, tuple(((i, i ^ bits) for i in range(owne...  22.4 us
    all_to_all x1, waiting for transfers between devices, head_shard(): lax.all_to_all(compact, BATCH_GROUP, split_axis=0, concat_axis=0, tiled=T...  19.3 us
    all_to_all x1, blocking collectives, head_shard(): lax.all_to_all(grads, SUM_GROUP, split_axis=0, concat_axis=0, tiled=True)  15.1 us
    all_gather x1, blocking collectives, head_shard(): normed_rows = lax.all_gather(normed_pred, ROW_GROUP, axis=0, tiled=True)  13.6 us
    pallas_call x4, Pallas kernels, in_vmem(): pl.pallas_call(kernel, out_shape=out_shape, in_specs=[pl.BlockSpec(memory...  11.3 us
    unnamed x41, local copies, waits for them, and re-layouts  10.8 us
    all_gather x1, blocking collectives, head_shard(): grad_rows = lax.all_gather(grad_mixed, ROW_GROUP, axis=0, tiled=True)  10 us
    all_to_all x1, starting transfers between devices, head_shard(): lax.all_to_all(compact, BATCH_GROUP, split_axis=0, concat_axis=0, tiled=T...  4 us
  transfers between devices with their start and end apart: 11, of which 1 were waited for; matrix products, arithmetic and copies ran while one was open for 15% of the time, Pallas kernels for 4%

profile of v1, /device:TPU:0, one launch (start us, length us, event | category | flops | bytes accessed | tf_op | source)
XLA Modules:
  0.0 152.8 jit_solution(15666519995367179010)
XLA Ops:
  7.2 1.8 %collective-permute-start = (bf16[128,1408]{1,0:T(8,128)(2,1)}, bf16[128,1408]{1,0:T(8,128)(2,1)S(1)}, u32[]{:S(2)}, u32[]{:S(2)}) collective-permute-start(bf16[128,1408]{1,0:T(8,128)(2,1)} %bitcast.34), channel_id=1, source_target_pairs={{0,0},{1,16},{16,1},{17,17},{2,2},{3,18},{18,3},{19,19},{4,4},{5,2... | collective-permute-start | bytes 1081352 | tf_op jit(solution)/shard_map/ppermute | solution.py:300
  9.4 1.0 fusion.13
  10.5 1.9 %constant_dynamic-slice_fusion.6 = (bf16[352,176]{1,0:T(8,128)(2,1)S(1)}, bf16[352,176]{1,0:T(8,128)(2,1)S(1)}, bf16[352,176]{1,0:T(8,128)(2,1)S(1)}, bf16[352,1...) fusion(bf16[352,4224]{1,0:T(8,128)(2,1)} %param.10, s32[]{:T(128)S(6)} %select_n.58, ...), kind=kLoop, calls=%fused_computation.49 | loop fusion | bytes 1486872 | tf_op jit(solution)/shard_map/dynamic_slice | solution.py:313
  12.4 1.0 pad_maximum_fusion.1
  13.4 13.6 %collective-permute-start.1 = (bf16[352,528]{1,0:T(8,128)(2,1)}, bf16[352,528]{1,0:T(8,128)(2,1)S(1)}, u32[]{:S(2)}, u32[]{:S(2)}) collective-permute-start(bf16[352,528]{1,0:T(8,128)(2,1)} %pad_maximum_fusion.1), channel_id=1, source_target_pairs={{0,1},{1,0},{2,3},{3,2},{4,5},{5,4},{6,7},{7,6},{8,9},{9,8},{10,11... | collective-permute-start | bytes 1115144 | tf_op jit(solution)/shard_map/ppermute | solution.py:303
  27.0 1.1 collective-permute-start.3
  29.2 0.9 select_reduce_fusion
  30.1 4.0 %all-to-all-start.1 = ((bf16[4,64,384]{2,1,0:T(8,128)(2,1)}), bf16[4,64,384]{2,1,0:T(8,128)(2,1)}, u32[]{:S(2)}, u32[]{:S(2)}) async-start(bf16[4,64,384]{2,1,0:T(8,128)(2,1)} %select_reduce_fusion), calls=%async_computation.1 | async-start | bytes 393216 | tf_op jit(solution)/shard_map/all_to_all | solution.py:330
  34.1 2.4 %copy.45 = bf16[384,1536]{0,1:T(8,128)(2,1)} copy(bf16[384,1536]{1,0:T(8,128)(2,1)} %param.15) | data formatting | bytes 2359296 | tf_op args[6]
  37.4 1.6 %constant_dynamic-slice_fusion.1 = bf16[384,4,1,48]{0,3,2,1:T(8,128)(2,1)} fusion(bf16[384,4,8,48]{0,3,2,1:T(8,128)(2,1)} %bitcast.31, s32[]{:T(128)S(6)} %select_n.69), kind=kLoop, calls=%fused_computation.44 | loop fusion | bytes 294916 | tf_op jit(solution)/shard_map/jit(dynamic_index_in_dim)/dynamic_slice | solution.py:358
  43.9 19.3 %all-to-all-done.1 = bf16[4,64,384]{2,1,0:T(8,128)(2,1)} async-done(((bf16[4,64,384]{2,1,0:T(8,128)(2,1)}), bf16[4,64,384]{2,1,0:T(8,128)(2,1)}, u32[]{:S(2)}, u32[]{:S(2)}) %all-to-all-start.1) | async-done | bytes 196640 | tf_op jit(solution)/shard_map/all_to_all | solution.py:330
  63.3 0.8 dynamic-slice_bitcast_fusion.1
  65.5 1.5 collective-permute-start.2
  67.3 2.7 %fusion.34 = (f32[128]{0:T(128)S(1)}, f32[128,384]{1,0:T(8,128)}) fusion(bf16[1536,384]{1,0:T(8,128)(2,1)S(1)} %copy-done, bf16[128,384]{1,0:T(8,128)(2,1)S(1)} %collective-permute-done.7, bf16[384,1536]{1,0:T(8,128)(2,1)} %param.15, f32[128]{0:T(128)S(1)} %add_rsqrt_fusion.1, f32[128]{0:T(128)S(1)} %broadcast_multiply_fusion.1), kind=kOutput, calls=%fused_computation.71 | convolution fusion | flops 304103296 | bytes 2655744 | tf_op jit(solution)/shard_map/dot_general | solution.py:349
  70.0 1.1 multiply_reduce_fusion
  71.8 5.1 %collective-permute-start.6 = (bf16[352,1408]{1,0:T(8,128)(2,1)}, bf16[352,1408]{1,0:T(8,128)(2,1)}, u32[]{:S(2)}, u32[]{:S(2)}) collective-permute-start(bf16[352,1408]{1,0:T(8,128)(2,1)} %collective-permute-done.5.two_ref), channel_id=1, source_target_pairs={{0,1},{1,0},{2,3},{3,2},{4,5},{5,4},{6,7},{7,6},{8,9},{9,8},{10,11... | collective-permute-start | bytes 2973704 | tf_op jit(solution)/shard_map/ppermute | solution.py:303
  77.0 1.7 %subtract_multiply_fusion.mixed_norm_ref = f32[128,384]{1,0:T(8,128)} fusion(f32[128,384]{1,0:T(8,128)} %get-tuple-element.19, f32[128]{0:T(128)S(1)} %get-tuple-element.15, f32[128]{0:T(128)S(1)} %broadcast_multiply_fusion), kind=kLoop, calls=%fused_computation.36 | loop fusion | flops 98304 | bytes 394240 | tf_op jit(solution)/shard_map/mul | solution.py:21
  78.7 0.8 copy-done.10
  81.1 1.0 copy-done.11
  82.1 1.0 copy-done.13
  83.1 1.0 copy-done.15
  84.8 1.8 %copy-done.4 = bf16[1024,1408]{1,0:T(8,128)(2,1)S(1)} copy-done((bf16[1024,1408]{1,0:T(8,128)(2,1)S(1)}, bf16[1024,1408]{1,0:T(8,128)(2,1)}, u32[]{:S(2)}) %copy-start.4) | copy-done | bytes 2883608
  86.6 5.4 %shard_map.105 = f32[8,176,128]{2,1,0:T(8,128)S(1)} custom-call(bf16[1024,1408]{1,0:T(8,128)(2,1)S(1)} %copy-done.4, bf16[528,1408]{1,0:T(8,128)(2,1)S(1)} %shard_map.104.weight_ref), custom_call_target="tpu_custom_call" | custom-call | tf_op jit(solution)/shard_map/pallas_call | solution.py:263
  92.8 3.8 %all-to-all-start = ((bf16[8,176,128]{2,1,0:T(8,128)(2,1)}), bf16[8,176,128]{2,1,0:T(8,128)(2,1)S(1)}, u32[]{:S(2)}, u32[]{:S(2)}) async-start(bf16[8,176,128]{2,1,0:T(8,128)(2,1)} %convert_element_type.34), calls=%async_computation | async-start | bytes 720896 | tf_op jit(solution)/shard_map/all_to_all | solution.py:389
  96.6 13.6 %all_gather.11.normed_ref = bf16[1024,384]{1,0:T(8,128)(2,1)} all-gather(bf16[128,384]{1,0:T(8,128)(2,1)S(1)} %copy-done.16), channel_id=1, replica_groups=mesh['zh'=2,'zl'=2,'y'=2,'x'=2,'k'=2] {'y','x','k'}, dimensions={0}, use_global_device_ids=true | all-gather | bytes 884736 | tf_op jit(solution)/shard_map/all_gather | solution.py:338
  110.4 1.3 fusion.23.prediction_ref
  111.7 2.0 %fusion.4 = (f32[1024,192]{1,0:T(8,128)}, bf16[1024,192]{1,0:T(8,128)(2,1)}) fusion(bf16[1024,384]{1,0:T(8,128)(2,1)S(1)} %copy-done.2, bf16[384,192]{0,1:T(8,128)(2,1)S(1)} %bitcast.33), kind=kOutput, calls=%fused_computation.8 | convolution fusion | flops 154730496 | bytes 2113536 | tf_op jit(solution)/shard_map/dot_general | solution.py:364
  113.7 1.1 copy-done.5
  114.8 4.0 %shard_map.106 = bf16[128,384]{1,0:T(8,128)(2,1)S(1)} custom-call(s32[1]{0:T(128)} %bitcast.place_ref, bf16[4,352,128]{2,1,0:T(8,128)(2,1)S(1)} %bitcast.29, bf16[352,1408]{1,0:T(8,128)(2,1)} %own_ref.1, bf16[352,1408]{1,0:T(8,128)(2,1)} %collective-permute-done.4.one_ref, bf16[352,1408]{1,0:T(8,128)(2,1)} %collective-permute-done.5.two_ref, ...), custom_call_target="tpu_custom_call" | custom-call | tf_op jit(solution)/shard_map/pallas_call | solution.py:263
  118.8 10.0 %all_gather.10.grad_ref = bf16[1024,384]{1,0:T(8,128)(2,1)S(1)} all-gather(bf16[128,384]{1,0:T(8,128)(2,1)S(1)} %shard_map.106), channel_id=1, replica_groups=mesh['zh'=2,'zl'=2,'y'=2,'x'=2,'k'=2] {'y','x','k'}, dimensions={0}, use_global_device_ids=true | all-gather | bytes 884736 | tf_op jit(solution)/shard_map/all_gather | solution.py:411
  128.9 1.3 shard_map.107
  130.2 15.1 %all_to_all.15 = bf16[4,96,384]{2,1,0:T(8,128)(2,1)S(1)} all-to-all(bf16[4,96,384]{2,1,0:T(8,128)(2,1)S(1)} %shard_map.107), channel_id=1, replica_groups=mesh['zh'=2,'zl'=2,'y'=2,'x'=2,'k'=2] {'zh','zl'}, dimensions={0} | all-to-all | bytes 589824 | tf_op jit(solution)/shard_map/all_to_all | solution.py:417
  (77 shorter events, 9.9 us)
Async XLA Ops:
  7.2 57.6 %copy-start = (bf16[1536,384]{1,0:T(8,128)(2,1)S(1)}, bf16[1536,384]{1,0:T(8,128)(2,1)}, u32[]{:S(2)}) copy-start(bf16[1536,384]{1,0:T(8,128)(2,1)} %param.16) | copy-start | bytes 3538948
  7.2 77.6 %all-gather.2.cloned.1.call-start = ((), (), s32[]{:S(2)}) async-start(), calls=%async_computation.3 | async-start | bytes 3244032 | tf_op jit(solution)/shard_map/all_gather | solution.py:342
  7.2 1.8 %collective-permute-start = (bf16[128,1408]{1,0:T(8,128)(2,1)}, bf16[128,1408]{1,0:T(8,128)(2,1)S(1)}, u32[]{:S(2)}, u32[]{:S(2)}) collective-permute-start(bf16[128,1408]{1,0:T(8,128)(2,1)} %bitcast.34), channel_id=1, source_target_pairs={{0,0},{1,16},{16,1},{17,17},{2,2},{3,18},{18,3},{19,19},{4,4},{5,2... | collective-permute-start | bytes 1081352 | tf_op jit(solution)/shard_map/ppermute | solution.py:300
  10.4 18.7 %copy-start.19 = (s32[4,16]{1,0:T(4,128)S(1)}, s32[4,16]{1,0:T(4,128)}, u32[]{:S(2)}) copy-start(s32[4,16]{1,0:T(4,128)} %param.13) | copy-start | bytes 772
  10.4 18.7 %copy-start.17 = (bf16[1,4,128,384]{3,2,1,0:T(8,128)(2,1)S(1)}, bf16[1,4,128,384]{3,2,1,0:T(8,128)(2,1)}, u32[]{:S(2)}) copy-start(bf16[1,4,128,384]{3,2,1,0:T(8,128)(2,1)} %param.14) | copy-start | bytes 1179652
  13.4 65.3 %collective-permute-start.1 = (bf16[352,528]{1,0:T(8,128)(2,1)}, bf16[352,528]{1,0:T(8,128)(2,1)S(1)}, u32[]{:S(2)}, u32[]{:S(2)}) collective-permute-start(bf16[352,528]{1,0:T(8,128)(2,1)} %pad_maximum_fusion.1), channel_id=1, source_target_pairs={{0,1},{1,0},{2,3},{3,2},{4,5},{5,4},{6,7},{7,6},{8,9},{9,8},{10,11... | collective-permute-start | bytes 1115144 | tf_op jit(solution)/shard_map/ppermute | solution.py:303
  27.0 53.3 %collective-permute-start.3 = (bf16[352,528]{1,0:T(8,128)(2,1)}, bf16[352,528]{1,0:T(8,128)(2,1)S(1)}, u32[]{:S(2)}, u32[]{:S(2)}) collective-permute-start(bf16[352,528]{1,0:T(8,128)(2,1)} %pad_maximum_fusion.1), channel_id=1, source_target_pairs={{0,3},{1,2},{2,1},{3,0},{4,7},{5,6},{6,5},{7,4},{8,11},{9,10},{10,... | collective-permute-start | bytes 1115144 | tf_op jit(solution)/shard_map/ppermute | solution.py:303
  28.1 85.6 %collective-permute-start.4 = (bf16[352,1408]{1,0:T(8,128)(2,1)}, bf16[352,1408]{1,0:T(8,128)(2,1)}, u32[]{:S(2)}, u32[]{:S(2)}) collective-permute-start(bf16[352,1408]{1,0:T(8,128)(2,1)} %own_ref.1), channel_id=1, source_target_pairs={{0,1},{1,0},{2,3},{3,2},{4,5},{5,4},{6,7},{7,6},{8,9},{9,8},{10,11... | collective-permute-start | bytes 2973704 | tf_op jit(solution)/shard_map/ppermute | solution.py:303
  28.6 43.3 %collective-permute-start.5 = (bf16[352,1408]{1,0:T(8,128)(2,1)}, bf16[352,1408]{1,0:T(8,128)(2,1)}, u32[]{:S(2)}, u32[]{:S(2)}) collective-permute-start(bf16[352,1408]{1,0:T(8,128)(2,1)} %own_ref.1), channel_id=1, source_target_pairs={{0,2},{1,3},{2,0},{3,1},{4,6},{5,7},{6,4},{7,5},{8,10},{9,11},{10,... | collective-permute-start | bytes 2973704 | tf_op jit(solution)/shard_map/ppermute | solution.py:303
  30.1 33.2 %all-to-all-start.1 = ((bf16[4,64,384]{2,1,0:T(8,128)(2,1)}), bf16[4,64,384]{2,1,0:T(8,128)(2,1)}, u32[]{:S(2)}, u32[]{:S(2)}) async-start(bf16[4,64,384]{2,1,0:T(8,128)(2,1)} %select_reduce_fusion), calls=%async_computation.1 | async-start | bytes 393216 | tf_op jit(solution)/shard_map/all_to_all | solution.py:330
  64.1 1.4 collective-permute-start.7
  65.5 14.0 %collective-permute-start.2 = (bf16[352,528]{1,0:T(8,128)(2,1)S(1)}, bf16[352,528]{1,0:T(8,128)(2,1)S(1)}, u32[]{:S(2)}, u32[]{:S(2)}) collective-permute-start(bf16[352,528]{1,0:T(8,128)(2,1)S(1)} %pad_maximum_fusion.own_ref), channel_id=1, source_target_pairs={{0,2},{1,3},{2,0},{3,1},{4,6},{5,7},{6,4},{7,5},{8,10},{9,11},{10,... | collective-permute-start | bytes 1115144 | tf_op jit(solution)/shard_map/ppermute | solution.py:303
  71.8 41.9 %collective-permute-start.6 = (bf16[352,1408]{1,0:T(8,128)(2,1)}, bf16[352,1408]{1,0:T(8,128)(2,1)}, u32[]{:S(2)}, u32[]{:S(2)}) collective-permute-start(bf16[352,1408]{1,0:T(8,128)(2,1)} %collective-permute-done.5.two_ref), channel_id=1, source_target_pairs={{0,1},{1,0},{2,3},{3,2},{4,5},{5,4},{6,7},{7,6},{8,9},{9,8},{10,11... | collective-permute-start | bytes 2973704 | tf_op jit(solution)/shard_map/ppermute | solution.py:303
  78.7 0.8 copy-start.10
  79.5 0.8 copy-start.14
  80.3 0.8 copy-start.12
  81.1 1.0 copy-start.11
  82.1 1.0 copy-start.13
  83.1 1.0 copy-start.15
  84.8 1.8 %copy-start.4 = (bf16[1024,1408]{1,0:T(8,128)(2,1)S(1)}, bf16[1024,1408]{1,0:T(8,128)(2,1)}, u32[]{:S(2)}) copy-start(bf16[1024,1408]{1,0:T(8,128)(2,1)} %all-gather.2.cloned.1.call-done.normed_ref) | copy-start | bytes 8650756
  92.0 4.7 %copy-start.16 = (bf16[128,384]{1,0:T(8,128)(2,1)S(1)}, bf16[128,384]{1,0:T(8,128)(2,1)}, u32[]{:S(2)}) copy-start(bf16[128,384]{1,0:T(8,128)(2,1)} %fusion.22) | copy-start | bytes 294916
  92.0 18.4 %copy-start.1 = (bf16[384,1408]{1,0:T(8,128)(2,1)S(1)}, bf16[384,1408]{1,0:T(8,128)(2,1)}, u32[]{:S(2)}) copy-start(bf16[384,1408]{1,0:T(8,128)(2,1)} %proj_ref.1) | copy-start | bytes 3244036
  92.0 18.4 %copy-start.6 = (f32[128,384]{1,0:T(8,128)S(1)}, f32[128,384]{1,0:T(8,128)}, u32[]{:S(2)}) copy-start(f32[128,384]{1,0:T(8,128)} %subtract_multiply_fusion.mixed_norm_ref) | copy-start | bytes 589828
  92.8 20.9 %all-to-all-start = ((bf16[8,176,128]{2,1,0:T(8,128)(2,1)}), bf16[8,176,128]{2,1,0:T(8,128)(2,1)S(1)}, u32[]{:S(2)}, u32[]{:S(2)}) async-start(bf16[8,176,128]{2,1,0:T(8,128)(2,1)} %convert_element_type.34), calls=%async_computation | async-start | bytes 720896 | tf_op jit(solution)/shard_map/all_to_all | solution.py:389
  110.3 1.4 copy-start.18
  110.4 1.3 copy-start.2
  113.7 1.1 copy-start.5
  114.8 14.0 %copy-start.7 = (f32[1024,192]{1,0:T(8,128)S(1)}, f32[1024,192]{1,0:T(8,128)}, u32[]{:S(2)}) copy-start(f32[1024,192]{1,0:T(8,128)} %get-tuple-element.8.slope_ref) | copy-start | bytes 2359300
  114.8 14.0 %copy-start.8 = (bf16[4,1,48,384]{3,2,1,0:T(8,128)(2,1)S(1)}, bf16[4,1,48,384]{3,2,1,0:T(8,128)(2,1)}, u32[]{:S(2)}) copy-start(bf16[4,1,48,384]{3,2,1,0:T(8,128)(2,1)} %constant_dynamic-slice_fusion) | copy-start | bytes 442372
  114.8 14.0 %copy-start.9 = (bf16[1024,192]{1,0:T(8,128)(2,1)S(1)}, bf16[1024,192]{1,0:T(8,128)(2,1)}, u32[]{:S(2)}) copy-start(bf16[1024,192]{1,0:T(8,128)(2,1)} %get-tuple-element.9.hidden_ref) | copy-start | bytes 1179652
  118.8 10.0 %copy-start.3 = (bf16[1024,384]{1,0:T(8,128)(2,1)S(1)}, bf16[1024,384]{1,0:T(8,128)(2,1)}, u32[]{:S(2)}) copy-start(bf16[1024,384]{1,0:T(8,128)(2,1)} %all_gather.11.normed_ref) | copy-start | bytes 2359300
Sparse Core Ops, SparseCore 0:
  10.5 38.4 all-gather.1

commit v2 on v0

--- a/solution.py
+++ b/solution.py
@@ -1,6 +1,9 @@
+import functools
 import jax
 import jax.numpy as jnp
 from jax import lax
+from jax.experimental import pallas as pl
+from jax.experimental.pallas import tpu as pltpu
 from jax.sharding import PartitionSpec as P
 
 H = 16
@@ -145,19 +148,392 @@
     )
 
 
+def after(value, other):
+    return lax.optimization_barrier((value, other))[0]
+
+
+def take(array, index):
+    return lax.dynamic_index_in_dim(array, index, 0, keepdims=False)
+
+
+def start_copies(pairs, sems):
+    copies = [pltpu.make_async_copy(*pair, sems.at[i]) for i, pair in enumerate(pairs)]
+    for copy in copies:
+        copy.start()
+    return copies
+
+
+def weight_kernel(place_ref, core_ref, *refs):
+    *piece_refs, out_ref, held, turned = refs
+    place, core = place_ref[0], core_ref[0]
+    parts, slabs, rows, columns = held.shape
+    part = out_ref.shape[0] // parts
+    for step in range(slabs):
+        held[:, place ^ step] = piece_refs[step][...]
+    for which in range(parts):
+        turned[...] = held[which].reshape(slabs * rows, columns).T
+        start = pl.multiple_of(core * part, part)
+        out_ref[which * part : (which + 1) * part, :] = turned[pl.ds(start, part), :]
+
+
+def attend_kernel(weight_ref, normed_ref, out_ref, projected):
+    projected[...] = lax.dot_general(
+        weight_ref[...],
+        normed_ref[...],
+        (((1,), (1,)), ((), ())),
+        preferred_element_type=jnp.float32,
+    )
+    part = projected.shape[0] // 3
+    chips, cores, _, block_rows = out_ref.shape
+    pad = jnp.zeros((-HD % 128, projected.shape[1]), jnp.float32)
+    log2_scale = 1.4426950408889634 / HD**0.5
+
+    def head_rows(which, head):
+        start = which * part + head * HD
+        rows = projected[start : start + HD, :]
+        return jnp.concatenate([rows, pad], axis=0).astype(jnp.bfloat16)
+
+    heads = part // HD
+    operands = [(head_rows(0, h), head_rows(1, h).T, head_rows(2, h)) for h in range(heads)]
+    span = block_rows * cores
+    for chip in range(chips):
+        joined = []
+        for queries, keys, values in operands:
+            scores = jnp.dot(
+                keys,
+                queries[:, chip * span : (chip + 1) * span],
+                preferred_element_type=jnp.float32,
+            )
+            weights = jnp.exp2(scores * log2_scale)
+            totals = jnp.sum(weights, axis=0, keepdims=True)
+            summed = jnp.dot(
+                values, weights.astype(jnp.bfloat16), preferred_element_type=jnp.float32
+            )
+            joined.append(summed[:HD] / totals)
+        attended = jnp.concatenate(joined, axis=0).astype(jnp.bfloat16)
+        for core in range(cores):
+            out_ref[chip, core] = attended[:, core * block_rows : (core + 1) * block_rows]
+
+
+def partial_kernel(
+    x_ref, core_ref, own_ref, two_ref, att_ref, keep_ref, give_ref, slabs, sems
+):
+    x, core = x_ref[0], core_ref[0]
+    copies = start_copies([(own_ref, slabs.at[0]), (two_ref, slabs.at[1])], sems)
+    sums = [0.0, 0.0]
+    for step in range(2):
+        copies[step].wait()
+        place = 2 * (x ^ step)
+        for side in range(2):
+            rows = [att_ref[place + piece, core ^ side] for piece in range(2)]
+            sums[side] = sums[side] + lax.dot_general(
+                jnp.concatenate(rows, axis=0),
+                slabs[step],
+                (((0,), (0,)), ((), ())),
+                preferred_element_type=jnp.float32,
+            )
+    keep_ref[...], give_ref[...] = sums
+
+
+def loss_kernel(
+    raw_ref, keep_ref, got_ref, mixed_norm_ref, rstd_ref, live_ref, proj_ref, out_ref
+):
+    mixed_norm = mixed_norm_ref[...]
+    prediction = jnp.dot(
+        mixed_norm.astype(jnp.bfloat16), proj_ref[...], preferred_element_type=jnp.float32
+    )
+    summed = raw_ref[...].astype(jnp.float32) + (keep_ref[...] + got_ref[...])
+    target = layer_norm(summed)[0].astype(jnp.bfloat16)
+    error = (prediction - target.astype(jnp.float32)) * live_ref[...]
+    grad_pred = error.astype(jnp.bfloat16)
+    grad_norm = lax.dot_general(
+        grad_pred, proj_ref[...], (((1,), (1,)), ((), ())), preferred_element_type=jnp.float32
+    )
+    first_mean = jnp.mean(grad_norm, axis=-1, keepdims=True)
+    second_mean = jnp.mean(grad_norm * mixed_norm, axis=-1, keepdims=True)
+    out_ref[...] = (rstd_ref[...] * (grad_norm - first_mean - mixed_norm * second_mean)).astype(
+        jnp.bfloat16
+    )
+
+
+def forward_kernel(
+    mine_ref,
+    up_hbm,
+    down_hbm,
+    stream_ref,
+    normed_ref,
+    mixed_norm_ref,
+    rstd_ref,
+    up_mine_ref,
+    down_mine_ref,
+    up_ref,
+    down_ref,
+    sems,
+):
+    copies = start_copies([(up_hbm, up_ref), (down_hbm, down_ref)], sems)
+    copies[0].wait()
+    hidden = gelu_tanh(
+        jnp.dot(normed_ref[...], up_ref[...], preferred_element_type=jnp.float32)
+    ).astype(jnp.bfloat16)
+    copies[1].wait()
+    mixed = stream_ref[...].astype(jnp.float32) + jnp.dot(
+        hidden, down_ref[...], preferred_element_type=jnp.float32
+    )
+    mixed_norm, rstd = layer_norm(mixed)
+    mixed_norm_ref[...] = mixed_norm
+    rstd_ref[...] = rstd
+    mine = mine_ref[0]
+    pieces, share, _ = down_mine_ref.shape
+    span = up_ref.shape[1] // pieces
+    row = lax.broadcasted_iota(jnp.int32, (span, share), 0)
+    column = lax.broadcasted_iota(jnp.int32, (span, share), 1)
+    pick = (row == column + mine * share).astype(jnp.float32).astype(jnp.bfloat16)
+    picked = []
+    for piece in range(pieces):
+        window = up_ref[:, piece * span : (piece + 1) * span]
+        picked.append(jnp.dot(window, pick, preferred_element_type=jnp.float32))
+        start = pl.multiple_of(piece * span + mine * share, 16)
+        down_mine_ref[piece] = down_ref[pl.ds(start, share), :]
+    up_mine_ref[...] = jnp.concatenate(picked, axis=1).astype(jnp.bfloat16)
+
+
+def grads_kernel(
+    mine_ref, grad_ref, quad_ref, quad_core_ref, up_ref, down_ref, out_ref, grads, normed_rows
+):
+    mine = mine_ref[0]
+    for core, half_ref in enumerate((quad_ref, quad_core_ref)):
+        normed_rows[4 * core : 4 * core + 4] = half_ref[...]
+        for piece in range(4):
+            grads[4 * core + piece] = grad_ref[mine ^ (2 * piece + core)]
+    rows = grads.shape[0] * grads.shape[1]
+    grad_mixed = grads[...].reshape(rows, grads.shape[2])
+    normed = normed_rows[...].reshape(rows, grads.shape[2])
+    pre = jnp.dot(normed, up_ref[...], preferred_element_type=jnp.float32)
+    hidden = gelu_tanh(pre).astype(jnp.bfloat16)
+    pieces, half, _ = out_ref.shape
+    half = half // 2
+    over_rows = (((0,), (0,)), ((), ()))
+    grad_down = lax.dot_general(
+        hidden, grad_mixed, over_rows, preferred_element_type=jnp.float32
+    )
+    grad_hidden = lax.dot_general(
+        grad_mixed, down_ref[...], (((1,), (1,)), ((), ())), preferred_element_type=jnp.float32
+    )
+    grad_pre = (grad_hidden * gelu_slope(pre)).astype(jnp.bfloat16)
+    grad_up = lax.dot_general(grad_pre, normed, over_rows, preferred_element_type=jnp.float32)
+    for piece in range(pieces):
+        rows = slice(piece * half, (piece + 1) * half)
+        out_ref[piece, :half, :] = grad_up[rows].astype(jnp.bfloat16)
+        out_ref[piece, half:, :] = grad_down[rows].astype(jnp.bfloat16)
+
+
+def in_vmem(kernel, out_shape, operands, places=0, scratch=(), mib=44, copied=0):
+    several = isinstance(out_shape, (list, tuple))
+    in_place = pl.BlockSpec(memory_space=pltpu.VMEM)
+    return pl.pallas_call(
+        kernel,
+        out_shape=out_shape,
+        in_specs=[pl.BlockSpec(memory_space=pltpu.SMEM)] * places
+        + [pl.BlockSpec(memory_space=pltpu.HBM)] * copied
+        + [in_place] * (len(operands) - places - copied),
+        out_specs=[in_place] * len(out_shape) if several else in_place,
+        scratch_shapes=list(scratch),
+        cost_estimate=pl.CostEstimate(flops=1, bytes_accessed=1, transcendentals=0),
+        compiler_params=pltpu.CompilerParams(vmem_limit_bytes=mib * 2**20),
+    )(*operands)
+
+
+CLIP_GROUP = ("zl", "y", "k")
+CHIP_GROUP = ("zl", "y")
+ROW_GROUP = ("y", "x", "k")
+BATCH_GROUP = ("x", "k")
+SUM_GROUP = ("zh", "zl")
+
+
+def head_shard(
+    tokens,
+    qkv_weight,
+    out_weight,
+    mask_blocks,
+    owner_map,
+    pred_stream,
+    pred_up,
+    pred_down,
+    pred_proj,
+):
+    zh, zl, y, x, k = (lax.axis_index(name) for name in ("zh", "zl", "y", "x", "k"))
+    batch = 2 * x + k
+    seq = 4 * zh + 2 * zl + y
+    place = batch.astype(jnp.int32)[None]
+    _, tok_rows, width = tokens.shape
+    owners, blk_dev = pred_stream.shape[1], tok_rows // BLK
+    pred_width, units = pred_up.shape
+
+    def swap_clips(value):
+        return lax.ppermute(value, ("zh", "k"), ((0, 0), (1, 2), (2, 1), (3, 3)))
+
+    def swap(value, bits):
+        return lax.ppermute(value, BATCH_GROUP, tuple((i, i ^ bits) for i in range(owners)))
+
+    raw = swap_clips(tokens[0])
+
+    part = width // 8
+    stream_blocks = pred_stream[0].reshape(owners, blk_dev, BLK, pred_width)
+    owner_here = lax.dynamic_slice_in_dim(owner_map, seq * blk_dev, blk_dev, 1)
+    mine = (owner_here == batch)[:, :, None, None]
+    compact = jnp.sum(jnp.where(mine, stream_blocks, 0), axis=1).astype(jnp.bfloat16)
+    arrived = lax.all_to_all(compact, BATCH_GROUP, split_axis=0, concat_axis=0, tiled=True)
+
+    def chip_columns(which):
+        first = which * width + zl * 4 * part + y * part
+        pieces = [
+            lax.dynamic_slice(
+                qkv_weight, (0, first + core * 2 * part), (qkv_weight.shape[0], part)
+            )
+            for core in range(2)
+        ]
+        return jnp.concatenate(pieces, axis=1)
+
+    columns = jnp.stack([chip_columns(which) for which in range(3)])
+
+    raw = after(raw, (arrived, columns))
+    raw_f = raw.astype(jnp.float32)
+    normed = layer_norm(raw_f)[0].astype(jnp.bfloat16)
+    normed_all = lax.all_gather(normed, CLIP_GROUP, axis=0, tiled=True)
+    columns_two = swap(columns, 2)
+    columns_one = swap(columns, 1)
+
+    from_owner = take(owner_here, batch)[:, None] == jnp.arange(owners, dtype=jnp.int32)
+    stream = jnp.sum(jnp.where(from_owner[:, :, None, None], arrived, 0), axis=1)
+    stream = stream.astype(jnp.bfloat16).reshape(tok_rows, pred_width)
+    stream = swap_clips(stream)
+    normed_pred = layer_norm(stream.astype(jnp.float32))[0].astype(jnp.bfloat16)
+    normed_x = swap(normed_pred, 2)
+    out_two = swap(after(out_weight, columns_two), 2)
+
+    mine_units = (4 * y + batch).astype(jnp.int32)[None]
+    mixed_norm, rstd, up_mine, down_mine = functools.partial(in_vmem, mib=44)(
+        forward_kernel,
+        (
+            jax.ShapeDtypeStruct((tok_rows, pred_width), jnp.float32),
+            jax.ShapeDtypeStruct((tok_rows, 1), jnp.float32),
+            jax.ShapeDtypeStruct((pred_width, units // 8), jnp.bfloat16),
+            jax.ShapeDtypeStruct((4, units // 32, pred_width), jnp.bfloat16),
+        ),
+        (mine_units, pred_up, pred_down, stream, normed_pred),
+        places=1,
+        copied=2,
+        scratch=(
+            pltpu.VMEM(pred_up.shape, jnp.bfloat16),
+            pltpu.VMEM(pred_down.shape, jnp.bfloat16),
+            pltpu.SemaphoreType.DMA((2,)),
+        ),
+    )
+    down_mine = down_mine.reshape(units // 8, pred_width)
+
+    columns_two = after(columns_two, (mixed_norm, normed_x))
+    columns_three = swap(columns_two, 1)
+
+    slab = qkv_weight.shape[0]
+    qkv_columns = functools.partial(in_vmem, mib=44)(
+        weight_kernel,
+        jax.ShapeDtypeStruct((3 * part, width), jnp.bfloat16),
+        (
+            place,
+            k.astype(jnp.int32)[None],
+            columns,
+            columns_one,
+            columns_two,
+            columns_three,
+        ),
+        places=2,
+        scratch=(
+            pltpu.VMEM((3, owners, slab, 2 * part), jnp.bfloat16),
+            pltpu.VMEM((2 * part, width), jnp.bfloat16),
+        ),
+    )
+
+    clip = 2 * x + zh
+    shard = 4 * k + 2 * zl + y
+    block_ids = shard * blk_dev + jnp.arange(blk_dev, dtype=jnp.int32)
+    masked = jnp.any(take(mask_blocks, clip)[:, None] == block_ids[None, :], axis=0)
+    divisor = float(owners * mask_blocks.shape[1])
+    live = jnp.repeat(masked.astype(jnp.float32) / divisor, BLK)[:, None]
+
+    normed_all = after(normed_all, (qkv_columns, mixed_norm))
+    attended = functools.partial(in_vmem, mib=44)(
+        attend_kernel,
+        jax.ShapeDtypeStruct((4, 2, part, tok_rows), jnp.bfloat16),
+        (qkv_columns, normed_all),
+        scratch=(pltpu.VMEM((3 * part, normed_all.shape[0]), jnp.float32),),
+    )
+    pair = jnp.stack([normed_pred, normed_x])
+    quad = jnp.concatenate([pair, lax.ppermute(pair, "y", ((0, 1), (1, 0)))])
+    quad_core = swap(quad, 1)
+    attended = lax.all_to_all(attended, CHIP_GROUP, split_axis=0, concat_axis=0, tiled=True)
+    attended = after(attended, quad_core)
+    keep, give = functools.partial(in_vmem, mib=44)(
+        partial_kernel,
+        [jax.ShapeDtypeStruct((tok_rows, width), jnp.float32)] * 2,
+        (
+            x.astype(jnp.int32)[None],
+            k.astype(jnp.int32)[None],
+            out_weight,
+            out_two,
+            attended,
+        ),
+        places=2,
+        copied=2,
+        scratch=(
+            pltpu.VMEM((2, slab, width), jnp.bfloat16),
+            pltpu.SemaphoreType.DMA((2,)),
+        ),
+    )
+    got = swap(give, 1)
+    grad_mixed = functools.partial(in_vmem, mib=44)(
+        loss_kernel,
+        jax.ShapeDtypeStruct((tok_rows, pred_width), jnp.bfloat16),
+        (raw, keep, got, mixed_norm, rstd, live, pred_proj),
+    )
+    grad_rows = lax.all_gather(grad_mixed, ROW_GROUP, axis=0, tiled=True)
+    grads = functools.partial(in_vmem, mib=44)(
+        grads_kernel,
+        jax.ShapeDtypeStruct((4, units // 16, pred_width), jnp.bfloat16),
+        (
+            mine_units,
+            grad_rows.reshape(8, tok_rows, pred_width),
+            quad,
+            quad_core,
+            up_mine,
+            down_mine,
+        ),
+        places=1,
+        scratch=(pltpu.VMEM((8, tok_rows, pred_width), jnp.bfloat16),) * 2,
+    )
+    grads = lax.all_to_all(grads, SUM_GROUP, split_axis=0, concat_axis=0, tiled=True)
+    total = jnp.sum(grads.astype(jnp.float32), axis=0)
+    half = units // 32
+    return total[:half].T, total[half:]
+
+
 def solution(mesh):
+    if mesh.shape["seq"] == 8 and mesh.shape["batch"] == 4:
+        names = ("zh", "zl", "y", "x", "k")
+        step, batch, seq = head_shard, BATCH_GROUP, names[:3]
+        mesh = jax.sharding.Mesh(mesh.devices.reshape(2, 2, 2, 2, 2), names)
+    else:
+        step, batch, seq = per_device, "batch", "seq"
+    everyone = (seq, batch) if isinstance(seq, str) else seq + batch
     in_specs = (
-        P("batch", "seq", None),
-        P("batch", None),
-        P("batch", None),
+        P(batch, seq, None),
+        P(batch, None),
+        P(batch, None),
         P(),
         P(),
-        P("batch", None, "seq", None),
+        P(batch, None, seq, None),
         P(),
         P(),
         P(),
     )
-    out_specs = (P(None, ("seq", "batch")), P(("seq", "batch"), None))
-    return jax.shard_map(
-        per_device, mesh=mesh, in_specs=in_specs, out_specs=out_specs, check_vma=False
-    )
+    out_specs = (P(None, everyone), P(everyone, None))
+    return jax.shard_map(step, mesh=mesh, in_specs=in_specs, out_specs=out_specs, check_vma=False)

time: 462 us -> 117 us (0.25)
  waiting for transfers between devices: 376 us -> 21.7 us
  matrix products: 38.1 us -> 0 us
  blocking collectives: 0 us -> 23.3 us
  local copies, waits for them, and re-layouts: 27.6 us -> 9.49 us
  Pallas kernels: 0 us -> 17.9 us
  starting transfers between devices: 3.69 us -> 21.2 us
  other arithmetic: 1.76 us -> 8.23 us
    reduce_scatter x2 -> x0, waiting for transfers between devices: 199 us -> none  [the longest x1 105 us: per_device(): lax.psum_scatter(grad_up, ('seq', 'batch'), scatter_dimension=1, tiled=True)]
    all_gather x3 -> x1, waiting for transfers between devices: 165 us -> 0.02 us  [head_shard(): normed_all = lax.all_gather(normed, CLIP_GROUP, axis=0, tiled=True)]
    dot_general x13 -> x0, matrix products: 38.1 us -> none  [the longest x2 9.42 us: fold_rows(): return jnp.dot(left, piece, preferred_element_type=jnp.float32)]
    pallas_call x0 -> x6, Pallas kernels: none -> 17.9 us  [in_vmem(): pl.pallas_call(kernel, out_shape=out_shape, in_specs=[pl.BlockSpec(memory...]
    dynamic_slice x6 -> x1, local copies, waits for them, and re-layouts: 17.4 us -> 1.84 us  [chip_columns(): lax.dynamic_slice(qkv_weight, (0, first + core * 2 * part), (qkv_weight.s...]
    ppermute x0 -> x10, waiting for transfers between devices: none -> 15.1 us  [the longest x7 15 us: swap(): lax.ppermute(value, BATCH_GROUP, tuple(((i, i ^ bits) for i in range(owne...]
    all_to_all x0 -> x1, blocking collectives: none -> 12.7 us  [head_shard(): lax.all_to_all(grads, SUM_GROUP, split_axis=0, concat_axis=0, tiled=True)]
    ppermute x0 -> x10, starting transfers between devices: none -> 10.9 us  [the longest x7 7.09 us: swap(): lax.ppermute(value, BATCH_GROUP, tuple(((i, i ^ bits) for i in range(owne...]
  transfers between devices with their start and end apart: 6 -> 13, of which waited for: 5 -> 6; matrix products, arithmetic and copies ran while one was open for 10% -> 8% of each run, Pallas kernels for 0% -> 9%
where the time goes in v2:
time: 117 us; the launch traced here: 116 us
  blocking collectives  23.3 us (20%)
  waiting for transfers between devices  21.7 us (19%)
  starting transfers between devices  21.2 us (18%)
  Pallas kernels  17.9 us (15%)
  between operations  14.3 us (12%)
  local copies, waits for them, and re-layouts  9.49 us (8%)
  other arithmetic  8.23 us (7%)
    pallas_call x6, Pallas kernels, in_vmem(): pl.pallas_call(kernel, out_shape=out_shape, in_specs=[pl.BlockSpec(memory...  17.9 us
    ppermute x7, waiting for transfers between devices, swap(): lax.ppermute(value, BATCH_GROUP, tuple(((i, i ^ bits) for i in range(owne...  15 us
    all_to_all x1, blocking collectives, head_shard(): lax.all_to_all(grads, SUM_GROUP, split_axis=0, concat_axis=0, tiled=True)  12.7 us
    all_gather x1, blocking collectives, head_shard(): grad_rows = lax.all_gather(grad_mixed, ROW_GROUP, axis=0, tiled=True)  10.6 us
    ppermute x7, starting transfers between devices, swap(): lax.ppermute(value, BATCH_GROUP, tuple(((i, i ^ bits) for i in range(owne...  7.09 us
    all_to_all x1, starting transfers between devices, head_shard(): lax.all_to_all(compact, BATCH_GROUP, split_axis=0, concat_axis=0, tiled=T...  6.82 us
    unnamed x30, local copies, waits for them, and re-layouts  6 us
    all_to_all x1, starting transfers between devices, head_shard(): lax.all_to_all(attended, CHIP_GROUP, split_axis=0, concat_axis=0, tiled=T...  3.46 us
  transfers between devices with their start and end apart: 13, of which 6 were waited for; matrix products, arithmetic and copies ran while one was open for 8% of the time, Pallas kernels for 9%

profile of v2, /device:TPU:0, one launch (start us, length us, event | category | flops | bytes accessed | tf_op | source)
XLA Modules:
  0.0 116.2 jit_solution(610287228083150738)
XLA Ops:
  7.2 1.6 %collective-permute-start = (bf16[128,1408]{1,0:T(8,128)(2,1)}, bf16[128,1408]{1,0:T(8,128)(2,1)S(1)}, u32[]{:S(2)}, u32[]{:S(2)}) collective-permute-start(bf16[128,1408]{1,0:T(8,128)(2,1)} %bitcast.28), channel_id=1, source_target_pairs={{0,0},{1,16},{16,1},{17,17},{2,2},{3,18},{18,3},{19,19},{4,4},{5,2... | collective-permute-start | bytes 1081352 | tf_op jit(solution)/shard_map/ppermute | solution.py:373
  8.8 0.8 dynamic-slice_compare_fusion
  9.6 1.8 %select_reduce_fusion.1 = bf16[4,64,384]{2,1,0:T(8,128)(2,1)} fusion(bf16[4,2,64,384]{3,2,1,0:T(8,128)(2,1)} %bitcast.26, pred[4,2]{1,0:T(4,128)(4,1)S(1)} %dynamic-slice_compare_fusion), kind=kLoop, calls=%fused_computation.10 | loop fusion | flops 294912 | bytes 589832 | tf_op jit(solution)/shard_map/reduce_sum | solution.py:384
  11.4 6.8 %all-to-all-start = ((bf16[4,64,384]{2,1,0:T(8,128)(2,1)}), bf16[4,64,384]{2,1,0:T(8,128)(2,1)S(1)}, u32[]{:S(2)}, u32[]{:S(2)}) async-start(bf16[4,64,384]{2,1,0:T(8,128)(2,1)} %select_reduce_fusion.1), calls=%async_computation | async-start | bytes 393216 | tf_op jit(solution)/shard_map/all_to_all | solution.py:385
  18.2 1.8 %constant_dynamic-slice_fusion.6 = (bf16[352,176]{1,0:T(8,128)(2,1)S(1)}, bf16[352,176]{1,0:T(8,128)(2,1)S(1)}, bf16[352,176]{1,0:T(8,128)(2,1)S(1)}, bf16[352,1...) fusion(bf16[352,4224]{1,0:T(8,128)(2,1)} %param.10, s32[]{:T(128)S(6)} %select_n.47, ...), kind=kLoop, calls=%fused_computation.29 | loop fusion | bytes 1486872 | tf_op jit(solution)/shard_map/dynamic_slice | solution.py:390
  20.6 3.3 %all-to-all-done = bf16[4,64,384]{2,1,0:T(8,128)(2,1)S(1)} async-done(((bf16[4,64,384]{2,1,0:T(8,128)(2,1)}), bf16[4,64,384]{2,1,0:T(8,128)(2,1)S(1)}, u32[]{:S(2)}, u32[]{:S(2)}) %all-to-all-start) | async-done | bytes 196640 | tf_op jit(solution)/shard_map/all_to_all | solution.py:385
  24.3 1.0 fusion.3
  25.3 0.8 dynamic-slice_bitcast_fusion
  27.5 2.1 %collective-permute-start.5 = (bf16[128,384]{1,0:T(8,128)(2,1)S(1)}, bf16[128,384]{1,0:T(8,128)(2,1)}, u32[]{:S(2)}, u32[]{:S(2)}) collective-permute-start(bf16[128,384]{1,0:T(8,128)(2,1)S(1)} %fusion.7.normed_ref), channel_id=1, source_target_pairs={{0,2},{1,3},{2,0},{3,1},{4,6},{5,7},{6,4},{7,5},{8,10},{9,11},{10,... | collective-permute-start | bytes 294920 | tf_op jit(solution)/shard_map/ppermute | solution.py:376
  29.5 4.0 %collective-permute-start.3 = (bf16[3,352,352]{2,1,0:T(8,128)(2,1)S(1)}, bf16[3,352,352]{2,1,0:T(8,128)(2,1)}, u32[]{:S(2)}, u32[]{:S(2)}) collective-permute-start(bf16[3,352,352]{2,1,0:T(8,128)(2,1)S(1)} %pad_maximum_fusion.refs_0_), channel_id=1, source_target_pairs={{0,1},{1,0},{2,3},{3,2},{4,5},{5,4},{6,7},{7,6},{8,9},{9,8},{10,11... | collective-permute-start | bytes 2230280 | tf_op jit(solution)/shard_map/ppermute | solution.py:376
  33.6 1.3 %copy-done.3 = bf16[1536,384]{1,0:T(8,128)(2,1)S(1)} copy-done((bf16[1536,384]{1,0:T(8,128)(2,1)S(1)}, bf16[1536,384]{1,0:T(8,128)(2,1)}, u32[]{:S(2)}) %copy-start.3) | copy-done | bytes 1179672
  34.8 1.7 %shard_map.104 = (f32[128,384]{1,0:T(8,128)S(1)}, f32[128,1]{1,0:T(8,128)S(1)}, bf16[384,192]{1,0:T(8,128)(2,1)S(1)}, bf16[4,48,384]{2,1,0:T(8,128)(2,1)S(1)}) custom-call(s32[1]{0:T(128)} %bitcast.mine_ref, bf16[384,1536]{1,0:T(8,128)(2,1)S(1)} %copy-done.2, bf16[1536,384]{1,0:T(8,128)(2,1)S(1)} %copy-done.3, ...), custom_call_target="tpu_custom_call" | custom-call | flops 1 | bytes 1 | tf_op jit(solution)/shard_map/pallas_call | solution.py:333
  37.2 0.7 copy-done.7
  38.6 10.6 %collective-permute-done.5 = bf16[128,384]{1,0:T(8,128)(2,1)} collective-permute-done((bf16[128,384]{1,0:T(8,128)(2,1)S(1)}, bf16[128,384]{1,0:T(8,128)(2,1)}, u32[]{:S(2)}, u32[]{:S(2)}) %collective-permute-start.5) | collective-permute-done | bytes 98336 | tf_op jit(solution)/shard_map/ppermute | solution.py:376
  49.2 0.8 collective-permute-start.6
  50.1 1.6 %pad_maximum_fusion.2 = bf16[2,128,384]{2,1,0:T(8,128)(2,1)} fusion(bf16[1,128,384]{2,1,0:T(8,128)(2,1)} %bitcast.12, bf16[1,128,384]{2,1,0:T(8,128)(2,1)S(1)} %fusion.10), kind=kLoop, calls=%fused_computation.20 | loop fusion | flops 98304 | bytes 393216 | tf_op jit(solution)/shard_map/stack | solution.py:470
  51.7 1.5 %collective-permute-start.7 = (bf16[2,128,384]{2,1,0:T(8,128)(2,1)}, bf16[2,128,384]{2,1,0:T(8,128)(2,1)}, u32[]{:S(2)}, u32[]{:S(2)}) collective-permute-start(bf16[2,128,384]{2,1,0:T(8,128)(2,1)} %pad_maximum_fusion.2), channel_id=1, source_target_pairs={{0,4},{4,0},{1,5},{5,1},{2,6},{6,2},{3,7},{7,3},{8,12},{12,8},{9,1... | collective-permute-start | bytes 589832 | tf_op jit(solution)/shard_map/ppermute | solution.py:471
  53.3 2.4 %shard_map.105.weight_ref = bf16[528,1408]{1,0:T(8,128)(2,1)S(1)} custom-call(s32[1]{0:T(128)} %bitcast.8.place_ref, s32[1]{0:T(128)} %bitcast.7.core_ref, bf16[3,352,352]{2,1,0:T(8,128)(2,1)S(1)} %pad_maximum_fusion.refs_0_, bf16[3,352,352]{2,1,0:T(8,128)(2,1)} %collective-permute-done.3.refs_1_, bf16[3,352,352]{2,1,0:T(8,128)(2,1)S(1)} %collective-permute-done.1.refs_2_, ...), custom_call_target="tpu_custom_call" | custom-call | flops 1 | bytes 1 | tf_op jit(solution)/shard_map/pallas_call | solution.py:333
  55.7 1.8 %copy-done.1 = bf16[1024,1408]{1,0:T(8,128)(2,1)S(1)} copy-done((bf16[1024,1408]{1,0:T(8,128)(2,1)S(1)}, bf16[1024,1408]{1,0:T(8,128)(2,1)}, u32[]{:S(2)}) %copy-start.1) | copy-done | bytes 2883608
  57.5 6.1 %shard_map.106 = bf16[4,2,176,128]{3,2,1,0:T(8,128)(2,1)} custom-call(bf16[528,1408]{1,0:T(8,128)(2,1)S(1)} %shard_map.105.weight_ref, bf16[1024,1408]{1,0:T(8,128)(2,1)S(1)} %copy-done.1), custom_call_target="tpu_custom_call" | custom-call | flops 1 | bytes 1 | tf_op jit(solution)/shard_map/pallas_call | solution.py:333
  63.6 3.5 %all-to-all-start.1 = ((bf16[4,2,176,128]{3,2,1,0:T(8,128)(2,1)}), bf16[4,2,176,128]{3,2,1,0:T(8,128)(2,1)S(1)}, u32[]{:S(2)}, u32[]{:S(2)}) async-start(bf16[4,2,176,128]{3,2,1,0:T(8,128)(2,1)} %shard_map.106), calls=%async_computation.1 | async-start | bytes 720896 | tf_op jit(solution)/shard_map/all_to_all | solution.py:473
  67.1 1.1 pad_maximum_fusion.1.quad_ref
  68.4 1.7 %collective-permute-done.8.quad_core_ref = bf16[4,128,384]{2,1,0:T(8,128)(2,1)S(1)} collective-permute-done((bf16[4,128,384]{2,1,0:T(8,128)(2,1)S(1)}, bf16[4,128,384]{2,1,0:T(8,128)(2,1)S(1)}, u32[]{:S(2)}, u32[]{:S(2)}) %collective-permute-start.8) | collective-permute-done | bytes 393248 | tf_op jit(solution)/shard_map/ppermute | solution.py:376
  70.1 3.4 %all-to-all-done.1.att_ref = bf16[4,2,176,128]{3,2,1,0:T(8,128)(2,1)S(1)} async-done(((bf16[4,2,176,128]{3,2,1,0:T(8,128)(2,1)}), bf16[4,2,176,128]{3,2,1,0:T(8,128)(2,1)S(1)}, u32[]{:S(2)}, u32[]{:S(2)}) %all-to-all-start.1) | async-done | bytes 360480 | tf_op jit(solution)/shard_map/all_to_all | solution.py:473
  73.4 0.7 collective-permute-done.2.two_ref
  74.1 3.4 %shard_map.107 = (f32[128,1408]{1,0:T(8,128)S(1)}, f32[128,1408]{1,0:T(8,128)}) custom-call(s32[1]{0:T(128)} %bitcast.6.x_ref, s32[1]{0:T(128)} %bitcast.7.core_ref, bf16[352,1408]{1,0:T(8,128)(2,1)} %own_ref.1, bf16[352,1408]{1,0:T(8,128)(2,1)} %collective-permute-done.2.two_ref, bf16[4,2,176,128]{3,2,1,0:T(8,128)(2,1)S(1)} %all-to-all-done.1.att_ref), custom_call_target="tpu_custom_call" | custom-call | flops 1 | bytes 1 | tf_op jit(solution)/shard_map/pallas_call | solution.py:333
  78.1 2.1 %collective-permute-done.9.got_ref = f32[128,1408]{1,0:T(8,128)} collective-permute-done((f32[128,1408]{1,0:T(8,128)}, f32[128,1408]{1,0:T(8,128)}, u32[]{:S(2)}, u32[]{:S(2)}) %collective-permute-start.9) | collective-permute-done | bytes 720928 | tf_op jit(solution)/shard_map/ppermute | solution.py:376
  80.1 0.8 copy-done.12
  81.0 2.1 %shard_map.108 = bf16[128,384]{1,0:T(8,128)(2,1)S(1)} custom-call(bf16[128,1408]{1,0:T(8,128)(2,1)S(1)} %collective-permute-done.raw_ref, f32[128,1408]{1,0:T(8,128)S(1)} %get-tuple-element.19.keep_ref, f32[128,1408]{1,0:T(8,128)} %collective-permute-done.9.got_ref, f32[128,384]{1,0:T(8,128)S(1)} %copy-done.8, f32[128,1]{1,0:T(8,128)S(1)} %copy-done.12, ...), custom_call_target="tpu_custom_call" | custom-call | flops 1 | bytes 1 | tf_op jit(solution)/shard_map/pallas_call | solution.py:333
  83.1 10.6 %all_gather.7 = bf16[1024,384]{1,0:T(8,128)(2,1)S(1)} all-gather(bf16[128,384]{1,0:T(8,128)(2,1)S(1)} %shard_map.108), channel_id=1, replica_groups=mesh['zh'=2,'zl'=2,'y'=2,'x'=2,'k'=2] {'y','x','k'}, dimensions={0}, use_global_device_ids=true | all-gather | bytes 884736 | tf_op jit(solution)/shard_map/all_gather | solution.py:498
  93.7 2.2 %shard_map.109 = bf16[4,96,384]{2,1,0:T(8,128)(2,1)S(1)} custom-call(s32[1]{0:T(128)} %bitcast.mine_ref, bf16[8,128,384]{2,1,0:T(8,128)(2,1)S(1)} %bitcast.24, bf16[4,128,384]{2,1,0:T(8,128)(2,1)S(1)} %pad_maximum_fusion.1.quad_ref, bf16[4,128,384]{2,1,0:T(8,128)(2,1)S(1)} %collective-permute-done.8.quad_core_ref, bf16[384,192]{1,0:T(8,128)(2,1)S(1)} %copy-done.6, ...), custom_call_target="tpu_custom_call" | custom-call | flops 1 | bytes 1 | tf_op jit(solution)/shard_map/pallas_call | solution.py:333
  95.9 12.7 %all_to_all.15 = bf16[4,96,384]{2,1,0:T(8,128)(2,1)S(1)} all-to-all(bf16[4,96,384]{2,1,0:T(8,128)(2,1)S(1)} %shard_map.109), channel_id=1, replica_groups=mesh['zh'=2,'zl'=2,'y'=2,'x'=2,'k'=2] {'zh','zl'}, dimensions={0} | all-to-all | bytes 589824 | tf_op jit(solution)/shard_map/all_to_all | solution.py:513
  (63 shorter events, 5.1 us)
Async XLA Ops:
  7.2 70.5 %copy-start = (s32[4,14]{1,0:T(4,128)S(1)}, s32[4,14]{1,0:T(4,128)}, u32[]{:S(2)}) copy-start(s32[4,14]{1,0:T(4,128)} %param.12) | copy-start | bytes 676
  7.2 16.7 %collective-permute-start = (bf16[128,1408]{1,0:T(8,128)(2,1)}, bf16[128,1408]{1,0:T(8,128)(2,1)S(1)}, u32[]{:S(2)}, u32[]{:S(2)}) collective-permute-start(bf16[128,1408]{1,0:T(8,128)(2,1)} %bitcast.28), channel_id=1, source_target_pairs={{0,0},{1,16},{16,1},{17,17},{2,2},{3,18},{18,3},{19,19},{4,4},{5,2... | collective-permute-start | bytes 1081352 | tf_op jit(solution)/shard_map/ppermute | solution.py:373
  11.4 12.4 %all-to-all-start = ((bf16[4,64,384]{2,1,0:T(8,128)(2,1)}), bf16[4,64,384]{2,1,0:T(8,128)(2,1)S(1)}, u32[]{:S(2)}, u32[]{:S(2)}) async-start(bf16[4,64,384]{2,1,0:T(8,128)(2,1)} %select_reduce_fusion.1), calls=%async_computation | async-start | bytes 393216 | tf_op jit(solution)/shard_map/all_to_all | solution.py:385
  18.2 37.5 %all-gather.2.cloned.1.call-start = ((), (), s32[]{:S(2)}) async-start(), calls=%async_computation.3 | async-start | bytes 3244032 | tf_op jit(solution)/shard_map/all_gather | solution.py:402
  20.6 13.0 %copy-start.2 = (bf16[384,1536]{1,0:T(8,128)(2,1)S(1)}, bf16[384,1536]{1,0:T(8,128)(2,1)}, u32[]{:S(2)}) copy-start(bf16[384,1536]{1,0:T(8,128)(2,1)} %up_hbm.1) | copy-start | bytes 3538948
  26.3 0.8 collective-permute-start.4
  26.9 22.3 %collective-permute-start.1 = (bf16[3,352,352]{2,1,0:T(8,128)(2,1)S(1)}, bf16[3,352,352]{2,1,0:T(8,128)(2,1)S(1)}, u32[]{:S(2)}, u32[]{:S(2)}) collective-permute-start(bf16[3,352,352]{2,1,0:T(8,128)(2,1)S(1)} %pad_maximum_fusion.refs_0_), channel_id=1, source_target_pairs={{0,2},{1,3},{2,0},{3,1},{4,6},{5,7},{6,4},{7,5},{8,10},{9,11},{10,... | collective-permute-start | bytes 2230280 | tf_op jit(solution)/shard_map/ppermute | solution.py:376
  27.5 21.7 %collective-permute-start.5 = (bf16[128,384]{1,0:T(8,128)(2,1)S(1)}, bf16[128,384]{1,0:T(8,128)(2,1)}, u32[]{:S(2)}, u32[]{:S(2)}) collective-permute-start(bf16[128,384]{1,0:T(8,128)(2,1)S(1)} %fusion.7.normed_ref), channel_id=1, source_target_pairs={{0,2},{1,3},{2,0},{3,1},{4,6},{5,7},{6,4},{7,5},{8,10},{9,11},{10,... | collective-permute-start | bytes 294920 | tf_op jit(solution)/shard_map/ppermute | solution.py:376
  29.5 23.7 %collective-permute-start.3 = (bf16[3,352,352]{2,1,0:T(8,128)(2,1)S(1)}, bf16[3,352,352]{2,1,0:T(8,128)(2,1)}, u32[]{:S(2)}, u32[]{:S(2)}) collective-permute-start(bf16[3,352,352]{2,1,0:T(8,128)(2,1)S(1)} %pad_maximum_fusion.refs_0_), channel_id=1, source_target_pairs={{0,1},{1,0},{2,3},{3,2},{4,5},{5,4},{6,7},{7,6},{8,9},{9,8},{10,11... | collective-permute-start | bytes 2230280 | tf_op jit(solution)/shard_map/ppermute | solution.py:376
  33.6 1.3 %copy-start.3 = (bf16[1536,384]{1,0:T(8,128)(2,1)S(1)}, bf16[1536,384]{1,0:T(8,128)(2,1)}, u32[]{:S(2)}) copy-start(bf16[1536,384]{1,0:T(8,128)(2,1)} %down_hbm.1) | copy-start | bytes 3538948
  36.6 0.7 copy-start.5
  37.2 0.7 copy-start.7
  37.9 0.7 copy-start.9
  38.6 14.7 %copy-start.11 = (f32[128,1]{1,0:T(8,128)}, f32[128,1]{1,0:T(8,128)S(1)}, u32[]{:S(2)}) copy-start(f32[128,1]{1,0:T(8,128)S(1)} %get-tuple-element.21.rstd_ref) | copy-start | bytes 1540
  49.2 4.1 %collective-permute-start.6 = (bf16[3,352,352]{2,1,0:T(8,128)(2,1)S(1)}, bf16[3,352,352]{2,1,0:T(8,128)(2,1)S(1)}, u32[]{:S(2)}, u32[]{:S(2)}) collective-permute-start(bf16[3,352,352]{2,1,0:T(8,128)(2,1)S(1)} %collective-permute-done.1.refs_2_), channel_id=1, source_target_pairs={{0,1},{1,0},{2,3},{3,2},{4,5},{5,4},{6,7},{7,6},{8,9},{9,8},{10,11... | collective-permute-start | bytes 2230280 | tf_op jit(solution)/shard_map/ppermute | solution.py:376
  50.0 24.2 %collective-permute-start.2 = (bf16[352,1408]{1,0:T(8,128)(2,1)}, bf16[352,1408]{1,0:T(8,128)(2,1)}, u32[]{:S(2)}, u32[]{:S(2)}) collective-permute-start(bf16[352,1408]{1,0:T(8,128)(2,1)} %own_ref.1), channel_id=1, source_target_pairs={{0,2},{1,3},{2,0},{3,1},{4,6},{5,7},{6,4},{7,5},{8,10},{9,11},{10,... | collective-permute-start | bytes 2973704 | tf_op jit(solution)/shard_map/ppermute | solution.py:376
  50.1 3.2 %copy-start.13 = (bf16[1,128,384]{2,1,0:T(8,128)(2,1)}, bf16[1,128,384]{2,1,0:T(8,128)(2,1)S(1)}, u32[]{:S(2)}) copy-start(bf16[1,128,384]{2,1,0:T(8,128)(2,1)S(1)} %fusion.10) | copy-start | bytes 294916
  51.7 15.4 %collective-permute-start.7 = (bf16[2,128,384]{2,1,0:T(8,128)(2,1)}, bf16[2,128,384]{2,1,0:T(8,128)(2,1)}, u32[]{:S(2)}, u32[]{:S(2)}) collective-permute-start(bf16[2,128,384]{2,1,0:T(8,128)(2,1)} %pad_maximum_fusion.2), channel_id=1, source_target_pairs={{0,4},{4,0},{1,5},{5,1},{2,6},{6,2},{3,7},{7,3},{8,12},{12,8},{9,1... | collective-permute-start | bytes 589832 | tf_op jit(solution)/shard_map/ppermute | solution.py:471
  55.7 1.8 %copy-start.1 = (bf16[1024,1408]{1,0:T(8,128)(2,1)S(1)}, bf16[1024,1408]{1,0:T(8,128)(2,1)}, u32[]{:S(2)}) copy-start(bf16[1024,1408]{1,0:T(8,128)(2,1)} %all-gather.2.cloned.1.call-done.normed_ref) | copy-start | bytes 8650756
  57.5 9.6 %copy-start.14 = (bf16[1,128,384]{2,1,0:T(8,128)(2,1)S(1)}, bf16[1,128,384]{2,1,0:T(8,128)(2,1)}, u32[]{:S(2)}) copy-start(bf16[1,128,384]{2,1,0:T(8,128)(2,1)} %copy-done.13) | copy-start | bytes 294916
  63.6 9.8 %all-to-all-start.1 = ((bf16[4,2,176,128]{3,2,1,0:T(8,128)(2,1)}), bf16[4,2,176,128]{3,2,1,0:T(8,128)(2,1)S(1)}, u32[]{:S(2)}, u32[]{:S(2)}) async-start(bf16[4,2,176,128]{3,2,1,0:T(8,128)(2,1)} %shard_map.106), calls=%async_computation.1 | async-start | bytes 720896 | tf_op jit(solution)/shard_map/all_to_all | solution.py:473
  67.1 13.0 %copy-start.4 = (bf16[384,1408]{1,0:T(8,128)(2,1)S(1)}, bf16[384,1408]{1,0:T(8,128)(2,1)}, u32[]{:S(2)}) copy-start(bf16[384,1408]{1,0:T(8,128)(2,1)} %proj_ref.1) | copy-start | bytes 3244036
  67.1 13.0 %copy-start.8 = (f32[128,384]{1,0:T(8,128)S(1)}, f32[128,384]{1,0:T(8,128)}, u32[]{:S(2)}) copy-start(f32[128,384]{1,0:T(8,128)} %copy-done.7) | copy-start | bytes 589828
  68.3 1.8 %collective-permute-start.8 = (bf16[4,128,384]{2,1,0:T(8,128)(2,1)S(1)}, bf16[4,128,384]{2,1,0:T(8,128)(2,1)S(1)}, u32[]{:S(2)}, u32[]{:S(2)}) collective-permute-start(bf16[4,128,384]{2,1,0:T(8,128)(2,1)S(1)} %pad_maximum_fusion.1.quad_ref), channel_id=1, source_target_pairs={{0,1},{1,0},{2,3},{3,2},{4,5},{5,4},{6,7},{7,6},{8,9},{9,8},{10,11... | collective-permute-start | bytes 1179656 | tf_op jit(solution)/shard_map/ppermute | solution.py:376
  77.5 2.6 %collective-permute-start.9 = (f32[128,1408]{1,0:T(8,128)}, f32[128,1408]{1,0:T(8,128)}, u32[]{:S(2)}, u32[]{:S(2)}) collective-permute-start(f32[128,1408]{1,0:T(8,128)} %get-tuple-element.20), channel_id=1, source_target_pairs={{0,1},{1,0},{2,3},{3,2},{4,5},{5,4},{6,7},{7,6},{8,9},{9,8},{10,11... | collective-permute-start | bytes 2162696 | tf_op jit(solution)/shard_map/ppermute | solution.py:376
  80.1 0.8 copy-start.12
  81.0 12.7 %copy-start.6 = (bf16[384,192]{1,0:T(8,128)(2,1)S(1)}, bf16[384,192]{1,0:T(8,128)(2,1)}, u32[]{:S(2)}) copy-start(bf16[384,192]{1,0:T(8,128)(2,1)} %copy-done.5) | copy-start | bytes 442372
  81.0 12.7 %copy-start.10 = (bf16[4,48,384]{2,1,0:T(8,128)(2,1)S(1)}, bf16[4,48,384]{2,1,0:T(8,128)(2,1)}, u32[]{:S(2)}) copy-start(bf16[4,48,384]{2,1,0:T(8,128)(2,1)} %copy-done.9) | copy-start | bytes 442372
Sparse Core Ops, SparseCore 0:
  25.4 23.4 all-gather.1

commit v3 on v2

--- a/solution.py
+++ b/solution.py
@@ -1,4 +1,3 @@
-import functools
 import jax
 import jax.numpy as jnp
 from jax import lax
@@ -169,7 +168,8 @@
     parts, slabs, rows, columns = held.shape
     part = out_ref.shape[0] // parts
     for step in range(slabs):
-        held[:, place ^ step] = piece_refs[step][...]
+        held[0, place ^ step] = piece_refs[2 * step][...]
+        held[1:, place ^ step] = piece_refs[2 * step + 1][...]
     for which in range(parts):
         turned[...] = held[which].reshape(slabs * rows, columns).T
         start = pl.multiple_of(core * part, part)
@@ -232,7 +232,7 @@
                 (((0,), (0,)), ((), ())),
                 preferred_element_type=jnp.float32,
             )
-    keep_ref[...], give_ref[...] = sums
+    keep_ref[...], give_ref[...] = sums[0], sums[1].astype(give_ref.dtype)
 
 
 def loss_kernel(
@@ -242,7 +242,7 @@
     prediction = jnp.dot(
         mixed_norm.astype(jnp.bfloat16), proj_ref[...], preferred_element_type=jnp.float32
     )
-    summed = raw_ref[...].astype(jnp.float32) + (keep_ref[...] + got_ref[...])
+    summed = raw_ref[...].astype(jnp.float32) + (keep_ref[...] + got_ref[...].astype(jnp.float32))
     target = layer_norm(summed)[0].astype(jnp.bfloat16)
     error = (prediction - target.astype(jnp.float32)) * live_ref[...]
     grad_pred = error.astype(jnp.bfloat16)
@@ -327,7 +327,7 @@
         out_ref[piece, half:, :] = grad_down[rows].astype(jnp.bfloat16)
 
 
-def in_vmem(kernel, out_shape, operands, places=0, scratch=(), mib=44, copied=0):
+def in_vmem(kernel, out_shape, operands, places=0, scratch=(), mib=32, copied=0):
     several = isinstance(out_shape, (list, tuple))
     in_place = pl.BlockSpec(memory_space=pltpu.VMEM)
     return pl.pallas_call(
@@ -394,14 +394,17 @@
         ]
         return jnp.concatenate(pieces, axis=1)
 
-    columns = jnp.stack([chip_columns(which) for which in range(3)])
-
-    raw = after(raw, (arrived, columns))
+    early, *late = (chip_columns(which) for which in range(3))
+    late = jnp.stack(late)
+    early_two = swap(early, 2)
+
+    raw = after(raw, (arrived, early_two))
     raw_f = raw.astype(jnp.float32)
     normed = layer_norm(raw_f)[0].astype(jnp.bfloat16)
     normed_all = lax.all_gather(normed, CLIP_GROUP, axis=0, tiled=True)
-    columns_two = swap(columns, 2)
-    columns_one = swap(columns, 1)
+    late_two = swap(late, 2)
+    early_one, late_one = swap(early, 1), swap(late, 1)
+    early_three = swap(early_two, 1)
 
     from_owner = take(owner_here, batch)[:, None] == jnp.arange(owners, dtype=jnp.int32)
     stream = jnp.sum(jnp.where(from_owner[:, :, None, None], arrived, 0), axis=1)
@@ -409,10 +412,10 @@
     stream = swap_clips(stream)
     normed_pred = layer_norm(stream.astype(jnp.float32))[0].astype(jnp.bfloat16)
     normed_x = swap(normed_pred, 2)
-    out_two = swap(after(out_weight, columns_two), 2)
+    out_two = swap(after(out_weight, late_two), 2)
 
     mine_units = (4 * y + batch).astype(jnp.int32)[None]
-    mixed_norm, rstd, up_mine, down_mine = functools.partial(in_vmem, mib=44)(
+    mixed_norm, rstd, up_mine, down_mine = in_vmem(
         forward_kernel,
         (
             jax.ShapeDtypeStruct((tok_rows, pred_width), jnp.float32),
@@ -431,20 +434,24 @@
     )
     down_mine = down_mine.reshape(units // 8, pred_width)
 
-    columns_two = after(columns_two, (mixed_norm, normed_x))
-    columns_three = swap(columns_two, 1)
+    late_two = after(late_two, (mixed_norm, normed_x))
+    late_three = swap(late_two, 1)
 
     slab = qkv_weight.shape[0]
-    qkv_columns = functools.partial(in_vmem, mib=44)(
+    qkv_columns = in_vmem(
         weight_kernel,
         jax.ShapeDtypeStruct((3 * part, width), jnp.bfloat16),
         (
             place,
             k.astype(jnp.int32)[None],
-            columns,
-            columns_one,
-            columns_two,
-            columns_three,
+            early,
+            late,
+            early_one,
+            late_one,
+            early_two,
+            late_two,
+            early_three,
+            late_three,
         ),
         places=2,
         scratch=(
@@ -461,7 +468,7 @@
     live = jnp.repeat(masked.astype(jnp.float32) / divisor, BLK)[:, None]
 
     normed_all = after(normed_all, (qkv_columns, mixed_norm))
-    attended = functools.partial(in_vmem, mib=44)(
+    attended = in_vmem(
         attend_kernel,
         jax.ShapeDtypeStruct((4, 2, part, tok_rows), jnp.bfloat16),
         (qkv_columns, normed_all),
@@ -472,9 +479,9 @@
     quad_core = swap(quad, 1)
     attended = lax.all_to_all(attended, CHIP_GROUP, split_axis=0, concat_axis=0, tiled=True)
     attended = after(attended, quad_core)
-    keep, give = functools.partial(in_vmem, mib=44)(
+    keep, give = in_vmem(
         partial_kernel,
-        [jax.ShapeDtypeStruct((tok_rows, width), jnp.float32)] * 2,
+        [jax.ShapeDtypeStruct((tok_rows, width), dtype) for dtype in (jnp.float32, jnp.bfloat16)],
         (
             x.astype(jnp.int32)[None],
             k.astype(jnp.int32)[None],
@@ -490,13 +497,13 @@
         ),
     )
     got = swap(give, 1)
-    grad_mixed = functools.partial(in_vmem, mib=44)(
+    grad_mixed = in_vmem(
         loss_kernel,
         jax.ShapeDtypeStruct((tok_rows, pred_width), jnp.bfloat16),
         (raw, keep, got, mixed_norm, rstd, live, pred_proj),
     )
     grad_rows = lax.all_gather(grad_mixed, ROW_GROUP, axis=0, tiled=True)
-    grads = functools.partial(in_vmem, mib=44)(
+    grads = in_vmem(
         grads_kernel,
         jax.ShapeDtypeStruct((4, units // 16, pred_width), jnp.bfloat16),
         (

time: 117 us -> 112 us (0.957)
  waiting for transfers between devices: 21.7 us -> 8.63 us
  blocking collectives: 23.3 us -> 34.2 us
  starting transfers between devices: 21.2 us -> 23.9 us
  other arithmetic: 8.23 us -> 5.82 us
  local copies, waits for them, and re-layouts: 9.49 us -> 7.61 us
  Pallas kernels: 17.9 us -> 16.6 us
    ppermute x7 -> x10, waiting for transfers between devices: 15 us -> 4.61 us  [swap(): lax.ppermute(value, BATCH_GROUP, tuple(((i, i ^ bits) for i in range(owne...]
    ppermute x7 -> x10, starting transfers between devices: 7.09 us -> 16.4 us  [swap(): lax.ppermute(value, BATCH_GROUP, tuple(((i, i ^ bits) for i in range(owne...]
    all_to_all x0 -> x1, blocking collectives: none -> 9.28 us  [head_shard(): lax.all_to_all(compact, BATCH_GROUP, split_axis=0, concat_axis=0, tiled=T...]
    all_to_all x1 -> x0, starting transfers between devices: 6.82 us -> none  [head_shard(): lax.all_to_all(compact, BATCH_GROUP, split_axis=0, concat_axis=0, tiled=T...]
    all_to_all x1 -> x0, waiting for transfers between devices: 3.26 us -> none  [head_shard(): lax.all_to_all(compact, BATCH_GROUP, split_axis=0, concat_axis=0, tiled=T...]
    unnamed x30 -> x34, local copies, waits for them, and re-layouts: 6 us -> 4.07 us
    reduce_sum x1, other arithmetic: 1.85 us -> 0.13 us  [head_shard(): jnp.sum(jnp.where(mine, stream_blocks, 0), axis=1).astype(jnp.bfloat16)]
    all_to_all x1, blocking collectives: 12.7 us -> 14.3 us  [head_shard(): lax.all_to_all(grads, SUM_GROUP, split_axis=0, concat_axis=0, tiled=True)]
  transfers between devices with their start and end apart: 13 -> 15, of which waited for: 6 -> 4; matrix products, arithmetic and copies ran while one was open for 8% -> 7% of each run, Pallas kernels for 9% -> 9%
where the time goes in v3:
time: 112 us; the launch traced here: 111 us
  blocking collectives  34.2 us (31%)
  starting transfers between devices  23.9 us (21%)
  Pallas kernels  16.6 us (15%)
  between operations  14.4 us (13%)
  waiting for transfers between devices  8.63 us (8%)
  local copies, waits for them, and re-layouts  7.61 us (7%)
  other arithmetic  5.82 us (5%)
    pallas_call x6, Pallas kernels, in_vmem(): pl.pallas_call(kernel, out_shape=out_shape, in_specs=[pl.BlockSpec(memory...  16.6 us
    ppermute x10, starting transfers between devices, swap(): lax.ppermute(value, BATCH_GROUP, tuple(((i, i ^ bits) for i in range(owne...  16.4 us
    all_to_all x1, blocking collectives, head_shard(): lax.all_to_all(grads, SUM_GROUP, split_axis=0, concat_axis=0, tiled=True)  14.3 us
    all_gather x1, blocking collectives, head_shard(): grad_rows = lax.all_gather(grad_mixed, ROW_GROUP, axis=0, tiled=True)  10.6 us
    all_to_all x1, blocking collectives, head_shard(): lax.all_to_all(compact, BATCH_GROUP, split_axis=0, concat_axis=0, tiled=T...  9.28 us
    ppermute x10, waiting for transfers between devices, swap(): lax.ppermute(value, BATCH_GROUP, tuple(((i, i ^ bits) for i in range(owne...  4.61 us
    unnamed x34, local copies, waits for them, and re-layouts  4.07 us
    all_to_all x1, waiting for transfers between devices, head_shard(): lax.all_to_all(attended, CHIP_GROUP, split_axis=0, concat_axis=0, tiled=T...  3.97 us
  transfers between devices with their start and end apart: 15, of which 4 were waited for; matrix products, arithmetic and copies ran while one was open for 7% of the time, Pallas kernels for 9%

profile of v3, /device:TPU:0, one launch (start us, length us, event | category | flops | bytes accessed | tf_op | source)
XLA Modules:
  0.0 111.1 jit_solution(7549839747576847681)
XLA Ops:
  7.2 1.8 %collective-permute-start = (bf16[128,1408]{1,0:T(8,128)(2,1)}, bf16[128,1408]{1,0:T(8,128)(2,1)S(1)}, u32[]{:S(2)}, u32[]{:S(2)}) collective-permute-start(bf16[128,1408]{1,0:T(8,128)(2,1)} %bitcast.28), channel_id=1, source_target_pairs={{0,0},{1,16},{16,1},{17,17},{2,2},{3,18},{18,3},{19,19},{4,4},{5,2... | collective-permute-start | bytes 1081352 | tf_op jit(solution)/shard_map/ppermute | solution.py:373
  9.0 2.6 %constant_dynamic-slice_fusion.4 = (bf16[352,176]{1,0:T(8,128)(2,1)S(1)}, bf16[352,176]{1,0:T(8,128)(2,1)S(1)}, bf16[352,176]{1,0:T(8,128)(2,1)S(1)}, bf16[352,1...) fusion(bf16[352,4224]{1,0:T(8,128)(2,1)} %param.10, s32[]{:T(128)S(6)} %select_n.49, ...), kind=kLoop, calls=%fused_computation.27 | loop fusion | bytes 1486872 | tf_op jit(solution)/shard_map/dynamic_slice | solution.py:390
  11.7 3.0 %collective-permute-start.1 = (bf16[352,352]{1,0:T(8,128)(2,1)S(1)}, bf16[352,352]{1,0:T(8,128)(2,1)S(1)}, u32[]{:S(2)}, u32[]{:S(2)}) collective-permute-start(bf16[352,352]{1,0:T(8,128)(2,1)S(1)} %pad_maximum_fusion.2.refs_0_), channel_id=1, source_target_pairs={{0,2},{1,3},{2,0},{3,1},{4,6},{5,7},{6,4},{7,5},{8,10},{9,11},{10,... | collective-permute-start | bytes 743432 | tf_op jit(solution)/shard_map/ppermute | solution.py:376
  14.9 9.3 %all_to_all.15 = bf16[4,64,384]{2,1,0:T(8,128)(2,1)S(1)} all-to-all(bf16[4,64,384]{2,1,0:T(8,128)(2,1)S(1)} %select_reduce_fusion.1), channel_id=1, replica_groups=mesh['zh'=2,'zl'=2,'y'=2,'x'=2,'k'=2] {'x','k'}, dimensions={0} | all-to-all | bytes 393216 | tf_op jit(solution)/shard_map/all_to_all | solution.py:385
  24.6 1.0 fusion.3
  25.7 1.3 %maximum_bitcast_fusion = (bf16[1,352,352]{2,1,0:T(8,128)(2,1)S(1)}, bf16[1,352,352]{2,1,0:T(8,128)(2,1)S(1)}) fusion(bf16[352,176]{1,0:T(8,128)(2,1)S(1)} %get-tuple-element.25, bf16[352,176]{1,0:T(8,128)(2,1)S(1)} %get-tuple-element.24, bf16[352,176]{1,0:T(8,128)(2,1)} %get-tuple-element.28, bf16[352,176]{1,0:T(8,128)(2,1)} %get-tuple-element.29), kind=kLoop, calls=%fused_computation.12 | loop fusion | flops 991232 | bytes 991232 | tf_op jit(solution)/shard_map/stack | solution.py:398
  27.2 0.7 collective-permute-start.6
  28.0 1.9 %collective-permute-start.2 = (bf16[2,352,352]{2,1,0:T(8,128)(2,1)S(1)}, bf16[2,352,352]{2,1,0:T(8,128)(2,1)S(1)}, u32[]{:S(2)}, u32[]{:S(2)}) collective-permute-start(bf16[2,352,352]{2,1,0:T(8,128)(2,1)S(1)} %pad_maximum_fusion.refs_1_), channel_id=1, source_target_pairs={{0,2},{1,3},{2,0},{3,1},{4,6},{5,7},{6,4},{7,5},{8,10},{9,11},{10,... | collective-permute-start | bytes 1486856 | tf_op jit(solution)/shard_map/ppermute | solution.py:376
  30.3 0.3 collective-permute-start.7
  30.6 5.6 %collective-permute-start.4 = (bf16[352,352]{1,0:T(8,128)(2,1)S(1)}, bf16[352,352]{1,0:T(8,128)(2,1)}, u32[]{:S(2)}, u32[]{:S(2)}) collective-permute-start(bf16[352,352]{1,0:T(8,128)(2,1)S(1)} %pad_maximum_fusion.2.refs_0_), channel_id=1, source_target_pairs={{0,1},{1,0},{2,3},{3,2},{4,5},{5,4},{6,7},{7,6},{8,9},{9,8},{10,11... | collective-permute-start | bytes 743432 | tf_op jit(solution)/shard_map/ppermute | solution.py:376
  36.2 1.3 %copy-done.3 = bf16[1536,384]{1,0:T(8,128)(2,1)S(1)} copy-done((bf16[1536,384]{1,0:T(8,128)(2,1)S(1)}, bf16[1536,384]{1,0:T(8,128)(2,1)}, u32[]{:S(2)}) %copy-start.3) | copy-done | bytes 1179672
  37.5 1.7 %shard_map.104 = (f32[128,384]{1,0:T(8,128)S(1)}, f32[128,1]{1,0:T(8,128)S(1)}, bf16[384,192]{1,0:T(8,128)(2,1)S(1)}, bf16[4,48,384]{2,1,0:T(8,128)(2,1)S(1)}) custom-call(s32[1]{0:T(128)} %bitcast.mine_ref, bf16[384,1536]{1,0:T(8,128)(2,1)S(1)} %copy-done.2, bf16[1536,384]{1,0:T(8,128)(2,1)S(1)} %copy-done.3, ...), custom_call_target="tpu_custom_call" | custom-call | flops 1 | bytes 1 | tf_op jit(solution)/shard_map/pallas_call | solution.py:333
  39.2 1.6 %collective-permute-done.2.refs_5_ = bf16[2,352,352]{2,1,0:T(8,128)(2,1)S(1)} collective-permute-done((bf16[2,352,352]{2,1,0:T(8,128)(2,1)S(1)}, bf16[2,352,352]{2,1,0:T(8,128)(2,1)S(1)}, u32[]{:S(2)}, u32[]{:S(2)}) %collective-permute-start.2) | collective-permute-done | bytes 495648 | tf_op jit(solution)/shard_map/ppermute | solution.py:376
  40.9 2.1 %collective-permute-start.3 = (bf16[352,1408]{1,0:T(8,128)(2,1)}, bf16[352,1408]{1,0:T(8,128)(2,1)}, u32[]{:S(2)}, u32[]{:S(2)}) collective-permute-start(bf16[352,1408]{1,0:T(8,128)(2,1)} %own_ref.1), channel_id=1, source_target_pairs={{0,2},{1,3},{2,0},{3,1},{4,6},{5,7},{6,4},{7,5},{8,10},{9,11},{10,... | collective-permute-start | bytes 2973704 | tf_op jit(solution)/shard_map/ppermute | solution.py:376
  43.0 3.2 %collective-permute-start.9 = (bf16[2,352,352]{2,1,0:T(8,128)(2,1)S(1)}, bf16[2,352,352]{2,1,0:T(8,128)(2,1)S(1)}, u32[]{:S(2)}, u32[]{:S(2)}) collective-permute-start(bf16[2,352,352]{2,1,0:T(8,128)(2,1)S(1)} %collective-permute-done.2.refs_5_), channel_id=1, source_target_pairs={{0,1},{1,0},{2,3},{3,2},{4,5},{5,4},{6,7},{7,6},{8,9},{9,8},{10,11... | collective-permute-start | bytes 1486856 | tf_op jit(solution)/shard_map/ppermute | solution.py:376
  46.3 0.7 pad_maximum_fusion.3
  47.0 1.6 %collective-permute-start.10 = (bf16[2,128,384]{2,1,0:T(8,128)(2,1)}, bf16[2,128,384]{2,1,0:T(8,128)(2,1)}, u32[]{:S(2)}, u32[]{:S(2)}) collective-permute-start(bf16[2,128,384]{2,1,0:T(8,128)(2,1)} %pad_maximum_fusion.3), channel_id=1, source_target_pairs={{0,4},{4,0},{1,5},{5,1},{2,6},{6,2},{3,7},{7,3},{8,12},{12,8},{9,1... | collective-permute-start | bytes 589832 | tf_op jit(solution)/shard_map/ppermute | solution.py:478
  48.7 2.4 %shard_map.105.weight_ref = bf16[528,1408]{1,0:T(8,128)(2,1)S(1)} custom-call(s32[1]{0:T(128)} %bitcast.7.place_ref, s32[1]{0:T(128)} %bitcast.4.core_ref, bf16[352,352]{1,0:T(8,128)(2,1)S(1)} %pad_maximum_fusion.2.refs_0_, bf16[2,352,352]{2,1,0:T(8,128)(2,1)S(1)} %pad_maximum_fusion.refs_1_, bf16[352,352]{1,0:T(8,128)(2,1)} %collective-permute-done.4.refs_2_, ...), custom_call_target="tpu_custom_call" | custom-call | flops 1 | bytes 1 | tf_op jit(solution)/shard_map/pallas_call | solution.py:333
  51.1 1.8 %copy-done.1 = bf16[1024,1408]{1,0:T(8,128)(2,1)S(1)} copy-done((bf16[1024,1408]{1,0:T(8,128)(2,1)S(1)}, bf16[1024,1408]{1,0:T(8,128)(2,1)}, u32[]{:S(2)}) %copy-start.1) | copy-done | bytes 2883608
  52.9 6.1 %shard_map.106 = bf16[4,2,176,128]{3,2,1,0:T(8,128)(2,1)} custom-call(bf16[528,1408]{1,0:T(8,128)(2,1)S(1)} %shard_map.105.weight_ref, bf16[1024,1408]{1,0:T(8,128)(2,1)S(1)} %copy-done.1), custom_call_target="tpu_custom_call" | custom-call | flops 1 | bytes 1 | tf_op jit(solution)/shard_map/pallas_call | solution.py:333
  59.0 3.5 %all-to-all-start.1 = ((bf16[4,2,176,128]{3,2,1,0:T(8,128)(2,1)}), bf16[4,2,176,128]{3,2,1,0:T(8,128)(2,1)S(1)}, u32[]{:S(2)}, u32[]{:S(2)}) async-start(bf16[4,2,176,128]{3,2,1,0:T(8,128)(2,1)} %shard_map.106), calls=%async_computation.1 | async-start | bytes 720896 | tf_op jit(solution)/shard_map/all_to_all | solution.py:480
  62.5 1.1 pad_maximum_fusion.1.quad_ref
  63.9 1.5 %collective-permute-done.11.quad_core_ref = bf16[4,128,384]{2,1,0:T(8,128)(2,1)S(1)} collective-permute-done((bf16[4,128,384]{2,1,0:T(8,128)(2,1)S(1)}, bf16[4,128,384]{2,1,0:T(8,128)(2,1)S(1)}, u32[]{:S(2)}, u32[]{:S(2)}) %collective-permute-start.11) | collective-permute-done | bytes 393248 | tf_op jit(solution)/shard_map/ppermute | solution.py:376
  65.4 4.0 %all-to-all-done.1.att_ref = bf16[4,2,176,128]{3,2,1,0:T(8,128)(2,1)S(1)} async-done(((bf16[4,2,176,128]{3,2,1,0:T(8,128)(2,1)}), bf16[4,2,176,128]{3,2,1,0:T(8,128)(2,1)S(1)}, u32[]{:S(2)}, u32[]{:S(2)}) %all-to-all-start.1) | async-done | bytes 360480 | tf_op jit(solution)/shard_map/all_to_all | solution.py:480
  69.4 3.3 %shard_map.107 = (f32[128,1408]{1,0:T(8,128)S(1)}, bf16[128,1408]{1,0:T(8,128)(2,1)}) custom-call(s32[1]{0:T(128)} %bitcast.3.x_ref, s32[1]{0:T(128)} %bitcast.4.core_ref, bf16[352,1408]{1,0:T(8,128)(2,1)} %own_ref.1, bf16[352,1408]{1,0:T(8,128)(2,1)} %collective-permute-done.3.two_ref, bf16[4,2,176,128]{3,2,1,0:T(8,128)(2,1)S(1)} %all-to-all-done.1.att_ref), custom_call_target="tpu_custom_call" | custom-call | flops 1 | bytes 1 | tf_op jit(solution)/shard_map/pallas_call | solution.py:333
  73.2 1.4 %collective-permute-done.12.got_ref = bf16[128,1408]{1,0:T(8,128)(2,1)S(1)} collective-permute-done((bf16[128,1408]{1,0:T(8,128)(2,1)}, bf16[128,1408]{1,0:T(8,128)(2,1)S(1)}, u32[]{:S(2)}, u32[]{:S(2)}) %collective-permute-start.12) | collective-permute-done | bytes 360480 | tf_op jit(solution)/shard_map/ppermute | solution.py:376
  74.6 0.9 copy-done.8
  75.5 0.9 shard_map.108
  76.4 10.6 %all_gather.7 = bf16[1024,384]{1,0:T(8,128)(2,1)S(1)} all-gather(bf16[128,384]{1,0:T(8,128)(2,1)S(1)} %shard_map.108), channel_id=1, replica_groups=mesh['zh'=2,'zl'=2,'y'=2,'x'=2,'k'=2] {'y','x','k'}, dimensions={0}, use_global_device_ids=true | all-gather | bytes 884736 | tf_op jit(solution)/shard_map/all_gather | solution.py:505
  87.0 2.2 %shard_map.109 = bf16[4,96,384]{2,1,0:T(8,128)(2,1)S(1)} custom-call(s32[1]{0:T(128)} %bitcast.mine_ref, bf16[8,128,384]{2,1,0:T(8,128)(2,1)S(1)} %bitcast.22, bf16[4,128,384]{2,1,0:T(8,128)(2,1)S(1)} %pad_maximum_fusion.1.quad_ref, bf16[4,128,384]{2,1,0:T(8,128)(2,1)S(1)} %collective-permute-done.11.quad_core_ref, bf16[384,192]{1,0:T(8,128)(2,1)S(1)} %copy-done.6, ...), custom_call_target="tpu_custom_call" | custom-call | flops 1 | bytes 1 | tf_op jit(solution)/shard_map/pallas_call | solution.py:333
  89.2 14.3 %all_to_all.16 = bf16[4,96,384]{2,1,0:T(8,128)(2,1)S(1)} all-to-all(bf16[4,96,384]{2,1,0:T(8,128)(2,1)S(1)} %shard_map.109), channel_id=1, replica_groups=mesh['zh'=2,'zl'=2,'y'=2,'x'=2,'k'=2] {'zh','zl'}, dimensions={0} | all-to-all | bytes 589824 | tf_op jit(solution)/shard_map/all_to_all | solution.py:520
  103.6 0.7 fusion.9
  (72 shorter events, 2.7 us)
Async XLA Ops:
  7.2 65.6 %copy-start = (s32[4,14]{1,0:T(4,128)S(1)}, s32[4,14]{1,0:T(4,128)}, u32[]{:S(2)}) copy-start(s32[4,14]{1,0:T(4,128)} %param.12) | copy-start | bytes 676
  7.2 7.5 %copy-start.16 = (s32[4,16]{1,0:T(4,128)S(1)}, s32[4,16]{1,0:T(4,128)}, u32[]{:S(2)}) copy-start(s32[4,16]{1,0:T(4,128)} %param.13) | copy-start | bytes 772
  7.2 7.6 %copy-start.15 = (bf16[1,4,128,384]{3,2,1,0:T(8,128)(2,1)S(1)}, bf16[1,4,128,384]{3,2,1,0:T(8,128)(2,1)}, u32[]{:S(2)}) copy-start(bf16[1,4,128,384]{3,2,1,0:T(8,128)(2,1)} %param.14) | copy-start | bytes 1179652
  7.2 43.9 %all-gather.2.cloned.1.call-start = ((), (), s32[]{:S(2)}) async-start(), calls=%async_computation.3 | async-start | bytes 3244032 | tf_op jit(solution)/shard_map/all_gather | solution.py:404
  7.2 17.0 %collective-permute-start = (bf16[128,1408]{1,0:T(8,128)(2,1)}, bf16[128,1408]{1,0:T(8,128)(2,1)S(1)}, u32[]{:S(2)}, u32[]{:S(2)}) collective-permute-start(bf16[128,1408]{1,0:T(8,128)(2,1)} %bitcast.28), channel_id=1, source_target_pairs={{0,0},{1,16},{16,1},{17,17},{2,2},{3,18},{18,3},{19,19},{4,4},{5,2... | collective-permute-start | bytes 1081352 | tf_op jit(solution)/shard_map/ppermute | solution.py:373
  11.7 12.5 %collective-permute-start.1 = (bf16[352,352]{1,0:T(8,128)(2,1)S(1)}, bf16[352,352]{1,0:T(8,128)(2,1)S(1)}, u32[]{:S(2)}, u32[]{:S(2)}) collective-permute-start(bf16[352,352]{1,0:T(8,128)(2,1)S(1)} %pad_maximum_fusion.2.refs_0_), channel_id=1, source_target_pairs={{0,2},{1,3},{2,0},{3,1},{4,6},{5,7},{6,4},{7,5},{8,10},{9,11},{10,... | collective-permute-start | bytes 743432 | tf_op jit(solution)/shard_map/ppermute | solution.py:376
  25.7 10.5 %copy-start.2 = (bf16[384,1536]{1,0:T(8,128)(2,1)S(1)}, bf16[384,1536]{1,0:T(8,128)(2,1)}, u32[]{:S(2)}) copy-start(bf16[384,1536]{1,0:T(8,128)(2,1)} %up_hbm.1) | copy-start | bytes 3538948
  27.2 2.6 %collective-permute-start.6 = (bf16[128,384]{1,0:T(8,128)(2,1)S(1)}, bf16[128,384]{1,0:T(8,128)(2,1)S(1)}, u32[]{:S(2)}, u32[]{:S(2)}) collective-permute-start(bf16[128,384]{1,0:T(8,128)(2,1)S(1)} %bitcast.27), channel_id=1, source_target_pairs={{0,0},{1,16},{16,1},{17,17},{2,2},{3,18},{18,3},{19,19},{4,4},{5,2... | collective-permute-start | bytes 294920 | tf_op jit(solution)/shard_map/ppermute | solution.py:373
  28.0 12.8 %collective-permute-start.2 = (bf16[2,352,352]{2,1,0:T(8,128)(2,1)S(1)}, bf16[2,352,352]{2,1,0:T(8,128)(2,1)S(1)}, u32[]{:S(2)}, u32[]{:S(2)}) collective-permute-start(bf16[2,352,352]{2,1,0:T(8,128)(2,1)S(1)} %pad_maximum_fusion.refs_1_), channel_id=1, source_target_pairs={{0,2},{1,3},{2,0},{3,1},{4,6},{5,7},{6,4},{7,5},{8,10},{9,11},{10,... | collective-permute-start | bytes 1486856 | tf_op jit(solution)/shard_map/ppermute | solution.py:376
  30.3 12.6 %collective-permute-start.7 = (bf16[128,384]{1,0:T(8,128)(2,1)S(1)}, bf16[128,384]{1,0:T(8,128)(2,1)S(1)}, u32[]{:S(2)}, u32[]{:S(2)}) collective-permute-start(bf16[128,384]{1,0:T(8,128)(2,1)S(1)} %fusion.7.normed_ref), channel_id=1, source_target_pairs={{0,2},{1,3},{2,0},{3,1},{4,6},{5,7},{6,4},{7,5},{8,10},{9,11},{10,... | collective-permute-start | bytes 294920 | tf_op jit(solution)/shard_map/ppermute | solution.py:376
  30.6 16.4 %collective-permute-start.4 = (bf16[352,352]{1,0:T(8,128)(2,1)S(1)}, bf16[352,352]{1,0:T(8,128)(2,1)}, u32[]{:S(2)}, u32[]{:S(2)}) collective-permute-start(bf16[352,352]{1,0:T(8,128)(2,1)S(1)} %pad_maximum_fusion.2.refs_0_), channel_id=1, source_target_pairs={{0,1},{1,0},{2,3},{3,2},{4,5},{5,4},{6,7},{7,6},{8,9},{9,8},{10,11... | collective-permute-start | bytes 743432 | tf_op jit(solution)/shard_map/ppermute | solution.py:376
  36.2 12.4 %collective-permute-start.5 = (bf16[2,352,352]{2,1,0:T(8,128)(2,1)S(1)}, bf16[2,352,352]{2,1,0:T(8,128)(2,1)}, u32[]{:S(2)}, u32[]{:S(2)}) collective-permute-start(bf16[2,352,352]{2,1,0:T(8,128)(2,1)S(1)} %pad_maximum_fusion.refs_1_), channel_id=1, source_target_pairs={{0,1},{1,0},{2,3},{3,2},{4,5},{5,4},{6,7},{7,6},{8,9},{9,8},{10,11... | collective-permute-start | bytes 1486856 | tf_op jit(solution)/shard_map/ppermute | solution.py:376
  36.2 1.3 %copy-start.3 = (bf16[1536,384]{1,0:T(8,128)(2,1)S(1)}, bf16[1536,384]{1,0:T(8,128)(2,1)}, u32[]{:S(2)}) copy-start(bf16[1536,384]{1,0:T(8,128)(2,1)} %down_hbm.1) | copy-start | bytes 3538948
  39.2 9.4 %copy-start.5 = (bf16[384,192]{1,0:T(8,128)(2,1)}, bf16[384,192]{1,0:T(8,128)(2,1)S(1)}, u32[]{:S(2)}) copy-start(bf16[384,192]{1,0:T(8,128)(2,1)S(1)} %get-tuple-element.22.up_ref) | copy-start | bytes 442372
  39.2 9.4 %copy-start.9 = (bf16[4,48,384]{2,1,0:T(8,128)(2,1)}, bf16[4,48,384]{2,1,0:T(8,128)(2,1)S(1)}, u32[]{:S(2)}) copy-start(bf16[4,48,384]{2,1,0:T(8,128)(2,1)S(1)} %get-tuple-element.23) | copy-start | bytes 442372
  39.2 9.5 %copy-start.7 = (f32[128,384]{1,0:T(8,128)}, f32[128,384]{1,0:T(8,128)S(1)}, u32[]{:S(2)}) copy-start(f32[128,384]{1,0:T(8,128)S(1)} %get-tuple-element.15.mixed_norm_ref) | copy-start | bytes 589828
  40.9 28.5 %collective-permute-start.3 = (bf16[352,1408]{1,0:T(8,128)(2,1)}, bf16[352,1408]{1,0:T(8,128)(2,1)}, u32[]{:S(2)}, u32[]{:S(2)}) collective-permute-start(bf16[352,1408]{1,0:T(8,128)(2,1)} %own_ref.1), channel_id=1, source_target_pairs={{0,2},{1,3},{2,0},{3,1},{4,6},{5,7},{6,4},{7,5},{8,10},{9,11},{10,... | collective-permute-start | bytes 2973704 | tf_op jit(solution)/shard_map/ppermute | solution.py:376
  43.0 5.7 %copy-start.13 = (bf16[128,384]{1,0:T(8,128)(2,1)}, bf16[128,384]{1,0:T(8,128)(2,1)S(1)}, u32[]{:S(2)}) copy-start(bf16[128,384]{1,0:T(8,128)(2,1)S(1)} %collective-permute-done.7) | copy-start | bytes 294916
  43.0 5.7 %collective-permute-start.9 = (bf16[2,352,352]{2,1,0:T(8,128)(2,1)S(1)}, bf16[2,352,352]{2,1,0:T(8,128)(2,1)S(1)}, u32[]{:S(2)}, u32[]{:S(2)}) collective-permute-start(bf16[2,352,352]{2,1,0:T(8,128)(2,1)S(1)} %collective-permute-done.2.refs_5_), channel_id=1, source_target_pairs={{0,1},{1,0},{2,3},{3,2},{4,5},{5,4},{6,7},{7,6},{8,9},{9,8},{10,11... | collective-permute-start | bytes 1486856 | tf_op jit(solution)/shard_map/ppermute | solution.py:376
  46.3 2.4 %copy-start.11 = (bf16[1,128,384]{2,1,0:T(8,128)(2,1)}, bf16[1,128,384]{2,1,0:T(8,128)(2,1)S(1)}, u32[]{:S(2)}) copy-start(bf16[1,128,384]{2,1,0:T(8,128)(2,1)S(1)} %fusion.10) | copy-start | bytes 294916
  46.3 2.4 %collective-permute-start.8 = (bf16[352,352]{1,0:T(8,128)(2,1)S(1)}, bf16[352,352]{1,0:T(8,128)(2,1)S(1)}, u32[]{:S(2)}, u32[]{:S(2)}) collective-permute-start(bf16[352,352]{1,0:T(8,128)(2,1)S(1)} %collective-permute-done.1.refs_4_), channel_id=1, source_target_pairs={{0,1},{1,0},{2,3},{3,2},{4,5},{5,4},{6,7},{7,6},{8,9},{9,8},{10,11... | collective-permute-start | bytes 743432 | tf_op jit(solution)/shard_map/ppermute | solution.py:376
  47.0 15.5 %collective-permute-start.10 = (bf16[2,128,384]{2,1,0:T(8,128)(2,1)}, bf16[2,128,384]{2,1,0:T(8,128)(2,1)}, u32[]{:S(2)}, u32[]{:S(2)}) collective-permute-start(bf16[2,128,384]{2,1,0:T(8,128)(2,1)} %pad_maximum_fusion.3), channel_id=1, source_target_pairs={{0,4},{4,0},{1,5},{5,1},{2,6},{6,2},{3,7},{7,3},{8,12},{12,8},{9,1... | collective-permute-start | bytes 589832 | tf_op jit(solution)/shard_map/ppermute | solution.py:478
  51.1 1.8 %copy-start.1 = (bf16[1024,1408]{1,0:T(8,128)(2,1)S(1)}, bf16[1024,1408]{1,0:T(8,128)(2,1)}, u32[]{:S(2)}) copy-start(bf16[1024,1408]{1,0:T(8,128)(2,1)} %all-gather.2.cloned.1.call-done.normed_ref) | copy-start | bytes 8650756
  52.9 9.6 %copy-start.12 = (bf16[1,128,384]{2,1,0:T(8,128)(2,1)S(1)}, bf16[1,128,384]{2,1,0:T(8,128)(2,1)}, u32[]{:S(2)}) copy-start(bf16[1,128,384]{2,1,0:T(8,128)(2,1)} %copy-done.11) | copy-start | bytes 294916
  52.9 9.6 %copy-start.14 = (bf16[128,384]{1,0:T(8,128)(2,1)S(1)}, bf16[128,384]{1,0:T(8,128)(2,1)}, u32[]{:S(2)}) copy-start(bf16[128,384]{1,0:T(8,128)(2,1)} %copy-done.13) | copy-start | bytes 294916
  59.0 10.3 %all-to-all-start.1 = ((bf16[4,2,176,128]{3,2,1,0:T(8,128)(2,1)}), bf16[4,2,176,128]{3,2,1,0:T(8,128)(2,1)S(1)}, u32[]{:S(2)}, u32[]{:S(2)}) async-start(bf16[4,2,176,128]{3,2,1,0:T(8,128)(2,1)} %shard_map.106), calls=%async_computation.1 | async-start | bytes 720896 | tf_op jit(solution)/shard_map/all_to_all | solution.py:480
  62.5 12.1 %copy-start.4 = (bf16[384,1408]{1,0:T(8,128)(2,1)S(1)}, bf16[384,1408]{1,0:T(8,128)(2,1)}, u32[]{:S(2)}) copy-start(bf16[384,1408]{1,0:T(8,128)(2,1)} %proj_ref.1) | copy-start | bytes 3244036
  63.6 1.8 %collective-permute-start.11 = (bf16[4,128,384]{2,1,0:T(8,128)(2,1)S(1)}, bf16[4,128,384]{2,1,0:T(8,128)(2,1)S(1)}, u32[]{:S(2)}, u32[]{:S(2)}) collective-permute-start(bf16[4,128,384]{2,1,0:T(8,128)(2,1)S(1)} %pad_maximum_fusion.1.quad_ref), channel_id=1, source_target_pairs={{0,1},{1,0},{2,3},{3,2},{4,5},{5,4},{6,7},{7,6},{8,9},{9,8},{10,11... | collective-permute-start | bytes 1179656 | tf_op jit(solution)/shard_map/ppermute | solution.py:376
  72.7 2.0 %collective-permute-start.12 = (bf16[128,1408]{1,0:T(8,128)(2,1)}, bf16[128,1408]{1,0:T(8,128)(2,1)S(1)}, u32[]{:S(2)}, u32[]{:S(2)}) collective-permute-start(bf16[128,1408]{1,0:T(8,128)(2,1)} %get-tuple-element.20), channel_id=1, source_target_pairs={{0,1},{1,0},{2,3},{3,2},{4,5},{5,4},{6,7},{7,6},{8,9},{9,8},{10,11... | collective-permute-start | bytes 1081352 | tf_op jit(solution)/shard_map/ppermute | solution.py:376
  74.6 0.9 copy-start.8
  75.5 11.5 %copy-start.6 = (bf16[384,192]{1,0:T(8,128)(2,1)S(1)}, bf16[384,192]{1,0:T(8,128)(2,1)}, u32[]{:S(2)}) copy-start(bf16[384,192]{1,0:T(8,128)(2,1)} %copy-done.5) | copy-start | bytes 442372
  75.5 11.5 %copy-start.10 = (bf16[4,48,384]{2,1,0:T(8,128)(2,1)S(1)}, bf16[4,48,384]{2,1,0:T(8,128)(2,1)}, u32[]{:S(2)}) copy-start(bf16[4,48,384]{2,1,0:T(8,128)(2,1)} %copy-done.9) | copy-start | bytes 442372
Sparse Core Ops, SparseCore 0:
  25.8 24.4 all-gather.1

commit v4 on v3

--- a/solution.py
+++ b/solution.py
@@ -412,7 +412,7 @@
     stream = swap_clips(stream)
     normed_pred = layer_norm(stream.astype(jnp.float32))[0].astype(jnp.bfloat16)
     normed_x = swap(normed_pred, 2)
-    out_two = swap(after(out_weight, late_two), 2)
+    out_two = swap(after(out_weight, (late_two, normed_x)), 2)
 
     mine_units = (4 * y + batch).astype(jnp.int32)[None]
     mixed_norm, rstd, up_mine, down_mine = in_vmem(

time: 112 us -> 111 us (level)
  waiting for transfers between devices: 8.63 us -> 10.7 us
  blocking collectives: 34.2 us -> 32.6 us
    ppermute x10, waiting for transfers between devices: 4.61 us -> 6.69 us  [swap(): lax.ppermute(value, BATCH_GROUP, tuple(((i, i ^ bits) for i in range(owne...]
    all_to_all x1, blocking collectives: 14.3 us -> 12.7 us  [head_shard(): lax.all_to_all(grads, SUM_GROUP, split_axis=0, concat_axis=0, tiled=True)]
    ppermute x10, starting transfers between devices: 16.4 us -> 15.3 us  [swap(): lax.ppermute(value, BATCH_GROUP, tuple(((i, i ^ bits) for i in range(owne...]
where the time goes in v4:
time: 111 us; the launch traced here: 110 us
  blocking collectives  32.6 us (29%)
  starting transfers between devices  22.8 us (21%)
  Pallas kernels  16.5 us (15%)
  between operations  14.3 us (13%)
  waiting for transfers between devices  10.7 us (10%)
  local copies, waits for them, and re-layouts  7.6 us (7%)
  other arithmetic  5.83 us (5%)
    pallas_call x6, Pallas kernels, in_vmem(): pl.pallas_call(kernel, out_shape=out_shape, in_specs=[pl.BlockSpec(memory...  16.5 us
    ppermute x10, starting transfers between devices, swap(): lax.ppermute(value, BATCH_GROUP, tuple(((i, i ^ bits) for i in range(owne...  15.3 us
    all_to_all x1, blocking collectives, head_shard(): lax.all_to_all(grads, SUM_GROUP, split_axis=0, concat_axis=0, tiled=True)  12.7 us
    all_gather x1, blocking collectives, head_shard(): grad_rows = lax.all_gather(grad_mixed, ROW_GROUP, axis=0, tiled=True)  10.5 us
    all_to_all x1, blocking collectives, head_shard(): lax.all_to_all(compact, BATCH_GROUP, split_axis=0, concat_axis=0, tiled=T...  9.28 us
    ppermute x10, waiting for transfers between devices, swap(): lax.ppermute(value, BATCH_GROUP, tuple(((i, i ^ bits) for i in range(owne...  6.69 us
    unnamed x34, local copies, waits for them, and re-layouts  4.07 us
    all_to_all x1, waiting for transfers between devices, head_shard(): lax.all_to_all(attended, CHIP_GROUP, split_axis=0, concat_axis=0, tiled=T...  3.98 us
  transfers between devices with their start and end apart: 15, of which 4 were waited for; matrix products, arithmetic and copies ran while one was open for 7% of the time, Pallas kernels for 9%

profile of v4, /device:TPU:0, one launch (start us, length us, event | category | flops | bytes accessed | tf_op | source)
XLA Modules:
  0.0 110.3 jit_solution(3927569028604407331)
XLA Ops:
  7.2 1.8 %collective-permute-start = (bf16[128,1408]{1,0:T(8,128)(2,1)}, bf16[128,1408]{1,0:T(8,128)(2,1)S(1)}, u32[]{:S(2)}, u32[]{:S(2)}) collective-permute-start(bf16[128,1408]{1,0:T(8,128)(2,1)} %bitcast.28), channel_id=1, source_target_pairs={{0,0},{1,16},{16,1},{17,17},{2,2},{3,18},{18,3},{19,19},{4,4},{5,2... | collective-permute-start | bytes 1081352 | tf_op jit(solution)/shard_map/ppermute | solution.py:373
  9.0 2.6 %constant_dynamic-slice_fusion.4 = (bf16[352,176]{1,0:T(8,128)(2,1)S(1)}, bf16[352,176]{1,0:T(8,128)(2,1)S(1)}, bf16[352,176]{1,0:T(8,128)(2,1)S(1)}, bf16[352,1...) fusion(bf16[352,4224]{1,0:T(8,128)(2,1)} %param.10, s32[]{:T(128)S(6)} %select_n.49, ...), kind=kLoop, calls=%fused_computation.27 | loop fusion | bytes 1486872 | tf_op jit(solution)/shard_map/dynamic_slice | solution.py:390
  11.7 3.0 %collective-permute-start.1 = (bf16[352,352]{1,0:T(8,128)(2,1)S(1)}, bf16[352,352]{1,0:T(8,128)(2,1)S(1)}, u32[]{:S(2)}, u32[]{:S(2)}) collective-permute-start(bf16[352,352]{1,0:T(8,128)(2,1)S(1)} %pad_maximum_fusion.2.refs_0_), channel_id=1, source_target_pairs={{0,2},{1,3},{2,0},{3,1},{4,6},{5,7},{6,4},{7,5},{8,10},{9,11},{10,... | collective-permute-start | bytes 743432 | tf_op jit(solution)/shard_map/ppermute | solution.py:376
  14.9 9.3 %all_to_all.15 = bf16[4,64,384]{2,1,0:T(8,128)(2,1)S(1)} all-to-all(bf16[4,64,384]{2,1,0:T(8,128)(2,1)S(1)} %select_reduce_fusion.1), channel_id=1, replica_groups=mesh['zh'=2,'zl'=2,'y'=2,'x'=2,'k'=2] {'x','k'}, dimensions={0} | all-to-all | bytes 393216 | tf_op jit(solution)/shard_map/all_to_all | solution.py:385
  24.6 1.0 fusion.3
  25.7 1.3 %maximum_bitcast_fusion = (bf16[1,352,352]{2,1,0:T(8,128)(2,1)S(1)}, bf16[1,352,352]{2,1,0:T(8,128)(2,1)S(1)}) fusion(bf16[352,176]{1,0:T(8,128)(2,1)S(1)} %get-tuple-element.25, bf16[352,176]{1,0:T(8,128)(2,1)S(1)} %get-tuple-element.24, bf16[352,176]{1,0:T(8,128)(2,1)} %get-tuple-element.28, bf16[352,176]{1,0:T(8,128)(2,1)} %get-tuple-element.29), kind=kLoop, calls=%fused_computation.12 | loop fusion | flops 991232 | bytes 991232 | tf_op jit(solution)/shard_map/stack | solution.py:398
  27.2 0.7 collective-permute-start.3
  28.0 1.9 %collective-permute-start.2 = (bf16[2,352,352]{2,1,0:T(8,128)(2,1)S(1)}, bf16[2,352,352]{2,1,0:T(8,128)(2,1)S(1)}, u32[]{:S(2)}, u32[]{:S(2)}) collective-permute-start(bf16[2,352,352]{2,1,0:T(8,128)(2,1)S(1)} %pad_maximum_fusion.refs_1_), channel_id=1, source_target_pairs={{0,2},{1,3},{2,0},{3,1},{4,6},{5,7},{6,4},{7,5},{8,10},{9,11},{10,... | collective-permute-start | bytes 1486856 | tf_op jit(solution)/shard_map/ppermute | solution.py:376
  30.3 0.3 collective-permute-start.4
  30.6 5.6 %collective-permute-start.6 = (bf16[352,352]{1,0:T(8,128)(2,1)S(1)}, bf16[352,352]{1,0:T(8,128)(2,1)}, u32[]{:S(2)}, u32[]{:S(2)}) collective-permute-start(bf16[352,352]{1,0:T(8,128)(2,1)S(1)} %pad_maximum_fusion.2.refs_0_), channel_id=1, source_target_pairs={{0,1},{1,0},{2,3},{3,2},{4,5},{5,4},{6,7},{7,6},{8,9},{9,8},{10,11... | collective-permute-start | bytes 743432 | tf_op jit(solution)/shard_map/ppermute | solution.py:376
  36.2 1.3 %copy-done.3 = bf16[1536,384]{1,0:T(8,128)(2,1)S(1)} copy-done((bf16[1536,384]{1,0:T(8,128)(2,1)S(1)}, bf16[1536,384]{1,0:T(8,128)(2,1)}, u32[]{:S(2)}) %copy-start.3) | copy-done | bytes 1179672
  37.5 1.7 %shard_map.104 = (f32[128,384]{1,0:T(8,128)S(1)}, f32[128,1]{1,0:T(8,128)S(1)}, bf16[384,192]{1,0:T(8,128)(2,1)S(1)}, bf16[4,48,384]{2,1,0:T(8,128)(2,1)S(1)}) custom-call(s32[1]{0:T(128)} %bitcast.mine_ref, bf16[384,1536]{1,0:T(8,128)(2,1)S(1)} %copy-done.2, bf16[1536,384]{1,0:T(8,128)(2,1)S(1)} %copy-done.3, ...), custom_call_target="tpu_custom_call" | custom-call | flops 1 | bytes 1 | tf_op jit(solution)/shard_map/pallas_call | solution.py:333
  39.2 3.7 %collective-permute-done.4 = bf16[128,384]{1,0:T(8,128)(2,1)S(1)} collective-permute-done((bf16[128,384]{1,0:T(8,128)(2,1)S(1)}, bf16[128,384]{1,0:T(8,128)(2,1)S(1)}, u32[]{:S(2)}, u32[]{:S(2)}) %collective-permute-start.4) | collective-permute-done | bytes 98336 | tf_op jit(solution)/shard_map/ppermute | solution.py:376
  43.0 2.1 %collective-permute-start.5 = (bf16[352,1408]{1,0:T(8,128)(2,1)}, bf16[352,1408]{1,0:T(8,128)(2,1)}, u32[]{:S(2)}, u32[]{:S(2)}) collective-permute-start(bf16[352,1408]{1,0:T(8,128)(2,1)} %own_ref.1), channel_id=1, source_target_pairs={{0,2},{1,3},{2,0},{3,1},{4,6},{5,7},{6,4},{7,5},{8,10},{9,11},{10,... | collective-permute-start | bytes 2973704 | tf_op jit(solution)/shard_map/ppermute | solution.py:376
  45.0 2.0 %collective-permute-start.9 = (bf16[2,352,352]{2,1,0:T(8,128)(2,1)S(1)}, bf16[2,352,352]{2,1,0:T(8,128)(2,1)S(1)}, u32[]{:S(2)}, u32[]{:S(2)}) collective-permute-start(bf16[2,352,352]{2,1,0:T(8,128)(2,1)S(1)} %collective-permute-done.2.refs_5_), channel_id=1, source_target_pairs={{0,1},{1,0},{2,3},{3,2},{4,5},{5,4},{6,7},{7,6},{8,9},{9,8},{10,11... | collective-permute-start | bytes 1486856 | tf_op jit(solution)/shard_map/ppermute | solution.py:376
  47.3 0.7 pad_maximum_fusion.3
  48.0 1.5 %collective-permute-start.10 = (bf16[2,128,384]{2,1,0:T(8,128)(2,1)}, bf16[2,128,384]{2,1,0:T(8,128)(2,1)}, u32[]{:S(2)}, u32[]{:S(2)}) collective-permute-start(bf16[2,128,384]{2,1,0:T(8,128)(2,1)} %pad_maximum_fusion.3), channel_id=1, source_target_pairs={{0,4},{4,0},{1,5},{5,1},{2,6},{6,2},{3,7},{7,3},{8,12},{12,8},{9,1... | collective-permute-start | bytes 589832 | tf_op jit(solution)/shard_map/ppermute | solution.py:478
  49.6 2.4 %shard_map.105.weight_ref = bf16[528,1408]{1,0:T(8,128)(2,1)S(1)} custom-call(s32[1]{0:T(128)} %bitcast.9.place_ref, s32[1]{0:T(128)} %bitcast.4.core_ref, bf16[352,352]{1,0:T(8,128)(2,1)S(1)} %pad_maximum_fusion.2.refs_0_, bf16[2,352,352]{2,1,0:T(8,128)(2,1)S(1)} %pad_maximum_fusion.refs_1_, bf16[352,352]{1,0:T(8,128)(2,1)} %collective-permute-done.6.refs_2_, ...), custom_call_target="tpu_custom_call" | custom-call | flops 1 | bytes 1 | tf_op jit(solution)/shard_map/pallas_call | solution.py:333
  52.0 1.8 %copy-done.1 = bf16[1024,1408]{1,0:T(8,128)(2,1)S(1)} copy-done((bf16[1024,1408]{1,0:T(8,128)(2,1)S(1)}, bf16[1024,1408]{1,0:T(8,128)(2,1)}, u32[]{:S(2)}) %copy-start.1) | copy-done | bytes 2883608
  53.8 6.1 %shard_map.106 = bf16[4,2,176,128]{3,2,1,0:T(8,128)(2,1)} custom-call(bf16[528,1408]{1,0:T(8,128)(2,1)S(1)} %shard_map.105.weight_ref, bf16[1024,1408]{1,0:T(8,128)(2,1)S(1)} %copy-done.1), custom_call_target="tpu_custom_call" | custom-call | flops 1 | bytes 1 | tf_op jit(solution)/shard_map/pallas_call | solution.py:333
  59.9 3.5 %all-to-all-start.1 = ((bf16[4,2,176,128]{3,2,1,0:T(8,128)(2,1)}), bf16[4,2,176,128]{3,2,1,0:T(8,128)(2,1)S(1)}, u32[]{:S(2)}, u32[]{:S(2)}) async-start(bf16[4,2,176,128]{3,2,1,0:T(8,128)(2,1)} %shard_map.106), calls=%async_computation.1 | async-start | bytes 720896 | tf_op jit(solution)/shard_map/all_to_all | solution.py:480
  63.4 1.1 pad_maximum_fusion.1.quad_ref
  64.7 1.5 %collective-permute-done.11.quad_core_ref = bf16[4,128,384]{2,1,0:T(8,128)(2,1)S(1)} collective-permute-done((bf16[4,128,384]{2,1,0:T(8,128)(2,1)S(1)}, bf16[4,128,384]{2,1,0:T(8,128)(2,1)S(1)}, u32[]{:S(2)}, u32[]{:S(2)}) %collective-permute-start.11) | collective-permute-done | bytes 393248 | tf_op jit(solution)/shard_map/ppermute | solution.py:376
  66.3 4.0 %all-to-all-done.1.att_ref = bf16[4,2,176,128]{3,2,1,0:T(8,128)(2,1)S(1)} async-done(((bf16[4,2,176,128]{3,2,1,0:T(8,128)(2,1)}), bf16[4,2,176,128]{3,2,1,0:T(8,128)(2,1)S(1)}, u32[]{:S(2)}, u32[]{:S(2)}) %all-to-all-start.1) | async-done | bytes 360480 | tf_op jit(solution)/shard_map/all_to_all | solution.py:480
  70.2 3.3 %shard_map.107 = (f32[128,1408]{1,0:T(8,128)S(1)}, bf16[128,1408]{1,0:T(8,128)(2,1)}) custom-call(s32[1]{0:T(128)} %bitcast.3.x_ref, s32[1]{0:T(128)} %bitcast.4.core_ref, bf16[352,1408]{1,0:T(8,128)(2,1)} %own_ref.1, bf16[352,1408]{1,0:T(8,128)(2,1)} %collective-permute-done.5.two_ref, bf16[4,2,176,128]{3,2,1,0:T(8,128)(2,1)S(1)} %all-to-all-done.1.att_ref), custom_call_target="tpu_custom_call" | custom-call | flops 1 | bytes 1 | tf_op jit(solution)/shard_map/pallas_call | solution.py:333
  74.0 1.4 %collective-permute-done.12.got_ref = bf16[128,1408]{1,0:T(8,128)(2,1)S(1)} collective-permute-done((bf16[128,1408]{1,0:T(8,128)(2,1)}, bf16[128,1408]{1,0:T(8,128)(2,1)S(1)}, u32[]{:S(2)}, u32[]{:S(2)}) %collective-permute-start.12) | collective-permute-done | bytes 360480 | tf_op jit(solution)/shard_map/ppermute | solution.py:376
  75.5 0.9 copy-done.8
  76.4 0.9 shard_map.108
  77.3 10.5 %all_gather.7 = bf16[1024,384]{1,0:T(8,128)(2,1)S(1)} all-gather(bf16[128,384]{1,0:T(8,128)(2,1)S(1)} %shard_map.108), channel_id=1, replica_groups=mesh['zh'=2,'zl'=2,'y'=2,'x'=2,'k'=2] {'y','x','k'}, dimensions={0}, use_global_device_ids=true | all-gather | bytes 884736 | tf_op jit(solution)/shard_map/all_gather | solution.py:505
  87.8 2.2 %shard_map.109 = bf16[4,96,384]{2,1,0:T(8,128)(2,1)S(1)} custom-call(s32[1]{0:T(128)} %bitcast.mine_ref, bf16[8,128,384]{2,1,0:T(8,128)(2,1)S(1)} %bitcast.22, bf16[4,128,384]{2,1,0:T(8,128)(2,1)S(1)} %pad_maximum_fusion.1.quad_ref, bf16[4,128,384]{2,1,0:T(8,128)(2,1)S(1)} %collective-permute-done.11.quad_core_ref, bf16[384,192]{1,0:T(8,128)(2,1)S(1)} %copy-done.6, ...), custom_call_target="tpu_custom_call" | custom-call | flops 1 | bytes 1 | tf_op jit(solution)/shard_map/pallas_call | solution.py:333
  90.1 12.7 %all_to_all.16 = bf16[4,96,384]{2,1,0:T(8,128)(2,1)S(1)} all-to-all(bf16[4,96,384]{2,1,0:T(8,128)(2,1)S(1)} %shard_map.109), channel_id=1, replica_groups=mesh['zh'=2,'zl'=2,'y'=2,'x'=2,'k'=2] {'zh','zl'}, dimensions={0} | all-to-all | bytes 589824 | tf_op jit(solution)/shard_map/all_to_all | solution.py:520
  102.8 0.7 fusion.9
  (72 shorter events, 2.7 us)
Async XLA Ops:
  7.2 66.4 %copy-start = (s32[4,14]{1,0:T(4,128)S(1)}, s32[4,14]{1,0:T(4,128)}, u32[]{:S(2)}) copy-start(s32[4,14]{1,0:T(4,128)} %param.12) | copy-start | bytes 676
  7.2 7.5 %copy-start.16 = (s32[4,16]{1,0:T(4,128)S(1)}, s32[4,16]{1,0:T(4,128)}, u32[]{:S(2)}) copy-start(s32[4,16]{1,0:T(4,128)} %param.13) | copy-start | bytes 772
  7.2 7.6 %copy-start.15 = (bf16[1,4,128,384]{3,2,1,0:T(8,128)(2,1)S(1)}, bf16[1,4,128,384]{3,2,1,0:T(8,128)(2,1)}, u32[]{:S(2)}) copy-start(bf16[1,4,128,384]{3,2,1,0:T(8,128)(2,1)} %param.14) | copy-start | bytes 1179652
  7.2 44.8 %all-gather.2.cloned.1.call-start = ((), (), s32[]{:S(2)}) async-start(), calls=%async_computation.3 | async-start | bytes 3244032 | tf_op jit(solution)/shard_map/all_gather | solution.py:404
  7.2 17.0 %collective-permute-start = (bf16[128,1408]{1,0:T(8,128)(2,1)}, bf16[128,1408]{1,0:T(8,128)(2,1)S(1)}, u32[]{:S(2)}, u32[]{:S(2)}) collective-permute-start(bf16[128,1408]{1,0:T(8,128)(2,1)} %bitcast.28), channel_id=1, source_target_pairs={{0,0},{1,16},{16,1},{17,17},{2,2},{3,18},{18,3},{19,19},{4,4},{5,2... | collective-permute-start | bytes 1081352 | tf_op jit(solution)/shard_map/ppermute | solution.py:373
  11.7 12.5 %collective-permute-start.1 = (bf16[352,352]{1,0:T(8,128)(2,1)S(1)}, bf16[352,352]{1,0:T(8,128)(2,1)S(1)}, u32[]{:S(2)}, u32[]{:S(2)}) collective-permute-start(bf16[352,352]{1,0:T(8,128)(2,1)S(1)} %pad_maximum_fusion.2.refs_0_), channel_id=1, source_target_pairs={{0,2},{1,3},{2,0},{3,1},{4,6},{5,7},{6,4},{7,5},{8,10},{9,11},{10,... | collective-permute-start | bytes 743432 | tf_op jit(solution)/shard_map/ppermute | solution.py:376
  25.7 10.5 %copy-start.2 = (bf16[384,1536]{1,0:T(8,128)(2,1)S(1)}, bf16[384,1536]{1,0:T(8,128)(2,1)}, u32[]{:S(2)}) copy-start(bf16[384,1536]{1,0:T(8,128)(2,1)} %up_hbm.1) | copy-start | bytes 3538948
  27.2 2.6 %collective-permute-start.3 = (bf16[128,384]{1,0:T(8,128)(2,1)S(1)}, bf16[128,384]{1,0:T(8,128)(2,1)S(1)}, u32[]{:S(2)}, u32[]{:S(2)}) collective-permute-start(bf16[128,384]{1,0:T(8,128)(2,1)S(1)} %bitcast.27), channel_id=1, source_target_pairs={{0,0},{1,16},{16,1},{17,17},{2,2},{3,18},{18,3},{19,19},{4,4},{5,2... | collective-permute-start | bytes 294920 | tf_op jit(solution)/shard_map/ppermute | solution.py:373
  28.0 14.9 %collective-permute-start.2 = (bf16[2,352,352]{2,1,0:T(8,128)(2,1)S(1)}, bf16[2,352,352]{2,1,0:T(8,128)(2,1)S(1)}, u32[]{:S(2)}, u32[]{:S(2)}) collective-permute-start(bf16[2,352,352]{2,1,0:T(8,128)(2,1)S(1)} %pad_maximum_fusion.refs_1_), channel_id=1, source_target_pairs={{0,2},{1,3},{2,0},{3,1},{4,6},{5,7},{6,4},{7,5},{8,10},{9,11},{10,... | collective-permute-start | bytes 1486856 | tf_op jit(solution)/shard_map/ppermute | solution.py:376
  30.3 12.6 %collective-permute-start.4 = (bf16[128,384]{1,0:T(8,128)(2,1)S(1)}, bf16[128,384]{1,0:T(8,128)(2,1)S(1)}, u32[]{:S(2)}, u32[]{:S(2)}) collective-permute-start(bf16[128,384]{1,0:T(8,128)(2,1)S(1)} %fusion.7.normed_ref), channel_id=1, source_target_pairs={{0,2},{1,3},{2,0},{3,1},{4,6},{5,7},{6,4},{7,5},{8,10},{9,11},{10,... | collective-permute-start | bytes 294920 | tf_op jit(solution)/shard_map/ppermute | solution.py:376
  30.6 17.4 %collective-permute-start.6 = (bf16[352,352]{1,0:T(8,128)(2,1)S(1)}, bf16[352,352]{1,0:T(8,128)(2,1)}, u32[]{:S(2)}, u32[]{:S(2)}) collective-permute-start(bf16[352,352]{1,0:T(8,128)(2,1)S(1)} %pad_maximum_fusion.2.refs_0_), channel_id=1, source_target_pairs={{0,1},{1,0},{2,3},{3,2},{4,5},{5,4},{6,7},{7,6},{8,9},{9,8},{10,11... | collective-permute-start | bytes 743432 | tf_op jit(solution)/shard_map/ppermute | solution.py:376
  36.2 13.3 %collective-permute-start.7 = (bf16[2,352,352]{2,1,0:T(8,128)(2,1)S(1)}, bf16[2,352,352]{2,1,0:T(8,128)(2,1)}, u32[]{:S(2)}, u32[]{:S(2)}) collective-permute-start(bf16[2,352,352]{2,1,0:T(8,128)(2,1)S(1)} %pad_maximum_fusion.refs_1_), channel_id=1, source_target_pairs={{0,1},{1,0},{2,3},{3,2},{4,5},{5,4},{6,7},{7,6},{8,9},{9,8},{10,11... | collective-permute-start | bytes 1486856 | tf_op jit(solution)/shard_map/ppermute | solution.py:376
  36.2 1.3 %copy-start.3 = (bf16[1536,384]{1,0:T(8,128)(2,1)S(1)}, bf16[1536,384]{1,0:T(8,128)(2,1)}, u32[]{:S(2)}) copy-start(bf16[1536,384]{1,0:T(8,128)(2,1)} %down_hbm.1) | copy-start | bytes 3538948
  39.2 10.3 %copy-start.5 = (bf16[384,192]{1,0:T(8,128)(2,1)}, bf16[384,192]{1,0:T(8,128)(2,1)S(1)}, u32[]{:S(2)}) copy-start(bf16[384,192]{1,0:T(8,128)(2,1)S(1)} %get-tuple-element.22.up_ref) | copy-start | bytes 442372
  39.2 10.3 %copy-start.9 = (bf16[4,48,384]{2,1,0:T(8,128)(2,1)}, bf16[4,48,384]{2,1,0:T(8,128)(2,1)S(1)}, u32[]{:S(2)}) copy-start(bf16[4,48,384]{2,1,0:T(8,128)(2,1)S(1)} %get-tuple-element.23) | copy-start | bytes 442372
  39.2 10.3 %copy-start.7 = (f32[128,384]{1,0:T(8,128)}, f32[128,384]{1,0:T(8,128)S(1)}, u32[]{:S(2)}) copy-start(f32[128,384]{1,0:T(8,128)S(1)} %get-tuple-element.15.mixed_norm_ref) | copy-start | bytes 589828
  43.0 6.6 %copy-start.13 = (bf16[128,384]{1,0:T(8,128)(2,1)}, bf16[128,384]{1,0:T(8,128)(2,1)S(1)}, u32[]{:S(2)}) copy-start(bf16[128,384]{1,0:T(8,128)(2,1)S(1)} %collective-permute-done.4) | copy-start | bytes 294916
  43.0 27.3 %collective-permute-start.5 = (bf16[352,1408]{1,0:T(8,128)(2,1)}, bf16[352,1408]{1,0:T(8,128)(2,1)}, u32[]{:S(2)}, u32[]{:S(2)}) collective-permute-start(bf16[352,1408]{1,0:T(8,128)(2,1)} %own_ref.1), channel_id=1, source_target_pairs={{0,2},{1,3},{2,0},{3,1},{4,6},{5,7},{6,4},{7,5},{8,10},{9,11},{10,... | collective-permute-start | bytes 2973704 | tf_op jit(solution)/shard_map/ppermute | solution.py:376
  45.0 4.4 %collective-permute-start.9 = (bf16[2,352,352]{2,1,0:T(8,128)(2,1)S(1)}, bf16[2,352,352]{2,1,0:T(8,128)(2,1)S(1)}, u32[]{:S(2)}, u32[]{:S(2)}) collective-permute-start(bf16[2,352,352]{2,1,0:T(8,128)(2,1)S(1)} %collective-permute-done.2.refs_5_), channel_id=1, source_target_pairs={{0,1},{1,0},{2,3},{3,2},{4,5},{5,4},{6,7},{7,6},{8,9},{9,8},{10,11... | collective-permute-start | bytes 1486856 | tf_op jit(solution)/shard_map/ppermute | solution.py:376
  47.2 2.4 %copy-start.11 = (bf16[1,128,384]{2,1,0:T(8,128)(2,1)}, bf16[1,128,384]{2,1,0:T(8,128)(2,1)S(1)}, u32[]{:S(2)}) copy-start(bf16[1,128,384]{2,1,0:T(8,128)(2,1)S(1)} %fusion.10) | copy-start | bytes 294916
  47.2 2.3 %collective-permute-start.8 = (bf16[352,352]{1,0:T(8,128)(2,1)S(1)}, bf16[352,352]{1,0:T(8,128)(2,1)S(1)}, u32[]{:S(2)}, u32[]{:S(2)}) collective-permute-start(bf16[352,352]{1,0:T(8,128)(2,1)S(1)} %collective-permute-done.1.refs_4_), channel_id=1, source_target_pairs={{0,1},{1,0},{2,3},{3,2},{4,5},{5,4},{6,7},{7,6},{8,9},{9,8},{10,11... | collective-permute-start | bytes 743432 | tf_op jit(solution)/shard_map/ppermute | solution.py:376
  48.0 15.4 %collective-permute-start.10 = (bf16[2,128,384]{2,1,0:T(8,128)(2,1)}, bf16[2,128,384]{2,1,0:T(8,128)(2,1)}, u32[]{:S(2)}, u32[]{:S(2)}) collective-permute-start(bf16[2,128,384]{2,1,0:T(8,128)(2,1)} %pad_maximum_fusion.3), channel_id=1, source_target_pairs={{0,4},{4,0},{1,5},{5,1},{2,6},{6,2},{3,7},{7,3},{8,12},{12,8},{9,1... | collective-permute-start | bytes 589832 | tf_op jit(solution)/shard_map/ppermute | solution.py:478
  52.0 1.8 %copy-start.1 = (bf16[1024,1408]{1,0:T(8,128)(2,1)S(1)}, bf16[1024,1408]{1,0:T(8,128)(2,1)}, u32[]{:S(2)}) copy-start(bf16[1024,1408]{1,0:T(8,128)(2,1)} %all-gather.2.cloned.1.call-done.normed_ref) | copy-start | bytes 8650756
  53.8 9.6 %copy-start.12 = (bf16[1,128,384]{2,1,0:T(8,128)(2,1)S(1)}, bf16[1,128,384]{2,1,0:T(8,128)(2,1)}, u32[]{:S(2)}) copy-start(bf16[1,128,384]{2,1,0:T(8,128)(2,1)} %copy-done.11) | copy-start | bytes 294916
  53.8 9.6 %copy-start.14 = (bf16[128,384]{1,0:T(8,128)(2,1)S(1)}, bf16[128,384]{1,0:T(8,128)(2,1)}, u32[]{:S(2)}) copy-start(bf16[128,384]{1,0:T(8,128)(2,1)} %copy-done.13) | copy-start | bytes 294916
  59.9 10.4 %all-to-all-start.1 = ((bf16[4,2,176,128]{3,2,1,0:T(8,128)(2,1)}), bf16[4,2,176,128]{3,2,1,0:T(8,128)(2,1)S(1)}, u32[]{:S(2)}, u32[]{:S(2)}) async-start(bf16[4,2,176,128]{3,2,1,0:T(8,128)(2,1)} %shard_map.106), calls=%async_computation.1 | async-start | bytes 720896 | tf_op jit(solution)/shard_map/all_to_all | solution.py:480
  63.4 12.1 %copy-start.4 = (bf16[384,1408]{1,0:T(8,128)(2,1)S(1)}, bf16[384,1408]{1,0:T(8,128)(2,1)}, u32[]{:S(2)}) copy-start(bf16[384,1408]{1,0:T(8,128)(2,1)} %proj_ref.1) | copy-start | bytes 3244036
  64.5 1.8 %collective-permute-start.11 = (bf16[4,128,384]{2,1,0:T(8,128)(2,1)S(1)}, bf16[4,128,384]{2,1,0:T(8,128)(2,1)S(1)}, u32[]{:S(2)}, u32[]{:S(2)}) collective-permute-start(bf16[4,128,384]{2,1,0:T(8,128)(2,1)S(1)} %pad_maximum_fusion.1.quad_ref), channel_id=1, source_target_pairs={{0,1},{1,0},{2,3},{3,2},{4,5},{5,4},{6,7},{7,6},{8,9},{9,8},{10,11... | collective-permute-start | bytes 1179656 | tf_op jit(solution)/shard_map/ppermute | solution.py:376
  73.5 2.0 %collective-permute-start.12 = (bf16[128,1408]{1,0:T(8,128)(2,1)}, bf16[128,1408]{1,0:T(8,128)(2,1)S(1)}, u32[]{:S(2)}, u32[]{:S(2)}) collective-permute-start(bf16[128,1408]{1,0:T(8,128)(2,1)} %get-tuple-element.20), channel_id=1, source_target_pairs={{0,1},{1,0},{2,3},{3,2},{4,5},{5,4},{6,7},{7,6},{8,9},{9,8},{10,11... | collective-permute-start | bytes 1081352 | tf_op jit(solution)/shard_map/ppermute | solution.py:376
  75.5 0.9 copy-start.8
  76.4 11.4 %copy-start.6 = (bf16[384,192]{1,0:T(8,128)(2,1)S(1)}, bf16[384,192]{1,0:T(8,128)(2,1)}, u32[]{:S(2)}) copy-start(bf16[384,192]{1,0:T(8,128)(2,1)} %copy-done.5) | copy-start | bytes 442372
  76.4 11.4 %copy-start.10 = (bf16[4,48,384]{2,1,0:T(8,128)(2,1)S(1)}, bf16[4,48,384]{2,1,0:T(8,128)(2,1)}, u32[]{:S(2)}) copy-start(bf16[4,48,384]{2,1,0:T(8,128)(2,1)} %copy-done.9) | copy-start | bytes 442372
Sparse Core Ops, SparseCore 0:
  25.8 24.4 all-gather.1

commit v5 on v4

--- a/solution.py
+++ b/solution.py
@@ -216,19 +216,17 @@
 
 
 def partial_kernel(
-    x_ref, core_ref, own_ref, two_ref, att_ref, keep_ref, give_ref, slabs, sems
+    x_ref, core_ref, two_ref, own_ref, att_ref, keep_ref, give_ref
 ):
     x, core = x_ref[0], core_ref[0]
-    copies = start_copies([(own_ref, slabs.at[0]), (two_ref, slabs.at[1])], sems)
     sums = [0.0, 0.0]
-    for step in range(2):
-        copies[step].wait()
+    for step, slab_ref in enumerate((own_ref, two_ref)):
         place = 2 * (x ^ step)
         for side in range(2):
             rows = [att_ref[place + piece, core ^ side] for piece in range(2)]
             sums[side] = sums[side] + lax.dot_general(
                 jnp.concatenate(rows, axis=0),
-                slabs[step],
+                slab_ref[...],
                 (((0,), (0,)), ((), ())),
                 preferred_element_type=jnp.float32,
             )
@@ -485,16 +483,11 @@
         (
             x.astype(jnp.int32)[None],
             k.astype(jnp.int32)[None],
+            out_two,
             out_weight,
-            out_two,
             attended,
         ),
         places=2,
-        copied=2,
-        scratch=(
-            pltpu.VMEM((2, slab, width), jnp.bfloat16),
-            pltpu.SemaphoreType.DMA((2,)),
-        ),
     )
     got = swap(give, 1)
     grad_mixed = in_vmem(

time: 111 us -> 111 us (level)
  no operation moved by 1% of the time
where the time goes in v5:
time: 111 us; the launch traced here: 110 us
  blocking collectives  32.6 us (29%)
  starting transfers between devices  22.7 us (20%)
  Pallas kernels  16.5 us (15%)
  between operations  14.3 us (13%)
  waiting for transfers between devices  10.7 us (10%)
  local copies, waits for them, and re-layouts  7.6 us (7%)
  other arithmetic  5.83 us (5%)
    pallas_call x6, Pallas kernels, in_vmem(): pl.pallas_call(kernel, out_shape=out_shape, in_specs=[pl.BlockSpec(memory...  16.5 us
    ppermute x10, starting transfers between devices, swap(): lax.ppermute(value, BATCH_GROUP, tuple(((i, i ^ bits) for i in range(owne...  15.2 us
    all_to_all x1, blocking collectives, head_shard(): lax.all_to_all(grads, SUM_GROUP, split_axis=0, concat_axis=0, tiled=True)  12.7 us
    all_gather x1, blocking collectives, head_shard(): grad_rows = lax.all_gather(grad_mixed, ROW_GROUP, axis=0, tiled=True)  10.5 us
    all_to_all x1, blocking collectives, head_shard(): lax.all_to_all(compact, BATCH_GROUP, split_axis=0, concat_axis=0, tiled=T...  9.28 us
    ppermute x10, waiting for transfers between devices, swap(): lax.ppermute(value, BATCH_GROUP, tuple(((i, i ^ bits) for i in range(owne...  6.72 us
    unnamed x34, local copies, waits for them, and re-layouts  4.07 us
    all_to_all x1, waiting for transfers between devices, head_shard(): lax.all_to_all(attended, CHIP_GROUP, split_axis=0, concat_axis=0, tiled=T...  3.98 us
  transfers between devices with their start and end apart: 15, of which 4 were waited for; matrix products, arithmetic and copies ran while one was open for 7% of the time, Pallas kernels for 9%

profile of v5, /device:TPU:0, one launch (start us, length us, event | category | flops | bytes accessed | tf_op | source)
XLA Modules:
  0.0 110.3 jit_solution(7673053379049047299)
XLA Ops:
  7.2 1.8 %collective-permute-start = (bf16[128,1408]{1,0:T(8,128)(2,1)}, bf16[128,1408]{1,0:T(8,128)(2,1)S(1)}, u32[]{:S(2)}, u32[]{:S(2)}) collective-permute-start(bf16[128,1408]{1,0:T(8,128)(2,1)} %bitcast.28), channel_id=1, source_target_pairs={{0,0},{1,16},{16,1},{17,17},{2,2},{3,18},{18,3},{19,19},{4,4},{5,2... | collective-permute-start | bytes 1081352 | tf_op jit(solution)/shard_map/ppermute | solution.py:371
  9.0 2.6 %constant_dynamic-slice_fusion.4 = (bf16[352,176]{1,0:T(8,128)(2,1)S(1)}, bf16[352,176]{1,0:T(8,128)(2,1)S(1)}, bf16[352,176]{1,0:T(8,128)(2,1)S(1)}, bf16[352,1...) fusion(bf16[352,4224]{1,0:T(8,128)(2,1)} %param.10, s32[]{:T(128)S(6)} %select_n.49, ...), kind=kLoop, calls=%fused_computation.27 | loop fusion | bytes 1486872 | tf_op jit(solution)/shard_map/dynamic_slice | solution.py:388
  11.7 3.0 %collective-permute-start.1 = (bf16[352,352]{1,0:T(8,128)(2,1)S(1)}, bf16[352,352]{1,0:T(8,128)(2,1)S(1)}, u32[]{:S(2)}, u32[]{:S(2)}) collective-permute-start(bf16[352,352]{1,0:T(8,128)(2,1)S(1)} %pad_maximum_fusion.2.refs_0_), channel_id=1, source_target_pairs={{0,2},{1,3},{2,0},{3,1},{4,6},{5,7},{6,4},{7,5},{8,10},{9,11},{10,... | collective-permute-start | bytes 743432 | tf_op jit(solution)/shard_map/ppermute | solution.py:374
  14.9 9.3 %all_to_all.15 = bf16[4,64,384]{2,1,0:T(8,128)(2,1)S(1)} all-to-all(bf16[4,64,384]{2,1,0:T(8,128)(2,1)S(1)} %select_reduce_fusion.1), channel_id=1, replica_groups=mesh['zh'=2,'zl'=2,'y'=2,'x'=2,'k'=2] {'x','k'}, dimensions={0} | all-to-all | bytes 393216 | tf_op jit(solution)/shard_map/all_to_all | solution.py:383
  24.6 1.0 fusion.3
  25.7 1.3 %maximum_bitcast_fusion = (bf16[1,352,352]{2,1,0:T(8,128)(2,1)S(1)}, bf16[1,352,352]{2,1,0:T(8,128)(2,1)S(1)}) fusion(bf16[352,176]{1,0:T(8,128)(2,1)S(1)} %get-tuple-element.25, bf16[352,176]{1,0:T(8,128)(2,1)S(1)} %get-tuple-element.24, bf16[352,176]{1,0:T(8,128)(2,1)} %get-tuple-element.28, bf16[352,176]{1,0:T(8,128)(2,1)} %get-tuple-element.29), kind=kLoop, calls=%fused_computation.12 | loop fusion | flops 991232 | bytes 991232 | tf_op jit(solution)/shard_map/stack | solution.py:396
  27.2 0.7 collective-permute-start.3
  28.0 1.9 %collective-permute-start.2 = (bf16[2,352,352]{2,1,0:T(8,128)(2,1)S(1)}, bf16[2,352,352]{2,1,0:T(8,128)(2,1)S(1)}, u32[]{:S(2)}, u32[]{:S(2)}) collective-permute-start(bf16[2,352,352]{2,1,0:T(8,128)(2,1)S(1)} %pad_maximum_fusion.refs_1_), channel_id=1, source_target_pairs={{0,2},{1,3},{2,0},{3,1},{4,6},{5,7},{6,4},{7,5},{8,10},{9,11},{10,... | collective-permute-start | bytes 1486856 | tf_op jit(solution)/shard_map/ppermute | solution.py:374
  30.3 0.3 collective-permute-start.4
  30.6 5.6 %collective-permute-start.6 = (bf16[352,352]{1,0:T(8,128)(2,1)S(1)}, bf16[352,352]{1,0:T(8,128)(2,1)}, u32[]{:S(2)}, u32[]{:S(2)}) collective-permute-start(bf16[352,352]{1,0:T(8,128)(2,1)S(1)} %pad_maximum_fusion.2.refs_0_), channel_id=1, source_target_pairs={{0,1},{1,0},{2,3},{3,2},{4,5},{5,4},{6,7},{7,6},{8,9},{9,8},{10,11... | collective-permute-start | bytes 743432 | tf_op jit(solution)/shard_map/ppermute | solution.py:374
  36.2 1.3 %copy-done.3 = bf16[1536,384]{1,0:T(8,128)(2,1)S(1)} copy-done((bf16[1536,384]{1,0:T(8,128)(2,1)S(1)}, bf16[1536,384]{1,0:T(8,128)(2,1)}, u32[]{:S(2)}) %copy-start.3) | copy-done | bytes 1179672
  37.5 1.7 %shard_map.104 = (f32[128,384]{1,0:T(8,128)S(1)}, f32[128,1]{1,0:T(8,128)S(1)}, bf16[384,192]{1,0:T(8,128)(2,1)S(1)}, bf16[4,48,384]{2,1,0:T(8,128)(2,1)S(1)}) custom-call(s32[1]{0:T(128)} %bitcast.mine_ref, bf16[384,1536]{1,0:T(8,128)(2,1)S(1)} %copy-done.2, bf16[1536,384]{1,0:T(8,128)(2,1)S(1)} %copy-done.3, ...), custom_call_target="tpu_custom_call" | custom-call | flops 1 | bytes 1 | tf_op jit(solution)/shard_map/pallas_call | solution.py:331
  39.2 3.7 %collective-permute-done.4 = bf16[128,384]{1,0:T(8,128)(2,1)S(1)} collective-permute-done((bf16[128,384]{1,0:T(8,128)(2,1)S(1)}, bf16[128,384]{1,0:T(8,128)(2,1)S(1)}, u32[]{:S(2)}, u32[]{:S(2)}) %collective-permute-start.4) | collective-permute-done | bytes 98336 | tf_op jit(solution)/shard_map/ppermute | solution.py:374
  43.0 2.1 %collective-permute-start.5 = (bf16[352,1408]{1,0:T(8,128)(2,1)}, bf16[352,1408]{1,0:T(8,128)(2,1)}, u32[]{:S(2)}, u32[]{:S(2)}) collective-permute-start(bf16[352,1408]{1,0:T(8,128)(2,1)} %own_ref.1), channel_id=1, source_target_pairs={{0,2},{1,3},{2,0},{3,1},{4,6},{5,7},{6,4},{7,5},{8,10},{9,11},{10,... | collective-permute-start | bytes 2973704 | tf_op jit(solution)/shard_map/ppermute | solution.py:374
  45.0 2.0 %collective-permute-start.9 = (bf16[2,352,352]{2,1,0:T(8,128)(2,1)S(1)}, bf16[2,352,352]{2,1,0:T(8,128)(2,1)S(1)}, u32[]{:S(2)}, u32[]{:S(2)}) collective-permute-start(bf16[2,352,352]{2,1,0:T(8,128)(2,1)S(1)} %collective-permute-done.2.refs_5_), channel_id=1, source_target_pairs={{0,1},{1,0},{2,3},{3,2},{4,5},{5,4},{6,7},{7,6},{8,9},{9,8},{10,11... | collective-permute-start | bytes 1486856 | tf_op jit(solution)/shard_map/ppermute | solution.py:374
  47.3 0.7 pad_maximum_fusion.3
  48.0 1.5 %collective-permute-start.10 = (bf16[2,128,384]{2,1,0:T(8,128)(2,1)}, bf16[2,128,384]{2,1,0:T(8,128)(2,1)}, u32[]{:S(2)}, u32[]{:S(2)}) collective-permute-start(bf16[2,128,384]{2,1,0:T(8,128)(2,1)} %pad_maximum_fusion.3), channel_id=1, source_target_pairs={{0,4},{4,0},{1,5},{5,1},{2,6},{6,2},{3,7},{7,3},{8,12},{12,8},{9,1... | collective-permute-start | bytes 589832 | tf_op jit(solution)/shard_map/ppermute | solution.py:476
  49.6 2.4 %shard_map.105.weight_ref = bf16[528,1408]{1,0:T(8,128)(2,1)S(1)} custom-call(s32[1]{0:T(128)} %bitcast.9.place_ref, s32[1]{0:T(128)} %bitcast.4.core_ref, bf16[352,352]{1,0:T(8,128)(2,1)S(1)} %pad_maximum_fusion.2.refs_0_, bf16[2,352,352]{2,1,0:T(8,128)(2,1)S(1)} %pad_maximum_fusion.refs_1_, bf16[352,352]{1,0:T(8,128)(2,1)} %collective-permute-done.6.refs_2_, ...), custom_call_target="tpu_custom_call" | custom-call | flops 1 | bytes 1 | tf_op jit(solution)/shard_map/pallas_call | solution.py:331
  52.0 1.8 %copy-done.1 = bf16[1024,1408]{1,0:T(8,128)(2,1)S(1)} copy-done((bf16[1024,1408]{1,0:T(8,128)(2,1)S(1)}, bf16[1024,1408]{1,0:T(8,128)(2,1)}, u32[]{:S(2)}) %copy-start.1) | copy-done | bytes 2883608
  53.8 6.1 %shard_map.106 = bf16[4,2,176,128]{3,2,1,0:T(8,128)(2,1)} custom-call(bf16[528,1408]{1,0:T(8,128)(2,1)S(1)} %shard_map.105.weight_ref, bf16[1024,1408]{1,0:T(8,128)(2,1)S(1)} %copy-done.1), custom_call_target="tpu_custom_call" | custom-call | flops 1 | bytes 1 | tf_op jit(solution)/shard_map/pallas_call | solution.py:331
  59.9 3.5 %all-to-all-start.1 = ((bf16[4,2,176,128]{3,2,1,0:T(8,128)(2,1)}), bf16[4,2,176,128]{3,2,1,0:T(8,128)(2,1)S(1)}, u32[]{:S(2)}, u32[]{:S(2)}) async-start(bf16[4,2,176,128]{3,2,1,0:T(8,128)(2,1)} %shard_map.106), calls=%async_computation.1 | async-start | bytes 720896 | tf_op jit(solution)/shard_map/all_to_all | solution.py:478
  63.4 1.1 pad_maximum_fusion.1.quad_ref
  64.7 1.5 %collective-permute-done.11.quad_core_ref = bf16[4,128,384]{2,1,0:T(8,128)(2,1)S(1)} collective-permute-done((bf16[4,128,384]{2,1,0:T(8,128)(2,1)S(1)}, bf16[4,128,384]{2,1,0:T(8,128)(2,1)S(1)}, u32[]{:S(2)}, u32[]{:S(2)}) %collective-permute-start.11) | collective-permute-done | bytes 393248 | tf_op jit(solution)/shard_map/ppermute | solution.py:374
  66.3 4.0 %all-to-all-done.1.att_ref = bf16[4,2,176,128]{3,2,1,0:T(8,128)(2,1)S(1)} async-done(((bf16[4,2,176,128]{3,2,1,0:T(8,128)(2,1)}), bf16[4,2,176,128]{3,2,1,0:T(8,128)(2,1)S(1)}, u32[]{:S(2)}, u32[]{:S(2)}) %all-to-all-start.1) | async-done | bytes 360480 | tf_op jit(solution)/shard_map/all_to_all | solution.py:478
  70.2 3.3 %shard_map.107 = (f32[128,1408]{1,0:T(8,128)S(1)}, bf16[128,1408]{1,0:T(8,128)(2,1)}) custom-call(s32[1]{0:T(128)} %bitcast.3.x_ref, s32[1]{0:T(128)} %bitcast.4.core_ref, bf16[352,1408]{1,0:T(8,128)(2,1)} %collective-permute-done.5.two_ref, bf16[352,1408]{1,0:T(8,128)(2,1)} %own_ref.1, bf16[4,2,176,128]{3,2,1,0:T(8,128)(2,1)S(1)} %all-to-all-done.1.att_ref), custom_call_target="tpu_custom_call" | custom-call | flops 1 | bytes 1 | tf_op jit(solution)/shard_map/pallas_call | solution.py:331
  73.9 1.5 %collective-permute-done.12.got_ref = bf16[128,1408]{1,0:T(8,128)(2,1)S(1)} collective-permute-done((bf16[128,1408]{1,0:T(8,128)(2,1)}, bf16[128,1408]{1,0:T(8,128)(2,1)S(1)}, u32[]{:S(2)}, u32[]{:S(2)}) %collective-permute-start.12) | collective-permute-done | bytes 360480 | tf_op jit(solution)/shard_map/ppermute | solution.py:374
  75.4 0.9 copy-done.8
  76.3 0.9 shard_map.108
  77.2 10.5 %all_gather.7 = bf16[1024,384]{1,0:T(8,128)(2,1)S(1)} all-gather(bf16[128,384]{1,0:T(8,128)(2,1)S(1)} %shard_map.108), channel_id=1, replica_groups=mesh['zh'=2,'zl'=2,'y'=2,'x'=2,'k'=2] {'y','x','k'}, dimensions={0}, use_global_device_ids=true | all-gather | bytes 884736 | tf_op jit(solution)/shard_map/all_gather | solution.py:498
  87.8 2.2 %shard_map.109 = bf16[4,96,384]{2,1,0:T(8,128)(2,1)S(1)} custom-call(s32[1]{0:T(128)} %bitcast.mine_ref, bf16[8,128,384]{2,1,0:T(8,128)(2,1)S(1)} %bitcast.22, bf16[4,128,384]{2,1,0:T(8,128)(2,1)S(1)} %pad_maximum_fusion.1.quad_ref, bf16[4,128,384]{2,1,0:T(8,128)(2,1)S(1)} %collective-permute-done.11.quad_core_ref, bf16[384,192]{1,0:T(8,128)(2,1)S(1)} %copy-done.6, ...), custom_call_target="tpu_custom_call" | custom-call | flops 1 | bytes 1 | tf_op jit(solution)/shard_map/pallas_call | solution.py:331
  90.0 12.7 %all_to_all.16 = bf16[4,96,384]{2,1,0:T(8,128)(2,1)S(1)} all-to-all(bf16[4,96,384]{2,1,0:T(8,128)(2,1)S(1)} %shard_map.109), channel_id=1, replica_groups=mesh['zh'=2,'zl'=2,'y'=2,'x'=2,'k'=2] {'zh','zl'}, dimensions={0} | all-to-all | bytes 589824 | tf_op jit(solution)/shard_map/all_to_all | solution.py:513
  102.8 0.7 fusion.9
  (72 shorter events, 2.6 us)
Async XLA Ops:
  7.2 66.3 %copy-start = (s32[4,14]{1,0:T(4,128)S(1)}, s32[4,14]{1,0:T(4,128)}, u32[]{:S(2)}) copy-start(s32[4,14]{1,0:T(4,128)} %param.12) | copy-start | bytes 676
  7.2 7.5 %copy-start.16 = (s32[4,16]{1,0:T(4,128)S(1)}, s32[4,16]{1,0:T(4,128)}, u32[]{:S(2)}) copy-start(s32[4,16]{1,0:T(4,128)} %param.13) | copy-start | bytes 772
  7.2 7.6 %copy-start.15 = (bf16[1,4,128,384]{3,2,1,0:T(8,128)(2,1)S(1)}, bf16[1,4,128,384]{3,2,1,0:T(8,128)(2,1)}, u32[]{:S(2)}) copy-start(bf16[1,4,128,384]{3,2,1,0:T(8,128)(2,1)} %param.14) | copy-start | bytes 1179652
  7.2 44.8 %all-gather.2.cloned.1.call-start = ((), (), s32[]{:S(2)}) async-start(), calls=%async_computation.3 | async-start | bytes 3244032 | tf_op jit(solution)/shard_map/all_gather | solution.py:402
  7.2 17.0 %collective-permute-start = (bf16[128,1408]{1,0:T(8,128)(2,1)}, bf16[128,1408]{1,0:T(8,128)(2,1)S(1)}, u32[]{:S(2)}, u32[]{:S(2)}) collective-permute-start(bf16[128,1408]{1,0:T(8,128)(2,1)} %bitcast.28), channel_id=1, source_target_pairs={{0,0},{1,16},{16,1},{17,17},{2,2},{3,18},{18,3},{19,19},{4,4},{5,2... | collective-permute-start | bytes 1081352 | tf_op jit(solution)/shard_map/ppermute | solution.py:371
  11.7 12.5 %collective-permute-start.1 = (bf16[352,352]{1,0:T(8,128)(2,1)S(1)}, bf16[352,352]{1,0:T(8,128)(2,1)S(1)}, u32[]{:S(2)}, u32[]{:S(2)}) collective-permute-start(bf16[352,352]{1,0:T(8,128)(2,1)S(1)} %pad_maximum_fusion.2.refs_0_), channel_id=1, source_target_pairs={{0,2},{1,3},{2,0},{3,1},{4,6},{5,7},{6,4},{7,5},{8,10},{9,11},{10,... | collective-permute-start | bytes 743432 | tf_op jit(solution)/shard_map/ppermute | solution.py:374
  25.7 10.5 %copy-start.2 = (bf16[384,1536]{1,0:T(8,128)(2,1)S(1)}, bf16[384,1536]{1,0:T(8,128)(2,1)}, u32[]{:S(2)}) copy-start(bf16[384,1536]{1,0:T(8,128)(2,1)} %up_hbm.1) | copy-start | bytes 3538948
  27.2 2.6 %collective-permute-start.3 = (bf16[128,384]{1,0:T(8,128)(2,1)S(1)}, bf16[128,384]{1,0:T(8,128)(2,1)S(1)}, u32[]{:S(2)}, u32[]{:S(2)}) collective-permute-start(bf16[128,384]{1,0:T(8,128)(2,1)S(1)} %bitcast.27), channel_id=1, source_target_pairs={{0,0},{1,16},{16,1},{17,17},{2,2},{3,18},{18,3},{19,19},{4,4},{5,2... | collective-permute-start | bytes 294920 | tf_op jit(solution)/shard_map/ppermute | solution.py:371
  28.0 14.9 %collective-permute-start.2 = (bf16[2,352,352]{2,1,0:T(8,128)(2,1)S(1)}, bf16[2,352,352]{2,1,0:T(8,128)(2,1)S(1)}, u32[]{:S(2)}, u32[]{:S(2)}) collective-permute-start(bf16[2,352,352]{2,1,0:T(8,128)(2,1)S(1)} %pad_maximum_fusion.refs_1_), channel_id=1, source_target_pairs={{0,2},{1,3},{2,0},{3,1},{4,6},{5,7},{6,4},{7,5},{8,10},{9,11},{10,... | collective-permute-start | bytes 1486856 | tf_op jit(solution)/shard_map/ppermute | solution.py:374
  30.3 12.6 %collective-permute-start.4 = (bf16[128,384]{1,0:T(8,128)(2,1)S(1)}, bf16[128,384]{1,0:T(8,128)(2,1)S(1)}, u32[]{:S(2)}, u32[]{:S(2)}) collective-permute-start(bf16[128,384]{1,0:T(8,128)(2,1)S(1)} %fusion.7.normed_ref), channel_id=1, source_target_pairs={{0,2},{1,3},{2,0},{3,1},{4,6},{5,7},{6,4},{7,5},{8,10},{9,11},{10,... | collective-permute-start | bytes 294920 | tf_op jit(solution)/shard_map/ppermute | solution.py:374
  30.6 17.4 %collective-permute-start.6 = (bf16[352,352]{1,0:T(8,128)(2,1)S(1)}, bf16[352,352]{1,0:T(8,128)(2,1)}, u32[]{:S(2)}, u32[]{:S(2)}) collective-permute-start(bf16[352,352]{1,0:T(8,128)(2,1)S(1)} %pad_maximum_fusion.2.refs_0_), channel_id=1, source_target_pairs={{0,1},{1,0},{2,3},{3,2},{4,5},{5,4},{6,7},{7,6},{8,9},{9,8},{10,11... | collective-permute-start | bytes 743432 | tf_op jit(solution)/shard_map/ppermute | solution.py:374
  36.2 13.3 %collective-permute-start.7 = (bf16[2,352,352]{2,1,0:T(8,128)(2,1)S(1)}, bf16[2,352,352]{2,1,0:T(8,128)(2,1)}, u32[]{:S(2)}, u32[]{:S(2)}) collective-permute-start(bf16[2,352,352]{2,1,0:T(8,128)(2,1)S(1)} %pad_maximum_fusion.refs_1_), channel_id=1, source_target_pairs={{0,1},{1,0},{2,3},{3,2},{4,5},{5,4},{6,7},{7,6},{8,9},{9,8},{10,11... | collective-permute-start | bytes 1486856 | tf_op jit(solution)/shard_map/ppermute | solution.py:374
  36.2 1.3 %copy-start.3 = (bf16[1536,384]{1,0:T(8,128)(2,1)S(1)}, bf16[1536,384]{1,0:T(8,128)(2,1)}, u32[]{:S(2)}) copy-start(bf16[1536,384]{1,0:T(8,128)(2,1)} %down_hbm.1) | copy-start | bytes 3538948
  39.2 10.3 %copy-start.5 = (bf16[384,192]{1,0:T(8,128)(2,1)}, bf16[384,192]{1,0:T(8,128)(2,1)S(1)}, u32[]{:S(2)}) copy-start(bf16[384,192]{1,0:T(8,128)(2,1)S(1)} %get-tuple-element.22.up_ref) | copy-start | bytes 442372
  39.2 10.3 %copy-start.9 = (bf16[4,48,384]{2,1,0:T(8,128)(2,1)}, bf16[4,48,384]{2,1,0:T(8,128)(2,1)S(1)}, u32[]{:S(2)}) copy-start(bf16[4,48,384]{2,1,0:T(8,128)(2,1)S(1)} %get-tuple-element.23) | copy-start | bytes 442372
  39.2 10.3 %copy-start.7 = (f32[128,384]{1,0:T(8,128)}, f32[128,384]{1,0:T(8,128)S(1)}, u32[]{:S(2)}) copy-start(f32[128,384]{1,0:T(8,128)S(1)} %get-tuple-element.15.mixed_norm_ref) | copy-start | bytes 589828
  43.0 6.6 %copy-start.13 = (bf16[128,384]{1,0:T(8,128)(2,1)}, bf16[128,384]{1,0:T(8,128)(2,1)S(1)}, u32[]{:S(2)}) copy-start(bf16[128,384]{1,0:T(8,128)(2,1)S(1)} %collective-permute-done.4) | copy-start | bytes 294916
  43.0 27.3 %collective-permute-start.5 = (bf16[352,1408]{1,0:T(8,128)(2,1)}, bf16[352,1408]{1,0:T(8,128)(2,1)}, u32[]{:S(2)}, u32[]{:S(2)}) collective-permute-start(bf16[352,1408]{1,0:T(8,128)(2,1)} %own_ref.1), channel_id=1, source_target_pairs={{0,2},{1,3},{2,0},{3,1},{4,6},{5,7},{6,4},{7,5},{8,10},{9,11},{10,... | collective-permute-start | bytes 2973704 | tf_op jit(solution)/shard_map/ppermute | solution.py:374
  45.0 4.4 %collective-permute-start.9 = (bf16[2,352,352]{2,1,0:T(8,128)(2,1)S(1)}, bf16[2,352,352]{2,1,0:T(8,128)(2,1)S(1)}, u32[]{:S(2)}, u32[]{:S(2)}) collective-permute-start(bf16[2,352,352]{2,1,0:T(8,128)(2,1)S(1)} %collective-permute-done.2.refs_5_), channel_id=1, source_target_pairs={{0,1},{1,0},{2,3},{3,2},{4,5},{5,4},{6,7},{7,6},{8,9},{9,8},{10,11... | collective-permute-start | bytes 1486856 | tf_op jit(solution)/shard_map/ppermute | solution.py:374
  47.2 2.4 %copy-start.11 = (bf16[1,128,384]{2,1,0:T(8,128)(2,1)}, bf16[1,128,384]{2,1,0:T(8,128)(2,1)S(1)}, u32[]{:S(2)}) copy-start(bf16[1,128,384]{2,1,0:T(8,128)(2,1)S(1)} %fusion.10) | copy-start | bytes 294916
  47.2 2.3 %collective-permute-start.8 = (bf16[352,352]{1,0:T(8,128)(2,1)S(1)}, bf16[352,352]{1,0:T(8,128)(2,1)S(1)}, u32[]{:S(2)}, u32[]{:S(2)}) collective-permute-start(bf16[352,352]{1,0:T(8,128)(2,1)S(1)} %collective-permute-done.1.refs_4_), channel_id=1, source_target_pairs={{0,1},{1,0},{2,3},{3,2},{4,5},{5,4},{6,7},{7,6},{8,9},{9,8},{10,11... | collective-permute-start | bytes 743432 | tf_op jit(solution)/shard_map/ppermute | solution.py:374
  48.0 15.4 %collective-permute-start.10 = (bf16[2,128,384]{2,1,0:T(8,128)(2,1)}, bf16[2,128,384]{2,1,0:T(8,128)(2,1)}, u32[]{:S(2)}, u32[]{:S(2)}) collective-permute-start(bf16[2,128,384]{2,1,0:T(8,128)(2,1)} %pad_maximum_fusion.3), channel_id=1, source_target_pairs={{0,4},{4,0},{1,5},{5,1},{2,6},{6,2},{3,7},{7,3},{8,12},{12,8},{9,1... | collective-permute-start | bytes 589832 | tf_op jit(solution)/shard_map/ppermute | solution.py:476
  52.0 1.8 %copy-start.1 = (bf16[1024,1408]{1,0:T(8,128)(2,1)S(1)}, bf16[1024,1408]{1,0:T(8,128)(2,1)}, u32[]{:S(2)}) copy-start(bf16[1024,1408]{1,0:T(8,128)(2,1)} %all-gather.2.cloned.1.call-done.normed_ref) | copy-start | bytes 8650756
  53.8 9.6 %copy-start.12 = (bf16[1,128,384]{2,1,0:T(8,128)(2,1)S(1)}, bf16[1,128,384]{2,1,0:T(8,128)(2,1)}, u32[]{:S(2)}) copy-start(bf16[1,128,384]{2,1,0:T(8,128)(2,1)} %copy-done.11) | copy-start | bytes 294916
  53.8 9.6 %copy-start.14 = (bf16[128,384]{1,0:T(8,128)(2,1)S(1)}, bf16[128,384]{1,0:T(8,128)(2,1)}, u32[]{:S(2)}) copy-start(bf16[128,384]{1,0:T(8,128)(2,1)} %copy-done.13) | copy-start | bytes 294916
  59.9 10.4 %all-to-all-start.1 = ((bf16[4,2,176,128]{3,2,1,0:T(8,128)(2,1)}), bf16[4,2,176,128]{3,2,1,0:T(8,128)(2,1)S(1)}, u32[]{:S(2)}, u32[]{:S(2)}) async-start(bf16[4,2,176,128]{3,2,1,0:T(8,128)(2,1)} %shard_map.106), calls=%async_computation.1 | async-start | bytes 720896 | tf_op jit(solution)/shard_map/all_to_all | solution.py:478
  63.4 12.0 %copy-start.4 = (bf16[384,1408]{1,0:T(8,128)(2,1)S(1)}, bf16[384,1408]{1,0:T(8,128)(2,1)}, u32[]{:S(2)}) copy-start(bf16[384,1408]{1,0:T(8,128)(2,1)} %proj_ref.1) | copy-start | bytes 3244036
  64.5 1.8 %collective-permute-start.11 = (bf16[4,128,384]{2,1,0:T(8,128)(2,1)S(1)}, bf16[4,128,384]{2,1,0:T(8,128)(2,1)S(1)}, u32[]{:S(2)}, u32[]{:S(2)}) collective-permute-start(bf16[4,128,384]{2,1,0:T(8,128)(2,1)S(1)} %pad_maximum_fusion.1.quad_ref), channel_id=1, source_target_pairs={{0,1},{1,0},{2,3},{3,2},{4,5},{5,4},{6,7},{7,6},{8,9},{9,8},{10,11... | collective-permute-start | bytes 1179656 | tf_op jit(solution)/shard_map/ppermute | solution.py:374
  73.5 1.9 %collective-permute-start.12 = (bf16[128,1408]{1,0:T(8,128)(2,1)}, bf16[128,1408]{1,0:T(8,128)(2,1)S(1)}, u32[]{:S(2)}, u32[]{:S(2)}) collective-permute-start(bf16[128,1408]{1,0:T(8,128)(2,1)} %get-tuple-element.20), channel_id=1, source_target_pairs={{0,1},{1,0},{2,3},{3,2},{4,5},{5,4},{6,7},{7,6},{8,9},{9,8},{10,11... | collective-permute-start | bytes 1081352 | tf_op jit(solution)/shard_map/ppermute | solution.py:374
  75.4 0.9 copy-start.8
  76.3 11.4 %copy-start.6 = (bf16[384,192]{1,0:T(8,128)(2,1)S(1)}, bf16[384,192]{1,0:T(8,128)(2,1)}, u32[]{:S(2)}) copy-start(bf16[384,192]{1,0:T(8,128)(2,1)} %copy-done.5) | copy-start | bytes 442372
  76.3 11.4 %copy-start.10 = (bf16[4,48,384]{2,1,0:T(8,128)(2,1)S(1)}, bf16[4,48,384]{2,1,0:T(8,128)(2,1)}, u32[]{:S(2)}) copy-start(bf16[4,48,384]{2,1,0:T(8,128)(2,1)} %copy-done.9) | copy-start | bytes 442372
Sparse Core Ops, SparseCore 0:
  25.8 24.4 all-gather.1
